TPU v7x, 256 devices: a whole 4x4x8 slice. The times are simulated.
256 devices in a mesh: ctx: 128 (over y_lo, x, z, core), dp: 2 (over y_hi).
Axes of the slice: x: 4, y: 4 (y_hi: 2, y_lo: 2; y = y_hi * 2 + y_lo), z: 8, core: 2. Of those that a mesh axis runs over, the one named last changes fastest.
Arguments:
- query_rows: bfloat16 [2, 16384, 4096], P('dp', 'ctx'), may hold values from -6 to 6
- key_rows: bfloat16 [2, 16384, 4096], P('dp', 'ctx'), may hold values from -6 to 6
- value_rows: bfloat16 [2, 16384, 4096], P('dp', 'ctx'), may hold values from -6 to 6
- conv_rows: bfloat16 [2, 16384, 4096], P('dp', 'ctx'), may hold values from -6 to 6
- grad_rows: bfloat16 [2, 16384, 4096], P('dp', 'ctx'), may hold values from -6 to 6
- residues: float32 [4096, 16], replicated, may hold values from -1.5 to 1.5
- decay_rates: float32 [4096, 16], replicated, may hold values from 1.5258789e-05 to 0.125
Outputs:
- grad_query: bfloat16 [2, 16384, 4096], P('dp', 'ctx')
- grad_key: bfloat16 [2, 16384, 4096], P('dp', 'ctx')
- grad_value: bfloat16 [2, 16384, 4096], P('dp', 'ctx')
- grad_coef: float32 [4096, 16], P('ctx')
All inputs are finite; a program needn't handle non-finite values.
Results may differ from a plain program's by a relative error of at most 0.012.
Values may be sent and summed in bfloat16 or wider, within the bound.
No kernel may reach another device: no remote copies, remote signals or barrier semaphores. Data moves between devices by JAX's collectives and lax.ppermute only.
A program may use at most 256 MiB of HBM per device.

v0:
```python
import math

import jax
import jax.numpy as jnp
from jax import lax
from jax.sharding import PartitionSpec as P

spectral_precision = lax.Precision.HIGH


def circle(product, period):
    turns = (product % period).astype(jnp.float32) * (2.0 * math.pi / period)
    return (jnp.cos(turns), jnp.sin(turns))


def forward_spectrum(signal, tables):
    outer_table, cos_twist, sin_twist, second_table, inverse_table = tables
    coarse_count = cos_twist.shape[0]
    fine_count = cos_twist.shape[1]
    section_one = jnp.einsum("cab,ak->ckb", signal, outer_table, precision=spectral_precision)
    real_one = section_one[:, :coarse_count]
    imag_one = section_one[:, coarse_count:]
    real_twist = real_one * cos_twist + imag_one * sin_twist
    imag_twist = imag_one * cos_twist - real_one * sin_twist
    joined = jnp.concatenate([real_twist, imag_twist], axis=2)
    section_two = jnp.einsum("ckb,bj->ckj", joined, second_table, precision=spectral_precision)
    return (section_two[:, :, :fine_count], section_two[:, :, fine_count:])


def inverse_signal(real_in, imag_in, tables, padded):
    outer_table, cos_twist, sin_twist, second_table, inverse_table = tables
    fine_count = cos_twist.shape[1]
    joined = jnp.concatenate([real_in, imag_in], axis=2)
    section_mid = jnp.einsum("ckj,jb->ckb", joined, inverse_table, precision=spectral_precision)
    real_mid = section_mid[:, :, :fine_count]
    imag_mid = section_mid[:, :, fine_count:]
    real_twist = real_mid * cos_twist - imag_mid * sin_twist
    imag_twist = imag_mid * cos_twist + real_mid * sin_twist
    stacked = jnp.concatenate([real_twist, imag_twist], axis=1)
    result = jnp.einsum("ckb,ak->cab", stacked, outer_table, precision=spectral_precision)
    return result / padded


def spectral_path(product, mixed_grad, residues, decay_rates):
    blocks = lax.axis_size("ctx")
    per_block = product.shape[0]
    channels = product.shape[1]
    owned_count = channels // blocks
    length = blocks * per_block
    padded = 2 * length
    moved_prod, moved_grad = (
        lax.all_to_all(product.T, "ctx", split_axis=0, concat_axis=1, tiled=True),
        lax.all_to_all(mixed_grad.T, "ctx", split_axis=0, concat_axis=1, tiled=True),
    )
    first_row = lax.axis_index("ctx") * owned_count
    rate_own = lax.dynamic_slice_in_dim(decay_rates, first_row, owned_count, 0)
    resid_own = lax.dynamic_slice_in_dim(residues, first_row, owned_count, 0)
    gain_own = jnp.sqrt(-jnp.expm1(-2.0 * rate_own))
    weight_own = resid_own * gain_own
    group_size = 4
    source = jnp.arange(blocks)
    coarse = jnp.arange(2 * blocks)
    fine = jnp.arange(per_block)
    cos_one, sin_one = circle(source[:, None] * coarse[None, :], 2 * blocks)
    cos_twist, sin_twist = circle(coarse[:, None] * fine[None, :], padded)
    cos_two, sin_two = circle(fine[:, None] * fine[None, :], per_block)
    outer_table = jnp.concatenate([cos_one, -sin_one], axis=1)
    second_table = jnp.concatenate(
        [jnp.concatenate([cos_two, -sin_two], axis=1), jnp.concatenate([sin_two, cos_two], axis=1)],
        axis=0,
    )
    inverse_table = jnp.concatenate(
        [jnp.concatenate([cos_two, sin_two], axis=1), jnp.concatenate([-sin_two, cos_two], axis=1)],
        axis=0,
    )
    tables = (outer_table, cos_twist, sin_twist, second_table, inverse_table)
    frequency = coarse[:, None] + 2 * blocks * fine[None, :]
    sin_full = circle(frequency, padded)[1]
    sin_half = circle(frequency, 2 * padded)[1]
    parity = (1 - 2 * (coarse % 2)).astype(jnp.float32)[:, None]

    def one_group(pieces):
        prod_group, grad_group, rate_group, weight_group = pieces
        prod_real, prod_imag = forward_spectrum(
            prod_group.astype(jnp.float32).reshape(group_size, blocks, per_block), tables
        )
        grad_real, grad_imag = forward_spectrum(
            grad_group.astype(jnp.float32).reshape(group_size, blocks, per_block), tables
        )
        cross_real = grad_real * prod_real + grad_imag * prod_imag
        cross_imag = grad_imag * prod_real - grad_real * prod_imag
        rate_wide = rate_group[:, :, None, None]
        decay_wide = jnp.exp(-rate_wide)
        denom_real = -jnp.expm1(-rate_wide) + 2.0 * decay_wide * sin_half * sin_half
        denom_imag = decay_wide * sin_full
        numer = jnp.where(
            parity > 0.0, -jnp.expm1(-rate_wide * length), 1.0 + jnp.exp(-rate_wide * length)
        )
        ratio = numer / (denom_real * denom_real + denom_imag * denom_imag)
        modal_real = ratio * denom_real
        modal_imag = -ratio * denom_imag
        weight_wide = weight_group[:, :, None, None]
        taps_real = jnp.sum(weight_wide * modal_real, axis=1)
        taps_imag = jnp.sum(weight_wide * modal_imag, axis=1)
        coef_group = (
            jnp.sum(
                cross_real[:, None] * modal_real + cross_imag[:, None] * modal_imag, axis=(2, 3)
            )
            / padded
        )
        mixed_real = grad_real * taps_real + grad_imag * taps_imag
        mixed_imag = grad_imag * taps_real - grad_real * taps_imag
        result = inverse_signal(mixed_real, mixed_imag, tables, padded)
        return (result.reshape(group_size, length).astype(jnp.bfloat16), coef_group)

    group_count = owned_count // group_size
    grad_chan, coef_sums = lax.map(
        one_group,
        (
            moved_prod.reshape(group_count, group_size, length),
            moved_grad.reshape(group_count, group_size, length),
            rate_own.reshape(group_count, group_size, -1),
            weight_own.reshape(group_count, group_size, -1),
        ),
    )
    grad_chan = grad_chan.reshape(owned_count, length)
    returned = lax.all_to_all(grad_chan, "ctx", split_axis=1, concat_axis=0, tiled=True)
    coef_part = gain_own * coef_sums.reshape(owned_count, -1) / math.sqrt(length)
    return (returned.T, coef_part)


def local(query_rows, key_rows, value_rows, conv_rows, grad_rows, residues, decay_rates):
    grad_local = grad_rows[0].astype(jnp.float32)
    key_float = key_rows[0].astype(jnp.float32)
    value_float = value_rows[0].astype(jnp.float32)
    mixed_grad = (grad_local * query_rows[0].astype(jnp.float32)).astype(jnp.bfloat16)
    product = (key_float * value_float).astype(jnp.bfloat16)
    grad_query = (grad_local * conv_rows[0].astype(jnp.float32)).astype(jnp.bfloat16)
    grad_mix, coef_local = spectral_path(product, mixed_grad, residues, decay_rates)
    grad_coef = lax.psum(coef_local, "dp")
    mix_float = grad_mix.astype(jnp.float32)
    grad_key = (mix_float * value_float).astype(jnp.bfloat16)
    grad_value = (mix_float * key_float).astype(jnp.bfloat16)
    return (grad_query[None], grad_key[None], grad_value[None], grad_coef)


def solution(mesh):
    in_specs = (
        P("dp", "ctx", None),
        P("dp", "ctx", None),
        P("dp", "ctx", None),
        P("dp", "ctx", None),
        P("dp", "ctx", None),
        P(),
        P(),
    )
    out_specs = (P("dp", "ctx", None), P("dp", "ctx", None), P("dp", "ctx", None), P("ctx", None))
    return jax.shard_map(local, mesh=mesh, in_specs=in_specs, out_specs=out_specs, check_vma=False)
```

profile of v0, /device:TPU:1, one launch (start us, length us, event | category | flops | bytes accessed | tf_op | source)
XLA Modules:
  0.0 279.8 jit_solution(9231312093379130583)
XLA Ops:
  0.6 1.7 copy.127
  3.4 1.3 fusion.71
  4.7 15.4 %all-to-all-start.1 = ((bf16[128,32,128]{2,1,0:T(8,128)(2,1)}), bf16[128,32,128]{2,1,0:T(8,128)(2,1)}, u32[]{:S(2)}, u32[]{:S(2)}) async-start(bf16[128,32,128]{2,1,0:T(8,128)(2,1)} %bitcast.9), calls=%async_computation.1 | async-start | bytes 2097152 | tf_op jit(solution)/shard_map/all_to_all | solution.py:52
  22.0 1.6 copy.123
  23.6 1.8 fusion.69
  25.4 23.1 %all-to-all-done.1 = bf16[128,32,128]{2,1,0:T(8,128)(2,1)} async-done(((bf16[128,32,128]{2,1,0:T(8,128)(2,1)}), bf16[128,32,128]{2,1,0:T(8,128)(2,1)}, u32[]{:S(2)}, u32[]{:S(2)}) %all-to-all-start.1) | async-done | bytes 1048608 | tf_op jit(solution)/shard_map/all_to_all | solution.py:52
  48.5 7.8 %all-to-all-start = ((bf16[128,32,128]{2,1,0:T(8,128)(2,1)}), bf16[128,32,128]{2,1,0:T(8,128)(2,1)S(1)}, u32[]{:S(2)}, u32[]{:S(2)}) async-start(bf16[128,32,128]{2,1,0:T(8,128)(2,1)} %bitcast.2), calls=%async_computation | async-start | bytes 2097152 | tf_op jit(solution)/shard_map/all_to_all | solution.py:53
  59.1 1.6 copy.129
  60.8 1.2 reshape.183
  62.0 23.1 %all-to-all-done = bf16[128,32,128]{2,1,0:T(8,128)(2,1)S(1)} async-done(((bf16[128,32,128]{2,1,0:T(8,128)(2,1)}), bf16[128,32,128]{2,1,0:T(8,128)(2,1)S(1)}, u32[]{:S(2)}, u32[]{:S(2)}) %all-to-all-start) | async-done | bytes 1048608 | tf_op jit(solution)/shard_map/all_to_all | solution.py:53
  85.5 1.1 reshape.180
  86.6 146.1 %while.15 = (s32[]{:T(128)}, bf16[8,4,16384]{2,1,0:T(4,128)(2,1)}, f32[8,4,16]{2,1,0:T(4,128)}, bf16[8,4,16384]{2,1,0:T(4,128)(2,1)}, f32[128,512]{1,0:T(8,128)S...) while((s32[]{:T(128)}, bf16[8,4,16384]{2,1,0:T(4,128)(2,1)}, ...), condition=%wide.region_4.5_spmd.clone.clone.clone, body=%wide.region_0.4_spmd.clone.clone.clone.sunk | while | flops 1857899520 | bytes 37254808 | solution.py:117
  86.6 1.2 dynamic-slice_bitcast_fusion.4
  91.9 1.0 fusion.122
  92.9 7.4 %multiply_reduce_fusion.3 = (f32[4,256,128]{2,1,0:T(8,128)S(1)}, f32[4,256,128]{2,1,0:T(8,128)S(1)}, f32[4,16]{1,0:T(4,128)}) fusion(f32[256,128]{1,0:T(8,128)S(1)} %get-tuple-element.407, f32[4,16]{1,0:T(4,128)S(1)} %get-tuple-element.408, f32[4,16]{1,0:T(4,128)S(1)} %get-tuple-element.409, f32[256,128]{1,0:T(8,128)S(1)} %get-tuple-element.410, ...), kind=kLoop, calls=%fused_computation.11.clone.1 | loop fusion | flops 39583680 | bytes 2426112 | tf_op jit(solution)/shard_map/while/body/eval_jaxpr/reduce_sum | solution.py:103
  104.9 1.2 dynamic-slice_bitcast_fusion.4
  110.2 1.0 fusion.122
  111.2 7.4 %multiply_reduce_fusion.3 = (f32[4,256,128]{2,1,0:T(8,128)S(1)}, f32[4,256,128]{2,1,0:T(8,128)S(1)}, f32[4,16]{1,0:T(4,128)}) fusion(f32[256,128]{1,0:T(8,128)S(1)} %get-tuple-element.407, f32[4,16]{1,0:T(4,128)S(1)} %get-tuple-element.408, f32[4,16]{1,0:T(4,128)S(1)} %get-tuple-element.409, f32[256,128]{1,0:T(8,128)S(1)} %get-tuple-element.410, ...), kind=kLoop, calls=%fused_computation.11.clone.1 | loop fusion | flops 39583680 | bytes 2426112 | tf_op jit(solution)/shard_map/while/body/eval_jaxpr/reduce_sum | solution.py:103
  123.2 1.2 dynamic-slice_bitcast_fusion.4
  128.5 1.0 fusion.122
  129.4 7.4 %multiply_reduce_fusion.3 = (f32[4,256,128]{2,1,0:T(8,128)S(1)}, f32[4,256,128]{2,1,0:T(8,128)S(1)}, f32[4,16]{1,0:T(4,128)}) fusion(f32[256,128]{1,0:T(8,128)S(1)} %get-tuple-element.407, f32[4,16]{1,0:T(4,128)S(1)} %get-tuple-element.408, f32[4,16]{1,0:T(4,128)S(1)} %get-tuple-element.409, f32[256,128]{1,0:T(8,128)S(1)} %get-tuple-element.410, ...), kind=kLoop, calls=%fused_computation.11.clone.1 | loop fusion | flops 39583680 | bytes 2426112 | tf_op jit(solution)/shard_map/while/body/eval_jaxpr/reduce_sum | solution.py:103
  137.4 0.8 copy-done.8
  141.4 1.2 dynamic-slice_bitcast_fusion.4
  146.7 1.0 fusion.122
  147.7 7.4 %multiply_reduce_fusion.3 = (f32[4,256,128]{2,1,0:T(8,128)S(1)}, f32[4,256,128]{2,1,0:T(8,128)S(1)}, f32[4,16]{1,0:T(4,128)}) fusion(f32[256,128]{1,0:T(8,128)S(1)} %get-tuple-element.407, f32[4,16]{1,0:T(4,128)S(1)} %get-tuple-element.408, f32[4,16]{1,0:T(4,128)S(1)} %get-tuple-element.409, f32[256,128]{1,0:T(8,128)S(1)} %get-tuple-element.410, ...), kind=kLoop, calls=%fused_computation.11.clone.1 | loop fusion | flops 39583680 | bytes 2426112 | tf_op jit(solution)/shard_map/while/body/eval_jaxpr/reduce_sum | solution.py:103
  159.7 1.2 dynamic-slice_bitcast_fusion.4
  165.0 1.0 fusion.122
  166.0 7.4 %multiply_reduce_fusion.3 = (f32[4,256,128]{2,1,0:T(8,128)S(1)}, f32[4,256,128]{2,1,0:T(8,128)S(1)}, f32[4,16]{1,0:T(4,128)}) fusion(f32[256,128]{1,0:T(8,128)S(1)} %get-tuple-element.407, f32[4,16]{1,0:T(4,128)S(1)} %get-tuple-element.408, f32[4,16]{1,0:T(4,128)S(1)} %get-tuple-element.409, f32[256,128]{1,0:T(8,128)S(1)} %get-tuple-element.410, ...), kind=kLoop, calls=%fused_computation.11.clone.1 | loop fusion | flops 39583680 | bytes 2426112 | tf_op jit(solution)/shard_map/while/body/eval_jaxpr/reduce_sum | solution.py:103
  177.9 1.2 dynamic-slice_bitcast_fusion.4
  183.2 1.0 fusion.122
  184.2 7.4 %multiply_reduce_fusion.3 = (f32[4,256,128]{2,1,0:T(8,128)S(1)}, f32[4,256,128]{2,1,0:T(8,128)S(1)}, f32[4,16]{1,0:T(4,128)}) fusion(f32[256,128]{1,0:T(8,128)S(1)} %get-tuple-element.407, f32[4,16]{1,0:T(4,128)S(1)} %get-tuple-element.408, f32[4,16]{1,0:T(4,128)S(1)} %get-tuple-element.409, f32[256,128]{1,0:T(8,128)S(1)} %get-tuple-element.410, ...), kind=kLoop, calls=%fused_computation.11.clone.1 | loop fusion | flops 39583680 | bytes 2426112 | tf_op jit(solution)/shard_map/while/body/eval_jaxpr/reduce_sum | solution.py:103
  192.2 0.8 copy-done.8
  196.2 1.2 dynamic-slice_bitcast_fusion.4
  201.5 1.0 fusion.122
  202.5 7.4 %multiply_reduce_fusion.3 = (f32[4,256,128]{2,1,0:T(8,128)S(1)}, f32[4,256,128]{2,1,0:T(8,128)S(1)}, f32[4,16]{1,0:T(4,128)}) fusion(f32[256,128]{1,0:T(8,128)S(1)} %get-tuple-element.407, f32[4,16]{1,0:T(4,128)S(1)} %get-tuple-element.408, f32[4,16]{1,0:T(4,128)S(1)} %get-tuple-element.409, f32[256,128]{1,0:T(8,128)S(1)} %get-tuple-element.410, ...), kind=kLoop, calls=%fused_computation.11.clone.1 | loop fusion | flops 39583680 | bytes 2426112 | tf_op jit(solution)/shard_map/while/body/eval_jaxpr/reduce_sum | solution.py:103
  214.4 1.2 dynamic-slice_bitcast_fusion.4
  219.8 1.0 fusion.122
  220.7 7.4 %multiply_reduce_fusion.3 = (f32[4,256,128]{2,1,0:T(8,128)S(1)}, f32[4,256,128]{2,1,0:T(8,128)S(1)}, f32[4,16]{1,0:T(4,128)}) fusion(f32[256,128]{1,0:T(8,128)S(1)} %get-tuple-element.407, f32[4,16]{1,0:T(4,128)S(1)} %get-tuple-element.408, f32[4,16]{1,0:T(4,128)S(1)} %get-tuple-element.409, f32[256,128]{1,0:T(8,128)S(1)} %get-tuple-element.410, ...), kind=kLoop, calls=%fused_computation.11.clone.1 | loop fusion | flops 39583680 | bytes 2426112 | tf_op jit(solution)/shard_map/while/body/eval_jaxpr/reduce_sum | solution.py:103
  228.7 0.8 copy-done.8
  232.7 2.4 all_to_all.40
  235.1 1.6 copy.130
  236.7 8.3 %all-to-all-start.2 = ((bf16[32,128,128]{2,0,1:T(8,128)(2,1)}), bf16[32,128,128]{2,0,1:T(8,128)(2,1)}, u32[]{:S(2)}, u32[]{:S(2)}) async-start(bf16[32,128,128]{2,0,1:T(8,128)(2,1)} %copy.130), calls=%async_computation.2 | async-start | bytes 2097152 | tf_op jit(solution)/shard_map/all_to_all | solution.py:127
  245.1 1.3 copy.131
  246.4 9.9 %psum.7 = f32[32,16]{1,0:T(8,128)S(1)} all-reduce(f32[32,16]{1,0:T(8,128)S(1)} %multiply_multiply_fusion.2), channel_id=1, replica_groups=mesh['ctx'=128,'dp'=2] {'dp'}, use_global_device_ids=true, to_apply=%region_5.6 | all-reduce | flops 512 | bytes 4096 | tf_op jit(solution)/shard_map/psum | solution.py:140
  257.0 16.5 %all-to-all-done.2 = bf16[32,128,128]{2,0,1:T(8,128)(2,1)} async-done(((bf16[32,128,128]{2,0,1:T(8,128)(2,1)}), bf16[32,128,128]{2,0,1:T(8,128)(2,1)}, u32[]{:S(2)}, u32[]{:S(2)}) %all-to-all-start.2) | async-done | bytes 1048608 | tf_op jit(solution)/shard_map/all_to_all | solution.py:127
  273.5 2.7 fusion.70
  276.2 2.3 copy.132
  278.4 1.3 copy.133
  (377 shorter events, 72.2 us)
Async XLA Ops:
  4.7 15.4 %copy-start.11 = (bf16[1,128,4096]{2,1,0:T(8,128)(2,1)S(1)}, bf16[1,128,4096]{2,1,0:T(8,128)(2,1)}, u32[]{:S(2)}) copy-start(bf16[1,128,4096]{2,1,0:T(8,128)(2,1)} %param.13) | copy-start | bytes 3145732
  4.7 43.8 %all-to-all-start.1 = ((bf16[128,32,128]{2,1,0:T(8,128)(2,1)}), bf16[128,32,128]{2,1,0:T(8,128)(2,1)}, u32[]{:S(2)}, u32[]{:S(2)}) async-start(bf16[128,32,128]{2,1,0:T(8,128)(2,1)} %bitcast.9), calls=%async_computation.1 | async-start | bytes 2097152 | tf_op jit(solution)/shard_map/all_to_all | solution.py:52
  48.5 36.5 %all-to-all-start = ((bf16[128,32,128]{2,1,0:T(8,128)(2,1)}), bf16[128,32,128]{2,1,0:T(8,128)(2,1)S(1)}, u32[]{:S(2)}, u32[]{:S(2)}) async-start(bf16[128,32,128]{2,1,0:T(8,128)(2,1)} %bitcast.2), calls=%async_computation | async-start | bytes 2097152 | tf_op jit(solution)/shard_map/all_to_all | solution.py:53
  86.6 4.0 %copy-start = (f32[256,256]{1,0:T(8,128)}, f32[256,256]{1,0:T(8,128)S(1)}, u32[]{:S(2)}) copy-start(f32[256,256]{1,0:T(8,128)S(1)} %get-tuple-element.461) | copy-start | bytes 786436 | tf_op jit(solution)/shard_map/while
  86.6 5.1 %copy-start.14 = (f32[8,4,16]{2,1,0:T(4,128)}, f32[8,4,16]{2,1,0:T(4,128)S(1)}, u32[]{:S(2)}) copy-start(f32[8,4,16]{2,1,0:T(4,128)S(1)} %get-tuple-element.462) | copy-start | bytes 6148 | tf_op jit(solution)/shard_map/while
  86.6 5.3 %copy-start.17 = (s32[128]{0:T(128)}, s32[128]{0:T(128)S(1)}, u32[]{:S(2)}) copy-start(s32[128]{0:T(128)S(1)} %get-tuple-element.466) | copy-start | bytes 1540 | tf_op jit(solution)/shard_map/while
  102.8 2.1 copy-start.1
  102.8 2.1 copy-start.15
  102.8 2.1 copy-start.18
  104.9 4.0 %copy-start = (f32[256,256]{1,0:T(8,128)}, f32[256,256]{1,0:T(8,128)S(1)}, u32[]{:S(2)}) copy-start(f32[256,256]{1,0:T(8,128)S(1)} %get-tuple-element.461) | copy-start | bytes 786436 | tf_op jit(solution)/shard_map/while
  104.9 5.1 %copy-start.14 = (f32[8,4,16]{2,1,0:T(4,128)}, f32[8,4,16]{2,1,0:T(4,128)S(1)}, u32[]{:S(2)}) copy-start(f32[8,4,16]{2,1,0:T(4,128)S(1)} %get-tuple-element.462) | copy-start | bytes 6148 | tf_op jit(solution)/shard_map/while
  104.9 5.3 %copy-start.17 = (s32[128]{0:T(128)}, s32[128]{0:T(128)S(1)}, u32[]{:S(2)}) copy-start(s32[128]{0:T(128)S(1)} %get-tuple-element.466) | copy-start | bytes 1540 | tf_op jit(solution)/shard_map/while
  121.0 2.1 copy-start.1
  121.0 2.1 copy-start.15
  123.1 4.0 %copy-start = (f32[256,256]{1,0:T(8,128)}, f32[256,256]{1,0:T(8,128)S(1)}, u32[]{:S(2)}) copy-start(f32[256,256]{1,0:T(8,128)S(1)} %get-tuple-element.461) | copy-start | bytes 786436 | tf_op jit(solution)/shard_map/while
  123.1 5.1 %copy-start.14 = (f32[8,4,16]{2,1,0:T(4,128)}, f32[8,4,16]{2,1,0:T(4,128)S(1)}, u32[]{:S(2)}) copy-start(f32[8,4,16]{2,1,0:T(4,128)S(1)} %get-tuple-element.462) | copy-start | bytes 6148 | tf_op jit(solution)/shard_map/while
  123.1 5.3 %copy-start.17 = (s32[128]{0:T(128)}, s32[128]{0:T(128)S(1)}, u32[]{:S(2)}) copy-start(s32[128]{0:T(128)S(1)} %get-tuple-element.466) | copy-start | bytes 1540 | tf_op jit(solution)/shard_map/while
  139.3 2.1 copy-start.1
  139.3 2.1 copy-start.15
  139.3 2.1 copy-start.18
  141.4 4.0 %copy-start = (f32[256,256]{1,0:T(8,128)}, f32[256,256]{1,0:T(8,128)S(1)}, u32[]{:S(2)}) copy-start(f32[256,256]{1,0:T(8,128)S(1)} %get-tuple-element.461) | copy-start | bytes 786436 | tf_op jit(solution)/shard_map/while
  141.4 5.1 %copy-start.14 = (f32[8,4,16]{2,1,0:T(4,128)}, f32[8,4,16]{2,1,0:T(4,128)S(1)}, u32[]{:S(2)}) copy-start(f32[8,4,16]{2,1,0:T(4,128)S(1)} %get-tuple-element.462) | copy-start | bytes 6148 | tf_op jit(solution)/shard_map/while
  141.4 5.3 %copy-start.17 = (s32[128]{0:T(128)}, s32[128]{0:T(128)S(1)}, u32[]{:S(2)}) copy-start(s32[128]{0:T(128)S(1)} %get-tuple-element.466) | copy-start | bytes 1540 | tf_op jit(solution)/shard_map/while
  157.6 2.1 copy-start.1
  159.7 4.0 %copy-start = (f32[256,256]{1,0:T(8,128)}, f32[256,256]{1,0:T(8,128)S(1)}, u32[]{:S(2)}) copy-start(f32[256,256]{1,0:T(8,128)S(1)} %get-tuple-element.461) | copy-start | bytes 786436 | tf_op jit(solution)/shard_map/while
  159.7 5.1 %copy-start.14 = (f32[8,4,16]{2,1,0:T(4,128)}, f32[8,4,16]{2,1,0:T(4,128)S(1)}, u32[]{:S(2)}) copy-start(f32[8,4,16]{2,1,0:T(4,128)S(1)} %get-tuple-element.462) | copy-start | bytes 6148 | tf_op jit(solution)/shard_map/while
  159.7 5.3 %copy-start.17 = (s32[128]{0:T(128)}, s32[128]{0:T(128)S(1)}, u32[]{:S(2)}) copy-start(s32[128]{0:T(128)S(1)} %get-tuple-element.466) | copy-start | bytes 1540 | tf_op jit(solution)/shard_map/while
  177.9 4.0 %copy-start = (f32[256,256]{1,0:T(8,128)}, f32[256,256]{1,0:T(8,128)S(1)}, u32[]{:S(2)}) copy-start(f32[256,256]{1,0:T(8,128)S(1)} %get-tuple-element.461) | copy-start | bytes 786436 | tf_op jit(solution)/shard_map/while
  177.9 5.1 %copy-start.14 = (f32[8,4,16]{2,1,0:T(4,128)}, f32[8,4,16]{2,1,0:T(4,128)S(1)}, u32[]{:S(2)}) copy-start(f32[8,4,16]{2,1,0:T(4,128)S(1)} %get-tuple-element.462) | copy-start | bytes 6148 | tf_op jit(solution)/shard_map/while
  177.9 5.3 %copy-start.17 = (s32[128]{0:T(128)}, s32[128]{0:T(128)S(1)}, u32[]{:S(2)}) copy-start(s32[128]{0:T(128)S(1)} %get-tuple-element.466) | copy-start | bytes 1540 | tf_op jit(solution)/shard_map/while
  194.1 2.1 copy-start.1
  194.1 2.1 copy-start.15
  194.1 2.1 copy-start.18
  196.2 4.0 %copy-start = (f32[256,256]{1,0:T(8,128)}, f32[256,256]{1,0:T(8,128)S(1)}, u32[]{:S(2)}) copy-start(f32[256,256]{1,0:T(8,128)S(1)} %get-tuple-element.461) | copy-start | bytes 786436 | tf_op jit(solution)/shard_map/while
  196.2 5.1 %copy-start.14 = (f32[8,4,16]{2,1,0:T(4,128)}, f32[8,4,16]{2,1,0:T(4,128)S(1)}, u32[]{:S(2)}) copy-start(f32[8,4,16]{2,1,0:T(4,128)S(1)} %get-tuple-element.462) | copy-start | bytes 6148 | tf_op jit(solution)/shard_map/while
  196.2 5.3 %copy-start.17 = (s32[128]{0:T(128)}, s32[128]{0:T(128)S(1)}, u32[]{:S(2)}) copy-start(s32[128]{0:T(128)S(1)} %get-tuple-element.466) | copy-start | bytes 1540 | tf_op jit(solution)/shard_map/while
  212.3 2.1 copy-start.1
  214.4 4.0 %copy-start = (f32[256,256]{1,0:T(8,128)}, f32[256,256]{1,0:T(8,128)S(1)}, u32[]{:S(2)}) copy-start(f32[256,256]{1,0:T(8,128)S(1)} %get-tuple-element.461) | copy-start | bytes 786436 | tf_op jit(solution)/shard_map/while
  214.4 5.1 %copy-start.14 = (f32[8,4,16]{2,1,0:T(4,128)}, f32[8,4,16]{2,1,0:T(4,128)S(1)}, u32[]{:S(2)}) copy-start(f32[8,4,16]{2,1,0:T(4,128)S(1)} %get-tuple-element.462) | copy-start | bytes 6148 | tf_op jit(solution)/shard_map/while
  214.4 5.3 %copy-start.17 = (s32[128]{0:T(128)}, s32[128]{0:T(128)S(1)}, u32[]{:S(2)}) copy-start(s32[128]{0:T(128)S(1)} %get-tuple-element.466) | copy-start | bytes 1540 | tf_op jit(solution)/shard_map/while
  230.6 2.1 copy-start.1
  230.6 2.1 copy-start.15
  230.6 2.1 copy-start.18
  236.7 8.3 %copy-start.9 = (bf16[1,128,4096]{1,2,0:T(8,128)(2,1)S(1)}, bf16[1,128,4096]{1,2,0:T(8,128)(2,1)}, u32[]{:S(2)}) copy-start(bf16[1,128,4096]{1,2,0:T(8,128)(2,1)} %get-tuple-element.306) | copy-start | bytes 3145732
  236.7 9.7 %copy-start.16 = (f32[8,4,16]{2,1,0:T(4,128)S(1)}, f32[8,4,16]{2,1,0:T(4,128)}, u32[]{:S(2)}) copy-start(f32[8,4,16]{2,1,0:T(4,128)} %get-tuple-element.116) | copy-start | bytes 6148
  236.7 36.8 %all-to-all-start.2 = ((bf16[32,128,128]{2,0,1:T(8,128)(2,1)}), bf16[32,128,128]{2,0,1:T(8,128)(2,1)}, u32[]{:S(2)}, u32[]{:S(2)}) async-start(bf16[32,128,128]{2,0,1:T(8,128)(2,1)} %copy.130), calls=%async_computation.2 | async-start | bytes 2097152 | tf_op jit(solution)/shard_map/all_to_all | solution.py:127
  245.1 28.4 %copy-start.5 = (bf16[1,128,4096]{1,2,0:T(8,128)(2,1)S(1)}, bf16[1,128,4096]{1,2,0:T(8,128)(2,1)}, u32[]{:S(2)}) copy-start(bf16[1,128,4096]{1,2,0:T(8,128)(2,1)} %copy-done.4) | copy-start | bytes 3145732
  245.1 28.4 %copy-start.7 = (bf16[1,128,4096]{1,2,0:T(8,128)(2,1)S(1)}, bf16[1,128,4096]{1,2,0:T(8,128)(2,1)}, u32[]{:S(2)}) copy-start(bf16[1,128,4096]{1,2,0:T(8,128)(2,1)} %copy-done.6) | copy-start | bytes 3145732
  (44 other events, 54.3 us)
where the time goes:
time: 281 us; the launch traced here: 280 us
  other arithmetic  90.4 us (32%)
  waiting for transfers between devices  62.7 us (22%)
  local copies, waits for them, and re-layouts  55.4 us (20%)
  starting transfers between devices  31.5 us (11%)
  matrix products  27 us (10%)
  blocking collectives  9.91 us (4%)
    reduce_sum x8, other arithmetic, one_group(): taps_real = jnp.sum(weight_wide * modal_real, axis=1)  59.5 us
    all_to_all x1, waiting for transfers between devices, spectral_path(): lax.all_to_all(product.T, 'ctx', split_axis=0, concat_axis=1, tiled=True)  23.1 us
    all_to_all x1, waiting for transfers between devices, spectral_path(): lax.all_to_all(mixed_grad.T, 'ctx', split_axis=0, concat_axis=1, tiled=True)  23.1 us
    while x168, local copies, waits for them, and re-layouts  21.1 us
    all_to_all x1, waiting for transfers between devices, spectral_path(): lax.all_to_all(grad_chan, 'ctx', split_axis=1, concat_axis=0, tiled=True)  16.5 us
    all_to_all x1, starting transfers between devices, spectral_path(): lax.all_to_all(product.T, 'ctx', split_axis=0, concat_axis=1, tiled=True)  15.4 us
    sin x17, other arithmetic, circle(): return (jnp.cos(turns), jnp.sin(turns))  12.1 us
    unnamed x29, local copies, waits for them, and re-layouts  11.9 us
  transfers between devices with their start and end apart: 3, of which 3 were waited for; matrix products, arithmetic and copies ran while one was open for 4% of the time, Pallas kernels for 0%

commit v1 on v0

v1 whole, which is shorter than its diff:
```python
import functools
import math

import jax
import jax.numpy as jnp
from jax import lax
from jax.experimental import pallas as pl
from jax.experimental.pallas import tpu as pltpu
from jax.sharding import PartitionSpec as P

F32 = jnp.float32
BF16 = jnp.bfloat16
LANES = 128
SUB = 8
TOKENS = 128
ROWS = TOKENS // SUB
MODES = 16
WIDTH = 512
TILES = WIDTH // LANES
VMEM_LIMIT = 48 * 1024 * 1024


def lane_slice(tile):
    return pl.ds(pl.multiple_of(tile * LANES, LANES), LANES)


def transposed(rows):
    count = rows.shape[1]
    first = lax.broadcasted_iota(jnp.int32, (count, count), 0)
    second = lax.broadcasted_iota(jnp.int32, (count, count), 1)
    unit = (first == second).astype(F32)
    return lax.dot_general(
        unit, rows, (((1,), (1,)), ((), ())), precision=lax.Precision.HIGHEST, preferred_element_type=F32
    )


def gain_of(rates):
    square = rates * rates
    series = 1.0 + square * (1.0 / 6.0 + square * (1.0 / 120.0 + square * (1.0 / 5040.0)))
    return jnp.sqrt(2.0 * rates * series * jnp.exp(-rates))


def wide(row):
    return jnp.broadcast_to(row, (SUB, LANES))


def swap_quarters(tile):
    j = lax.broadcasted_iota(jnp.int32, (SUB, LANES), 0) & 3
    q = lax.broadcasted_iota(jnp.int32, (SUB, LANES), 1) >> 5
    for bit in (1, 2):
        j_set = (j & bit) != 0
        q_set = (q & bit) != 0
        up = pltpu.roll(pltpu.roll(tile, bit, 0), LANES - 32 * bit, 1)
        down = pltpu.roll(pltpu.roll(tile, SUB - bit, 0), 32 * bit, 1)
        tile = jnp.where(j_set == q_set, tile, jnp.where(j_set, up, down))
    return tile


def scatter_rows(modes_ref, slab_ref, first):
    for pair in range(2):
        moved = swap_quarters(modes_ref[SUB * pair : SUB * pair + SUB, :])
        for k in range(2):
            for q in range(4):
                row = SUB * q + first + 2 * pair + k
                slab_ref[row : row + 1, :] = moved[4 * k + q : 4 * k + q + 1, :]


def summary_kernel(
    grad_ref, query_ref, key_ref, value_ref, decay_ref,
    mixed_ref, product_ref, rate_ref, send_ref,
    powers, mixed_tile, product_tile, state_rows, carry_rows, slab,
):
    rates = transposed(decay_ref[...])
    rate_ref[...] = rates
    for index, power in enumerate((1.0, 2.0, 4.0, 8.0)):
        powers[index] = jnp.exp(-power * rates)

    def one_tile(tile, _):
        lanes = lane_slice(tile)
        mixed = (grad_ref[:, lanes].astype(F32) * query_ref[:, lanes].astype(F32)).astype(BF16)
        product = (key_ref[:, lanes].astype(F32) * value_ref[:, lanes].astype(F32)).astype(BF16)
        mixed_ref[:, lanes] = mixed
        product_ref[:, lanes] = product
        mixed_tile[...] = mixed.astype(F32)
        product_tile[...] = product.astype(F32)
        for base in range(0, MODES, 4):
            group = range(base, base + 4)
            eighth = [wide(powers[3, m : m + 1, lanes]) for m in group]
            state = [mixed_tile[TOKENS - SUB :, :]] * 4
            carry = [product_tile[:SUB, :]] * 4
            for i in range(1, ROWS):
                low = TOKENS - SUB - SUB * i
                mixed_row = mixed_tile[low : low + SUB, :]
                product_row = product_tile[SUB * i : SUB * i + SUB, :]
                state = [s * a + mixed_row for s, a in zip(state, eighth)]
                carry = [c * a + product_row for c, a in zip(carry, eighth)]
            for at, m in enumerate(group):
                one, two, four = [wide(powers[p, m : m + 1, lanes]) for p in range(3)]
                s = state[at]
                s = s + four * pltpu.roll(s, 4, 0)
                s = s + two * pltpu.roll(s, 6, 0)
                s = s + one * pltpu.roll(s, 7, 0)
                state_rows[m : m + 1, :] = s[0:1, :]
                c = carry[at]
                c = c + one * pltpu.roll(c, 1, 0)
                c = c + two * pltpu.roll(c, 2, 0)
                c = (c + four * pltpu.roll(c, 4, 0)) * one
                carry_rows[m : m + 1, :] = c[7:8, :]
        scatter_rows(state_rows, slab, 0)
        scatter_rows(carry_rows, slab, 4)
        send_ref[pl.ds(pl.multiple_of(tile * 32, 32), 32), :] = slab[...].astype(BF16)
        return 0

    lax.fori_loop(0, TILES, one_tile, 0)


def local_kernel(
    mixed_ref, product_ref, rate_ref, residue_ref,
    near_ref, send_ref,
    powers, weights, mixed_tile, product_tile, near_tile, coef_rows, slab,
):
    rates = rate_ref[...]
    weights[...] = transposed(residue_ref[...]) * gain_of(rates)
    for index, power in enumerate((1.0, 16.0, 32.0, 64.0)):
        powers[index] = jnp.exp(-power * rates)
    place = lax.broadcasted_iota(jnp.int32, (SUB, LANES), 0)
    slab[...] = jnp.zeros_like(slab)

    def one_tile(tile, _):
        lanes = lane_slice(tile)
        mixed_tile[...] = mixed_ref[:, lanes].astype(F32)
        product_tile[...] = product_ref[:, lanes].astype(F32)
        for base in range(0, MODES, 8):
            group = range(base, base + 8)
            one = [wide(powers[0, m : m + 1, lanes]) for m in group]
            weight = [wide(weights[m : m + 1, lanes]) for m in group]
            state = [mixed_tile[pl.ds(ROWS - 1, SUB, stride=ROWS), :]] * 8
            for j in range(ROWS - 2, -1, -1):
                mixed_row = mixed_tile[pl.ds(j, SUB, stride=ROWS), :]
                state = [s * a + mixed_row for s, a in zip(state, one)]
            for at, m in enumerate(group):
                s = state[at]
                for index, step in ((1, 1), (2, 2), (3, 4)):
                    shifted = jnp.where(place < SUB - step, pltpu.roll(s, SUB - step, 0), 0.0)
                    s = s + wide(powers[index, m : m + 1, lanes]) * shifted
                state[at] = jnp.where(place < SUB - 1, pltpu.roll(s, SUB - 1, 0), 0.0)
            total = [None] * 8
            for j in range(ROWS - 1, -1, -1):
                mixed_row = mixed_tile[pl.ds(j, SUB, stride=ROWS), :]
                product_row = product_tile[pl.ds(j, SUB, stride=ROWS), :]
                state = [s * a + mixed_row for s, a in zip(state, one)]
                terms = [s * w for s, w in zip(state, weight)]
                while len(terms) > 1:
                    terms = [x + y for x, y in zip(terms[::2], terms[1::2])]
                rows = slice(SUB * j, SUB * j + SUB)
                near_tile[rows, :] = terms[0] if base == 0 else near_tile[rows, :] + terms[0]
                total = [s * product_row if t is None else t + s * product_row for s, t in zip(state, total)]
            for at, m in enumerate(group):
                t = total[at]
                t = t + pltpu.roll(t, 4, 0)
                t = t + pltpu.roll(t, 2, 0)
                t = t + pltpu.roll(t, 1, 0)
                coef_rows[m : m + 1, :] = t[0:1, :]
        for i in range(ROWS):
            near_ref[SUB * i : SUB * i + SUB, lanes] = near_tile[pl.ds(64 * (i % 2) + i // 2, SUB, stride=SUB), :]
        scatter_rows(coef_rows, slab, 4)
        send_ref[pl.ds(pl.multiple_of(tile * 32, 32), 32), :] = slab[...].astype(BF16)
        return 0

    lax.fori_loop(0, TILES, one_tile, 0)


def scan_kernel(blocks, received_ref, coef_ref, rate_ref, send_ref, far_ref):
    decay = jnp.exp(-float(TOKENS) * rate_ref[...])
    low = lax.broadcasted_iota(jnp.int32, (SUB, LANES), 0) < 4

    def step(back, held):
        state, far = held
        start = pl.multiple_of((blocks // 2 - 1 - back) * 16, 16)
        pair = received_ref[pl.ds(start, 16), :].astype(F32)
        coef = coef_ref[pl.ds(start, 16), :].astype(F32)
        out = [None, None]
        for which in (1, 0):
            here = pair[SUB * which : SUB * which + SUB, :]
            out[which] = jnp.where(low, state, coef[SUB * which : SUB * which + SUB, :])
            far = far + here * state
            state = jnp.where(low, here, pltpu.roll(here, 4, 0)) + decay * state
        send_ref[pl.ds(start, 16), :] = jnp.concatenate(out, axis=0).astype(BF16)
        return state, far

    zero = jnp.zeros((SUB, LANES), F32)
    _, far = lax.fori_loop(0, blocks // 2, step, (zero, zero), unroll=4)
    far_ref[...] = far


def coef_kernel(blocks, scale, received_ref, far_ref, rate_ref, out_ref):
    def step(at, held):
        rows = received_ref[pl.ds(pl.multiple_of(at * 16, 16), 16), :].astype(F32)
        return held[0] + rows[:SUB, :], held[1] + rows[SUB:, :]

    first, second = lax.fori_loop(0, blocks // 2, step, (far_ref[...], jnp.zeros((SUB, LANES), F32)), unroll=8)
    out_ref[...] = (first + second) * gain_of(rate_ref[...]) * scale


def output_kernel(
    near_ref, received_ref, rate_ref, residue_ref, key_ref, value_ref,
    grad_key_ref, grad_value_ref,
    powers, weights, slab, heads,
):
    rates = rate_ref[...]
    weights[...] = transposed(residue_ref[...]) * gain_of(rates)
    powers[...] = jnp.exp(-8.0 * rates)
    back = (SUB - lax.broadcasted_iota(jnp.int32, (SUB, LANES), 0)).astype(F32)

    def one_tile(tile, _):
        lanes = lane_slice(tile)
        slab[...] = received_ref[pl.ds(pl.multiple_of(tile * 32, 32), 32), :].astype(F32)
        for pair in range(2):
            parts = [slab[pl.ds(2 * pair + k, 4, stride=SUB), :] for k in range(2)]
            heads[SUB * pair : SUB * pair + SUB, :] = swap_quarters(jnp.concatenate(parts, axis=0))
        heads[...] = heads[...] * weights[:, lanes]
        eighth = [wide(powers[m : m + 1, lanes]) for m in range(MODES)]
        state = [
            wide(heads[m : m + 1, :]) * jnp.exp(-back * wide(rate_ref[m : m + 1, lanes])) for m in range(MODES)
        ]
        for i in range(ROWS - 1, -1, -2):
            both = []
            for row in (i, i - 1):
                terms = state
                while len(terms) > 1:
                    terms = [x + y for x, y in zip(terms[::2], terms[1::2])]
                both.append(near_ref[SUB * row : SUB * row + SUB, lanes] + terms[0])
                if row > 0:
                    state = [s * a for s, a in zip(state, eighth)]
            rows = slice(SUB * (i - 1), SUB * (i - 1) + 16)
            mix = jnp.concatenate(both[::-1], axis=0).astype(BF16).astype(F32)
            grad_key_ref[rows, lanes] = (mix * value_ref[rows, lanes].astype(F32)).astype(BF16)
            grad_value_ref[rows, lanes] = (mix * key_ref[rows, lanes].astype(F32)).astype(BF16)
        return 0

    lax.fori_loop(0, TILES, one_tile, 0)


def gate_kernel(grad_ref, conv_ref, out_ref):
    out_ref[...] = (grad_ref[...].astype(F32) * conv_ref[...].astype(F32)).astype(BF16)


def call(kernel, grid, in_specs, out_specs, out_shape, scratch, flops, moved):
    return pl.pallas_call(
        kernel,
        grid=grid,
        in_specs=in_specs,
        out_specs=out_specs,
        out_shape=out_shape,
        scratch_shapes=scratch,
        compiler_params=pltpu.CompilerParams(vmem_limit_bytes=VMEM_LIMIT),
        cost_estimate=pl.CostEstimate(flops=flops, bytes_accessed=moved, transcendentals=0),
    )


def local(query_rows, key_rows, value_rows, conv_rows, grad_rows, residues, decay_rates):
    blocks = lax.axis_size("ctx")
    tokens, channels = query_rows.shape[1:]
    steps = channels // WIDTH
    own = channels // blocks
    length = blocks * tokens
    query, key, value, conv, grad = (x[0] for x in (query_rows, key_rows, value_rows, conv_rows, grad_rows))

    token_block = pl.BlockSpec((tokens, WIDTH), lambda n: (0, n))
    table_block = pl.BlockSpec((WIDTH, MODES), lambda n: (n, 0))
    mode_block = pl.BlockSpec((MODES, WIDTH), lambda n: (0, n))
    slab_block = pl.BlockSpec((TILES * 32, LANES), lambda n: (n, 0))
    token_half = jax.ShapeDtypeStruct((tokens, channels), BF16)
    token_full = jax.ShapeDtypeStruct((tokens, channels), F32)
    mode_table = jax.ShapeDtypeStruct((MODES, channels), F32)
    slabs = jax.ShapeDtypeStruct((blocks * SUB, LANES), BF16)
    tile_scratch = pltpu.VMEM((TOKENS, LANES), F32)
    rows_scratch = pltpu.VMEM((MODES, LANES), F32)
    slab_scratch = pltpu.VMEM((32, LANES), F32)

    mixed, product, rates, summary = call(
        summary_kernel, (steps,),
        [token_block] * 4 + [table_block],
        [token_block, token_block, mode_block, slab_block],
        [token_half, token_half, mode_table, slabs],
        [pltpu.VMEM((4, MODES, WIDTH), F32), tile_scratch, tile_scratch, rows_scratch, rows_scratch, slab_scratch],
        10**9, 8 * 2**20,
    )(grad, query, key, value, decay_rates)

    def exchange(rows):
        moved = lax.all_to_all(rows.reshape(blocks, SUB, LANES), "ctx", split_axis=0, concat_axis=0, tiled=True)
        return moved.reshape(blocks * SUB, LANES)

    received = exchange(summary)

    near, coef_slabs = call(
        local_kernel, (steps,),
        [token_block, token_block, mode_block, table_block],
        [token_block, slab_block],
        [token_full, slabs],
        [
            pltpu.VMEM((4, MODES, WIDTH), F32), pltpu.VMEM((MODES, WIDTH), F32),
            tile_scratch, tile_scratch, tile_scratch, rows_scratch, slab_scratch,
        ],
        2 * 10**9, 6 * 2**20,
    )(mixed, product, rates, residues)

    first = lax.axis_index("ctx") * own
    rate_own, _ = lax.optimization_barrier((lax.dynamic_slice_in_dim(decay_rates, first, own, 0), summary))
    rate_own = rate_own.T.reshape(4, LANES)
    rate_own = jnp.concatenate([rate_own, rate_own], axis=0)

    whole = lambda rows, dtype: (pl.BlockSpec((rows, LANES), lambda: (0, 0)), jax.ShapeDtypeStruct((rows, LANES), dtype))
    slab_spec, _ = whole(blocks * SUB, BF16)
    small_spec, small = whole(SUB, F32)
    carries, far = call(
        functools.partial(scan_kernel, blocks), (),
        [slab_spec, slab_spec, small_spec], [slab_spec, small_spec], [slabs, small], [],
        10**6, 2**20,
    )(received, coef_slabs, rate_own)

    returned = exchange(carries)

    gate_in, _ = lax.optimization_barrier((conv, carries))
    grad_query = call(
        gate_kernel, (4,),
        [pl.BlockSpec((tokens, channels // 4), lambda n: (0, n))] * 2,
        pl.BlockSpec((tokens, channels // 4), lambda n: (0, n)), token_half, [],
        10**6, 3 * 2**20,
    )(grad, gate_in)

    coef_part = call(
        functools.partial(coef_kernel, blocks, 1.0 / math.sqrt(length)), (),
        [slab_spec, small_spec, small_spec], small_spec, small, [],
        10**6, 2**18,
    )(returned, far, rate_own)
    other = lax.ppermute(coef_part, "dp", [(0, 1), (1, 0)])

    grad_key, grad_value = call(
        output_kernel, (steps,),
        [token_block, slab_block, mode_block, table_block, token_block, token_block],
        [token_block, token_block], [token_half, token_half],
        [pltpu.VMEM((MODES, WIDTH), F32), pltpu.VMEM((MODES, WIDTH), F32), slab_scratch, rows_scratch],
        10**9, 6 * 2**20,
    )(near, returned, rates, residues, key, value)

    coef = (coef_part + other)[4:].reshape(4, 4, own).transpose(2, 0, 1).reshape(own, MODES)
    return (grad_query[None], grad_key[None], grad_value[None], coef)


def solution(mesh):
    rows = P("dp", "ctx", None)
    return jax.shard_map(
        local,
        mesh=mesh,
        in_specs=(rows, rows, rows, rows, rows, P(), P()),
        out_specs=(rows, rows, rows, P("ctx", None)),
        check_vma=False,
    )
```

time: 281 us -> 110 us (0.39)
  other arithmetic: 90.4 us -> 0.01 us
  waiting for transfers between devices: 62.7 us -> 10.5 us
  Pallas kernels: 0 us -> 50.5 us
  local copies, waits for them, and re-layouts: 55.4 us -> 17.9 us
  matrix products: 27 us -> 0 us
  blocking collectives: 9.91 us -> 0 us
    reduce_sum x8 -> x0, other arithmetic: 59.5 us -> none  [one_group(): taps_real = jnp.sum(weight_wide * modal_real, axis=1)]
    all_to_all x3 -> x2, waiting for transfers between devices: 62.7 us -> 10.5 us  [exchange(): lax.all_to_all(rows.reshape(blocks, SUB, LANES), 'ctx', split_axis=0, con...]
    pallas_call x0 -> x6, Pallas kernels: none -> 50.5 us  [the longest x1 18.9 us: local(): call(local_kernel, (steps,), [token_block, token_block, mode_block, table...]
    dot_general x48 -> x0, matrix products: 27 us -> none  [the longest x16 9.8 us: forward_spectrum(): jnp.einsum('ckb,bj->ckj', joined, second_table, precision=spectral_precis...]
    while x168 -> x0, local copies, waits for them, and re-layouts: 21.1 us -> none
    sin x17 -> x0, other arithmetic: 12.1 us -> none  [circle(): return (jnp.cos(turns), jnp.sin(turns))]
    psum x1 -> x0, blocking collectives: 9.91 us -> none  [local(): grad_coef = lax.psum(coef_local, 'dp')]
    all_to_all x4 -> x0, local copies, waits for them, and re-layouts: 6.06 us -> none  [the longest x2 4.02 us: spectral_path(): lax.all_to_all(grad_chan, 'ctx', split_axis=1, concat_axis=0, tiled=True)]
  transfers between devices with their start and end apart: 3 -> 3, of which waited for: 3 -> 1; matrix products, arithmetic and copies ran while one was open for 4% -> 3% of each run, Pallas kernels for 0% -> 31%
where the time goes in v1:
time: 110 us
  Pallas kernels  50.5 us (46%)
  starting transfers between devices  30.1 us (27%)
  local copies, waits for them, and re-layouts  17.9 us (16%)
  waiting for transfers between devices  10.5 us (10%)
    all_to_all x2, starting transfers between devices, exchange(): lax.all_to_all(rows.reshape(blocks, SUB, LANES), 'ctx', split_axis=0, con...  27.4 us
    pallas_call x1, Pallas kernels, local(): call(local_kernel, (steps,), [token_block, token_block, mode_block, table...  18.9 us
    pallas_call x1, Pallas kernels, local(): call(summary_kernel, (steps,), [token_block] * 4 + [table_block], [token_...  16.5 us
    unnamed x32, local copies, waits for them, and re-layouts  16.3 us
    pallas_call x1, Pallas kernels, local(): call(output_kernel, (steps,), [token_block, slab_block, mode_block, table...  12.9 us
    all_to_all x2, waiting for transfers between devices, exchange(): lax.all_to_all(rows.reshape(blocks, SUB, LANES), 'ctx', split_axis=0, con...  10.5 us
    ppermute x1, starting transfers between devices, local(): other = lax.ppermute(coef_part, 'dp', [(0, 1), (1, 0)])  2.71 us
  transfers between devices with their start and end apart: 3, of which 1 were waited for; matrix products, arithmetic and copies ran while one was open for 3% of the time, Pallas kernels for 31%

profile of v1, /device:TPU:1, one launch (start us, length us, event | category | flops | bytes accessed | tf_op | source)
XLA Modules:
  0.0 109.7 jit_solution(4589293018239424297)
XLA Ops:
  0.6 0.0 copy-start
  0.6 0.0 copy-start.1
  0.7 3.0 %copy.11.decay_ref = f32[4096,16]{1,0:T(8,128)} copy(f32[4096,16]{0,1:T(8,128)} %param.13) | data formatting | bytes 524288 | tf_op args[6]
  3.7 0.0 copy-done
  3.7 0.0 copy-done.1
  3.7 0.0 copy-start.6
  3.7 1.2 %copy-done.6 = bf16[1,128,4096]{2,1,0:T(8,128)(2,1)S(1)} copy-done((bf16[1,128,4096]{2,1,0:T(8,128)(2,1)S(1)}, bf16[1,128,4096]{2,1,0:T(8,128)(2,1)}, u32[]{:S(2)}) %copy-start.6) | copy-done | bytes 1048600
  4.9 0.0 copy-start.14
  4.9 16.5 %shard_map.102 = (bf16[128,4096]{1,0:T(8,128)(2,1)S(1)}, bf16[128,4096]{1,0:T(8,128)(2,1)S(1)}, f32[16,4096]{1,0:T(8,128)S(1)}, bf16[1024,128]{1,0:T(8,128)(2,1)}) custom-call(bf16[128,4096]{1,0:T(8,128)(2,1)S(1)} %bitcast.16, bf16[128,4096]{1,0:T(8,128)(2,1)S(1)} %bitcast.26, bf16[128,4096]{1,0:T(8,128)(2,1)S(1)} %bitcast.18, bf16[128,4096]{1,0:T(8,128)(2,1)} %bitcast.20, ...), custom_call_target="tpu_custom_call" | custom-call | flops 1000000000 | bytes 8388608 | tf_op jit(solution)/shard_map/pallas_call | solution.py:281
  21.4 0.0 copy-start.10
  21.4 1.0 copy-done.10
  22.4 0.0 copy-start.12
  22.4 1.0 copy-done.12
  23.4 0.0 copy-start.8
  23.4 14.8 %all-to-all-start = ((bf16[128,8,128]{2,1,0:T(8,128)(2,1)}), bf16[128,8,128]{2,1,0:T(8,128)(2,1)S(1)}, u32[]{:S(2)}, u32[]{:S(2)}) async-start(bf16[128,8,128]{2,1,0:T(8,128)(2,1)} %bitcast.5), calls=%async_computation | async-start | bytes 524288 | tf_op jit(solution)/shard_map/all_to_all | solution.py:291
  38.2 0.0 copy-done.14
  38.2 1.9 %copy.12.residue_ref = f32[4096,16]{1,0:T(8,128)} copy(f32[4096,16]{0,1:T(8,128)S(1)} %copy-done.14) | data formatting | bytes 524288 | tf_op args[5]
  40.1 0.8 constant_dynamic-slice_fusion
  40.9 0.1 reshape.31
  41.0 0.0 copy-start.11
  41.0 1.2 %copy-done.11 = bf16[128,4096]{1,0:T(8,128)(2,1)S(1)} copy-done((bf16[128,4096]{1,0:T(8,128)(2,1)S(1)}, bf16[128,4096]{1,0:T(8,128)(2,1)}, u32[]{:S(2)}) %copy-start.11) | copy-done | bytes 1048600
  42.2 0.0 copy-start.13
  42.2 1.2 %copy-done.13 = bf16[128,4096]{1,0:T(8,128)(2,1)S(1)} copy-done((bf16[128,4096]{1,0:T(8,128)(2,1)S(1)}, bf16[128,4096]{1,0:T(8,128)(2,1)}, u32[]{:S(2)}) %copy-start.13) | copy-done | bytes 1048600
  43.4 18.9 %shard_map.103 = (f32[128,4096]{1,0:T(8,128)S(1)}, bf16[1024,128]{1,0:T(8,128)(2,1)S(1)}) custom-call(bf16[128,4096]{1,0:T(8,128)(2,1)S(1)} %copy-done.11, bf16[128,4096]{1,0:T(8,128)(2,1)S(1)} %copy-done.13, f32[16,4096]{1,0:T(8,128)S(1)} %get-tuple-element.19.rate_ref, f32[4096,16]{1,0:T(8,128)} %copy.12.residue_ref), custom_call_target="tpu_custom_call" | custom-call | flops 2000000000 | bytes 6291456 | tf_op jit(solution)/shard_map/pallas_call | solution.py:296
  62.3 0.0 copy-done.8
  62.3 0.0 copy-start.3
  62.3 1.3 %copy-done.3 = f32[128,4096]{1,0:T(8,128)} copy-done((f32[128,4096]{1,0:T(8,128)}, f32[128,4096]{1,0:T(8,128)S(1)}, u32[]{:S(2)}) %copy-start.3) | copy-done | bytes 2097176
  63.6 0.0 all-to-all-done
  63.6 0.3 shard_map.104
  64.0 0.0 copy-start.7
  64.0 0.7 copy-done.7
  64.7 0.0 copy-start.2
  64.7 12.6 %all-to-all-start.1 = ((bf16[128,8,128]{2,1,0:T(8,128)(2,1)}), bf16[128,8,128]{2,1,0:T(8,128)(2,1)S(1)}, u32[]{:S(2)}, u32[]{:S(2)}) async-start(bf16[128,8,128]{2,1,0:T(8,128)(2,1)} %bitcast.27), calls=%async_computation.1 | async-start | bytes 524288 | tf_op jit(solution)/shard_map/all_to_all | solution.py:291
  77.2 0.0 copy-start.5
  77.3 1.2 %copy-done.5 = bf16[1,128,4096]{2,1,0:T(8,128)(2,1)S(1)} copy-done((bf16[1,128,4096]{2,1,0:T(8,128)(2,1)S(1)}, bf16[1,128,4096]{2,1,0:T(8,128)(2,1)}, u32[]{:S(2)}) %copy-start.5) | copy-done | bytes 1048600
  78.5 1.7 %shard_map.105 = bf16[128,4096]{1,0:T(8,128)(2,1)} custom-call(bf16[128,4096]{1,0:T(8,128)(2,1)S(1)} %bitcast.17, bf16[128,4096]{1,0:T(8,128)(2,1)S(1)} %bitcast.24), custom_call_target="tpu_custom_call" | custom-call | flops 1000000 | bytes 3145728 | tf_op jit(solution)/shard_map/pallas_call | solution.py:325
  80.2 10.5 %all-to-all-done.1 = bf16[128,8,128]{2,1,0:T(8,128)(2,1)S(1)} async-done(((bf16[128,8,128]{2,1,0:T(8,128)(2,1)}), bf16[128,8,128]{2,1,0:T(8,128)(2,1)S(1)}, u32[]{:S(2)}, u32[]{:S(2)}) %all-to-all-start.1) | async-done | bytes 262176 | tf_op jit(solution)/shard_map/all_to_all | solution.py:291
  90.7 0.1 shard_map.107
  90.9 2.7 %collective-permute-start = (f32[8,128]{1,0:T(8,128)S(1)}, f32[8,128]{1,0:T(8,128)S(1)}, u32[]{:S(2)}, u32[]{:S(2)}) collective-permute-start(f32[8,128]{1,0:T(8,128)S(1)} %shard_map.107), channel_id=1, source_target_pairs={{0,1},{1,0},{2,3},{3,2},{4,5},{5,4},{6,7},{7,6},{8,9},{9,8},{10,11... | collective-permute-start | bytes 12296 | tf_op jit(solution)/shard_map/ppermute | solution.py:337
  93.6 0.0 copy-done.2
  93.6 0.0 copy-start.4
  93.6 1.6 %copy-done.4 = f32[128,4096]{1,0:T(8,128)S(1)} copy-done((f32[128,4096]{1,0:T(8,128)S(1)}, f32[128,4096]{1,0:T(8,128)}, u32[]{:S(2)}) %copy-start.4) | copy-done | bytes 2097176
  95.2 0.0 copy-start.9
  95.2 0.9 copy-done.9
  96.1 12.9 %shard_map.106 = (bf16[128,4096]{1,0:T(8,128)(2,1)}, bf16[128,4096]{1,0:T(8,128)(2,1)}) custom-call(f32[128,4096]{1,0:T(8,128)S(1)} %copy-done.4, bf16[1024,128]{1,0:T(8,128)(2,1)S(1)} %bitcast.23, f32[16,4096]{1,0:T(8,128)S(1)} %copy-done.9, f32[4096,16]{1,0:T(8,128)} %copy.12.residue_ref, bf16[128,4096]{1,0:T(8,128)(2,1)S(1)} %bitcast.19, ...), custom_call_target="tpu_custom_call" | custom-call | flops 1000000000 | bytes 6291456 | tf_op jit(solution)/shard_map/pallas_call | solution.py:339
  109.0 0.0 collective-permute-done
  109.0 0.7 reshape.34
  (3 shorter events, 0.0 us)
Async XLA Ops:
  0.6 3.1 %copy-start = (bf16[1,128,4096]{2,1,0:T(8,128)(2,1)S(1)}, bf16[1,128,4096]{2,1,0:T(8,128)(2,1)}, u32[]{:S(2)}) copy-start(bf16[1,128,4096]{2,1,0:T(8,128)(2,1)} %param.11) | copy-start | bytes 3145732
  0.6 3.0 %copy-start.1 = (bf16[1,128,4096]{2,1,0:T(8,128)(2,1)S(1)}, bf16[1,128,4096]{2,1,0:T(8,128)(2,1)}, u32[]{:S(2)}) copy-start(bf16[1,128,4096]{2,1,0:T(8,128)(2,1)} %param.8) | copy-start | bytes 3145732
  3.7 1.2 %copy-start.6 = (bf16[1,128,4096]{2,1,0:T(8,128)(2,1)S(1)}, bf16[1,128,4096]{2,1,0:T(8,128)(2,1)}, u32[]{:S(2)}) copy-start(bf16[1,128,4096]{2,1,0:T(8,128)(2,1)} %param.7) | copy-start | bytes 3145732
  4.9 33.3 %copy-start.14 = (f32[4096,16]{0,1:T(8,128)S(1)}, f32[4096,16]{0,1:T(8,128)}, u32[]{:S(2)}) copy-start(f32[4096,16]{0,1:T(8,128)} %param.12) | copy-start | bytes 786436
  21.4 1.0 copy-start.10
  22.4 1.0 copy-start.12
  23.4 38.9 %copy-start.8 = (f32[16,4096]{1,0:T(8,128)}, f32[16,4096]{1,0:T(8,128)S(1)}, u32[]{:S(2)}) copy-start(f32[16,4096]{1,0:T(8,128)S(1)} %get-tuple-element.19.rate_ref) | copy-start | bytes 786436
  23.4 40.2 %all-to-all-start = ((bf16[128,8,128]{2,1,0:T(8,128)(2,1)}), bf16[128,8,128]{2,1,0:T(8,128)(2,1)S(1)}, u32[]{:S(2)}, u32[]{:S(2)}) async-start(bf16[128,8,128]{2,1,0:T(8,128)(2,1)} %bitcast.5), calls=%async_computation | async-start | bytes 524288 | tf_op jit(solution)/shard_map/all_to_all | solution.py:291
  41.0 1.2 %copy-start.11 = (bf16[128,4096]{1,0:T(8,128)(2,1)S(1)}, bf16[128,4096]{1,0:T(8,128)(2,1)}, u32[]{:S(2)}) copy-start(bf16[128,4096]{1,0:T(8,128)(2,1)} %copy-done.10) | copy-start | bytes 3145732
  42.2 1.2 %copy-start.13 = (bf16[128,4096]{1,0:T(8,128)(2,1)S(1)}, bf16[128,4096]{1,0:T(8,128)(2,1)}, u32[]{:S(2)}) copy-start(bf16[128,4096]{1,0:T(8,128)(2,1)} %copy-done.12) | copy-start | bytes 3145732
  62.3 1.3 %copy-start.3 = (f32[128,4096]{1,0:T(8,128)}, f32[128,4096]{1,0:T(8,128)S(1)}, u32[]{:S(2)}) copy-start(f32[128,4096]{1,0:T(8,128)S(1)} %get-tuple-element.24.near_ref) | copy-start | bytes 6291460
  64.0 0.7 copy-start.7
  64.7 28.9 %copy-start.2 = (bf16[1,128,4096]{2,1,0:T(8,128)(2,1)S(1)}, bf16[1,128,4096]{2,1,0:T(8,128)(2,1)}, u32[]{:S(2)}) copy-start(bf16[1,128,4096]{2,1,0:T(8,128)(2,1)} %param.9) | copy-start | bytes 3145732
  64.7 26.1 %all-to-all-start.1 = ((bf16[128,8,128]{2,1,0:T(8,128)(2,1)}), bf16[128,8,128]{2,1,0:T(8,128)(2,1)S(1)}, u32[]{:S(2)}, u32[]{:S(2)}) async-start(bf16[128,8,128]{2,1,0:T(8,128)(2,1)} %bitcast.27), calls=%async_computation.1 | async-start | bytes 524288 | tf_op jit(solution)/shard_map/all_to_all | solution.py:291
  77.2 1.2 %copy-start.5 = (bf16[1,128,4096]{2,1,0:T(8,128)(2,1)S(1)}, bf16[1,128,4096]{2,1,0:T(8,128)(2,1)}, u32[]{:S(2)}) copy-start(bf16[1,128,4096]{2,1,0:T(8,128)(2,1)} %param.10) | copy-start | bytes 3145732
  90.9 18.2 %collective-permute-start = (f32[8,128]{1,0:T(8,128)S(1)}, f32[8,128]{1,0:T(8,128)S(1)}, u32[]{:S(2)}, u32[]{:S(2)}) collective-permute-start(f32[8,128]{1,0:T(8,128)S(1)} %shard_map.107), channel_id=1, source_target_pairs={{0,1},{1,0},{2,3},{3,2},{4,5},{5,4},{6,7},{7,6},{8,9},{9,8},{10,11... | collective-permute-start | bytes 12296 | tf_op jit(solution)/shard_map/ppermute | solution.py:337
  93.6 1.6 %copy-start.4 = (f32[128,4096]{1,0:T(8,128)S(1)}, f32[128,4096]{1,0:T(8,128)}, u32[]{:S(2)}) copy-start(f32[128,4096]{1,0:T(8,128)} %copy-done.3) | copy-start | bytes 6291460
  95.2 0.9 copy-start.9

commit v2 on v1

v2 whole, which is shorter than its diff:
```python
import functools
import math

import jax
import jax.numpy as jnp
from jax import lax
from jax.experimental import pallas as pl
from jax.experimental.pallas import tpu as pltpu
from jax.sharding import PartitionSpec as P

F32 = jnp.float32
BF16 = jnp.bfloat16
LANES = 128
SUB = 8
TOKENS = 128
ROWS = TOKENS // SUB
MODES = 16
QUADS = 4
WIDTH = 1024
VMEM_LIMIT = 60 * 1024 * 1024
SMALL_LIMIT = 4 * 1024 * 1024


def lane_slice(tile):
    return pl.ds(pl.multiple_of(tile * LANES, LANES), LANES)


def slab_rows(tile):
    return pl.ds(pl.multiple_of(tile * 32, 32), 32)


def gain_of(rates):
    square = rates * rates
    series = 1.0 + square * (1.0 / 6.0 + square * (1.0 / 120.0 + square * (1.0 / 5040.0)))
    return jnp.sqrt(2.0 * rates * series * jnp.exp(-rates))


def wide(row):
    return jnp.broadcast_to(row, (SUB, LANES))


def halves_sum(terms):
    while len(terms) > 1:
        terms = [x + y for x, y in zip(terms[::2], terms[1::2])]
    return terms[0]


def swap_quarters(tile):
    j = lax.broadcasted_iota(jnp.int32, (SUB, LANES), 0) & 3
    q = lax.broadcasted_iota(jnp.int32, (SUB, LANES), 1) >> 5
    for bit in (1, 2):
        j_set = (j & bit) != 0
        q_set = (q & bit) != 0
        up, down = pltpu.roll(tile, bit, 0), pltpu.roll(tile, SUB - bit, 0)
        if bit == 2:
            moved = pltpu.roll(jnp.where(j_set, up, down), 64, 1)
        else:
            moved = jnp.where(j_set, pltpu.roll(up, LANES - 32, 1), pltpu.roll(down, 32, 1))
        tile = jnp.where(j_set == q_set, tile, moved)
    return tile


def natural(tokens_sub, row):
    return tokens_sub[pl.ds(64 * (row % 2) + row // 2, SUB, stride=SUB), :]


def fold(first, second, bit, place):
    clear = (place & bit) == 0
    left = jnp.where(clear, first, pltpu.roll(second, bit, 0))
    right = jnp.where(clear, pltpu.roll(first, SUB - bit, 0), second)
    return left + right


def sublane_sums(tiles, place):
    for bit in (4, 2, 1):
        tiles = [fold(tiles[i], tiles[i + bit], bit, place) for i in range(bit)]
    return tiles[0]


def each_tile(width, body, slots=2):
    def some(at, _):
        for slot in range(slots):
            body(slots * at + slot, slot)
        return 0

    lax.fori_loop(0, width // (slots * LANES), some, 0)


def weighted_sums(state, entry, rows_of, place):
    for bit, power in ((4, 3), (2, 2), (1, 1)):
        clear = (place & bit) == 0
        weights = [rows_of(power, bit, i) for i in range(bit)]
        for which, tiles in enumerate((state, entry)):
            folded = []
            for i, weight in enumerate(weights):
                first, second = tiles[i], tiles[i + bit]
                left = jnp.where(clear, first, pltpu.roll(second, bit, 0))
                right = jnp.where(clear, pltpu.roll(first, SUB - bit, 0), second)
                folded.append(left + weight * right if which == 0 else right + weight * left)
            if which == 0:
                state = folded
            else:
                entry = folded
    return state[0], entry[0]


def summary_kernel(
    grad_ref, query_ref, key_ref, value_ref, rate_ref,
    mixed_ref, product_ref, state_ref, entry_ref, send_ref,
    powers, full,
):
    rates = rate_ref[...]
    for index, power in enumerate((1.0, 16.0, 32.0, 64.0)):
        powers[index] = jnp.exp(-power * rates)
    place = lax.broadcasted_iota(jnp.int32, (SUB, LANES), 0)

    def body(tile, slot):
        lanes = lane_slice(tile)
        mixed_full, product_full = full.at[slot, 0], full.at[slot, 1]
        mixed = (grad_ref[:, lanes].astype(F32) * query_ref[:, lanes].astype(F32)).astype(BF16)
        product = (key_ref[:, lanes].astype(F32) * value_ref[:, lanes].astype(F32)).astype(BF16)
        mixed_full[...] = mixed.astype(F32)
        product_full[...] = product.astype(F32)
        g = [mixed_full[pl.ds(j, SUB, stride=ROWS), :] for j in range(ROWS)]
        p = [product_full[pl.ds(j, SUB, stride=ROWS), :] for j in range(ROWS)]
        for j in range(0, ROWS, 2):
            rows = slice(SUB * j, SUB * j + 16)
            mixed_ref[rows, lanes] = jnp.concatenate([g[j], g[j + 1]], axis=0).astype(BF16)
            product_ref[rows, lanes] = jnp.concatenate([p[j], p[j + 1]], axis=0).astype(BF16)
        sums = []
        for half in range(2):
            states, entries = [], []
            for base in range(SUB * half, SUB * half + SUB, 4):
                group = range(base, base + 4)
                one = [wide(powers[0, m : m + 1, lanes]) for m in group]
                state = [g[ROWS - 1]] * 4
                entry = [p[0] * a for a in one]
                for i in range(1, ROWS):
                    state = [s * a + g[ROWS - 1 - i] for s, a in zip(state, one)]
                    entry = [(e + p[i]) * a for e, a in zip(entry, one)]
                for s, e, m in zip(state, entry, group):
                    state_ref[SUB * m : SUB * m + SUB, lanes] = s
                    entry_ref[SUB * m : SUB * m + SUB, lanes] = e
                states += state
                entries += entry

            def rows_of(power, bit, i):
                if bit == 1:
                    return powers[power, SUB * half : SUB * half + SUB, lanes]
                modes = [SUB * half + i + bit * at for at in range(SUB // bit)]
                out = wide(powers[power, modes[-1] : modes[-1] + 1, lanes])
                for at in range(len(modes) - 2, -1, -1):
                    out = jnp.where(place < bit * (at + 1), wide(powers[power, modes[at] : modes[at] + 1, lanes]), out)
                return out

            s, e = weighted_sums(states, entries, rows_of, place)
            low = place < 4
            sums += [jnp.where(low, s, pltpu.roll(e, 4, 0)), jnp.where(low, pltpu.roll(s, 4, 0), e)]
        send_ref[slab_rows(tile), :] = jnp.concatenate(sums, axis=0).astype(BF16)

    each_tile(grad_ref.shape[1], body)


def local_kernel(
    scale, mixed_ref, product_ref, state_ref, entry_ref, rate_ref, residue_ref,
    near_ref, lead_ref, send_ref,
    powers, weights, taps, lags, slabs, runs,
):
    rates = rate_ref[...]
    powers[...] = jnp.exp(-rates)
    gains = gain_of(rates)
    term = residue_ref[...] * gains
    for d in range(ROWS):
        taps[d : d + 1, :] = jnp.sum(term, axis=0, keepdims=True)
        term = term * powers[...]
        if d == 0:
            weights[...] = term
    for index, power in enumerate((16.0, 32.0, 64.0)):
        runs[index] = jnp.exp(-power * rates)
    place = lax.broadcasted_iota(jnp.int32, (SUB, LANES), 0)

    def body(tile, slot):
        lanes = lane_slice(tile)
        g, p = [], []
        for j in range(0, ROWS, 2):
            rows = slice(SUB * j, SUB * j + 16)
            pair = mixed_ref[rows, lanes].astype(F32)
            g += [pair[:SUB, :], pair[SUB:, :]]
            pair = product_ref[rows, lanes].astype(F32)
            p += [pair[:SUB, :], pair[SUB:, :]]
        near = [None] * ROWS
        for d in range(ROWS):
            tap = wide(taps[d : d + 1, lanes])
            for j in range(ROWS - d):
                near[j] = tap * g[j + d] if d == 0 else near[j] + tap * g[j + d]
        for j in range(ROWS):
            near_ref[SUB * j : SUB * j + SUB, lanes] = near[j]
        lag = []
        for d in range(ROWS):
            total = g[d] * p[0]
            for j in range(1, ROWS - d):
                total = total + g[j + d] * p[j]
            lag.append(total)
        for half in range(2):
            rows = slice(SUB * half, SUB * half + SUB)
            lags[0, rows, lanes] = sublane_sums(lag[rows], place)
            cross = []
            for m in range(SUB * half, SUB * half + SUB):
                mode_rows = slice(SUB * m, SUB * m + SUB)
                carry = state_ref[mode_rows, lanes]
                for index, step in ((0, 1), (1, 2), (2, 4)):
                    later = jnp.where(place < SUB - step, pltpu.roll(carry, SUB - step, 0), 0.0)
                    carry = carry + wide(runs[index, m : m + 1, lanes]) * later
                carry = jnp.where(place < SUB - 1, pltpu.roll(carry, SUB - 1, 0), 0.0)
                cross.append(carry * entry_ref[mode_rows, lanes])
                lead_ref[mode_rows, lanes] = carry * wide(weights[m : m + 1, lanes])
            lags[1, rows, lanes] = sublane_sums(cross, place)

    each_tile(mixed_ref.shape[1], body)
    coef = jnp.broadcast_to(lags[0, ROWS - 1 : ROWS, :], rates.shape)
    for d in range(ROWS - 2, -1, -1):
        coef = coef * powers[...] + lags[0, d : d + 1, :]
    lags[1] = (coef + lags[1]) * gains * scale
    slabs[...] = jnp.zeros_like(slabs)

    def ship(tile, slot):
        lanes = lane_slice(tile)
        slab = slabs.at[slot]
        for pair in range(2):
            moved = swap_quarters(lags[1, SUB * pair : SUB * pair + SUB, lanes])
            for k in range(2):
                for q in range(4):
                    row = SUB * q + 4 + 2 * pair + k
                    slab[row : row + 1, :] = moved[4 * k + q : 4 * k + q + 1, :]
        send_ref[slab_rows(tile), :] = slab[...].astype(BF16)

    each_tile(mixed_ref.shape[1], ship, 8)


def scan_kernel(scale, received_ref, coef_ref, rate_ref, send_ref):
    blocks = received_ref.shape[0] // SUB
    rates = rate_ref[...]
    decay = jnp.exp(-float(TOKENS) * rates)
    place = lax.broadcasted_iota(jnp.int32, (SUB, LANES), 0)
    low = place < 4

    def step(back, held):
        state, far = held
        start = pl.multiple_of((blocks // 2 - 1 - back) * 16, 16)
        pair = received_ref[pl.ds(start, 16), :].astype(F32)
        coef = coef_ref[pl.ds(start, 16), :].astype(F32)
        out = [None, None]
        for which in (1, 0):
            here = pair[SUB * which : SUB * which + SUB, :]
            out[which] = jnp.where(low, state, coef[SUB * which : SUB * which + SUB, :])
            far = far + here * state
            state = jnp.where(low, here, pltpu.roll(here, 4, 0)) + decay * state
        send_ref[pl.ds(start, 16), :] = jnp.concatenate(out, axis=0).astype(BF16)
        return state, far

    zero = jnp.zeros((SUB, LANES), F32)
    _, far = lax.fori_loop(0, blocks // 2, step, (zero, zero), unroll=4)
    far = swap_quarters(far * gain_of(rates) * scale)
    me = lax.axis_index("ctx")
    mine = slab_rows(me // QUADS)
    extra = [jnp.where(place == 4 + me % QUADS, wide(far[4 + q : 5 + q, :]), 0.0) for q in range(QUADS)]
    send_ref[mine, :] = (send_ref[mine, :].astype(F32) + jnp.concatenate(extra, axis=0)).astype(BF16)


def total_kernel(received_ref, out_ref):
    def step(at, held):
        rows = received_ref[pl.ds(pl.multiple_of(at * 16, 16), 16), :].astype(F32)
        return held[0] + rows[:SUB, :], held[1] + rows[SUB:, :]

    zero = jnp.zeros((SUB, LANES), F32)
    first, second = lax.fori_loop(0, received_ref.shape[0] // 16, step, (zero, zero), unroll=8)
    out_ref[...] = first + second


def output_kernel(
    near_ref, lead_ref, received_ref, rate_ref, residue_ref, key_ref, value_ref,
    grad_key_ref, grad_value_ref,
    powers, weights, slabs, mixes,
):
    rates = rate_ref[...]
    powers[...] = jnp.exp(-rates)
    weights[...] = residue_ref[...] * gain_of(rates) * powers[...]
    back = (16 * (SUB - 1 - lax.broadcasted_iota(jnp.int32, (SUB, LANES), 0))).astype(F32)

    def body(tile, slot):
        lanes = lane_slice(tile)
        slab, mix_sub = slabs.at[slot], mixes.at[slot]
        slab[...] = received_ref[slab_rows(tile), :].astype(F32)
        one = [wide(powers[m : m + 1, lanes]) for m in range(MODES)]
        state = []
        for m in range(MODES):
            row = SUB * (m // 4) + m % 4
            head = wide(slab[row : row + 1, :] * weights[m : m + 1, lanes])
            reach = jnp.exp(-back * wide(rate_ref[m : m + 1, lanes]))
            state.append(lead_ref[SUB * m : SUB * m + SUB, lanes] + head * reach)
        for j in range(ROWS - 1, -1, -1):
            rows = slice(SUB * j, SUB * j + SUB)
            mix_sub[rows, :] = near_ref[rows, lanes] + halves_sum(state)
            if j > 0:
                state = [s * a for s, a in zip(state, one)]
        for i in range(0, ROWS, 2):
            rows = slice(SUB * i, SUB * i + 16)
            mix = jnp.concatenate([natural(mix_sub, i), natural(mix_sub, i + 1)], axis=0).astype(BF16).astype(F32)
            grad_key_ref[rows, lanes] = (mix * value_ref[rows, lanes].astype(F32)).astype(BF16)
            grad_value_ref[rows, lanes] = (mix * key_ref[rows, lanes].astype(F32)).astype(BF16)

    each_tile(near_ref.shape[1], body)


def gate_kernel(grad_ref, conv_ref, out_ref):
    out_ref[...] = (grad_ref[...].astype(F32) * conv_ref[...].astype(F32)).astype(BF16)


def call(kernel, grid, in_specs, out_specs, out_shape, scratch=(), flops=10**6, moved=2**20, limit=VMEM_LIMIT):
    return pl.pallas_call(
        kernel,
        grid=grid,
        in_specs=in_specs,
        out_specs=out_specs,
        out_shape=out_shape,
        scratch_shapes=scratch,
        compiler_params=pltpu.CompilerParams(vmem_limit_bytes=limit),
        cost_estimate=pl.CostEstimate(flops=flops, bytes_accessed=moved, transcendentals=0),
    )


def local(query_rows, key_rows, value_rows, conv_rows, grad_rows, residues, decay_rates):
    blocks = lax.axis_size("ctx")
    tokens, channels = query_rows.shape[1:]
    own = channels // blocks
    scale = 1.0 / math.sqrt(blocks * tokens)
    query, key, value, conv, grad = (x[0] for x in (query_rows, key_rows, value_rows, conv_rows, grad_rows))
    rates, residue = decay_rates.T, residues.T

    def table(*shape):
        return pltpu.VMEM(shape, F32)

    token_block = pl.BlockSpec((tokens, WIDTH), lambda n: (0, n))
    mode_block = pl.BlockSpec((MODES, WIDTH), lambda n: (0, n))
    slab_block = pl.BlockSpec((WIDTH // LANES * 32, LANES), lambda n: (n, 0))
    token_half = jax.ShapeDtypeStruct((tokens, channels), BF16)
    token_full = jax.ShapeDtypeStruct((tokens, channels), F32)
    slabs = jax.ShapeDtypeStruct((blocks * SUB, LANES), BF16)
    steps = (channels // WIDTH,)

    mixed, product, states, entries, summary = call(
        summary_kernel, steps,
        [token_block] * 4 + [mode_block],
        [token_block] * 4 + [slab_block],
        [token_half, token_half, token_full, token_full, slabs],
        [table(4, MODES, WIDTH), table(2, 2, TOKENS, LANES)],
        10**9, 10 * 2**20,
    )(grad, query, key, value, rates)

    def exchange(rows):
        moved = lax.all_to_all(rows.reshape(blocks, SUB, LANES), "ctx", split_axis=0, concat_axis=0, tiled=True)
        return moved.reshape(blocks * SUB, LANES)

    received = exchange(summary)

    near, lead, coef_slabs = call(
        functools.partial(local_kernel, scale), steps,
        [token_block] * 4 + [mode_block] * 2,
        [token_block, token_block, slab_block],
        [token_full, token_full, slabs],
        [
            table(MODES, WIDTH), table(MODES, WIDTH), table(MODES, WIDTH), table(2, MODES, WIDTH),
            table(8, 32, LANES), table(3, MODES, WIDTH),
        ],
        10**9, 10 * 2**20,
    )(mixed, product, states, entries, rates, residue)

    me = lax.axis_index("ctx")
    rates_late, _ = lax.optimization_barrier((rates, summary))
    rate_own = lax.dynamic_slice(rates_late, (4 * (me % QUADS), LANES * (me // QUADS)), (4, LANES))
    rate_own = jnp.concatenate([rate_own, rate_own], axis=0)

    vmem = pl.BlockSpec(memory_space=pltpu.VMEM)
    carries = call(
        functools.partial(scan_kernel, scale), (), [vmem] * 3, vmem, slabs, limit=SMALL_LIMIT
    )(received, coef_slabs, rate_own)

    returned = exchange(carries)

    gate_in, _ = lax.optimization_barrier((conv, carries))
    gate_block = pl.BlockSpec((tokens, channels // 4), lambda n: (0, n))
    grad_query = call(gate_kernel, (4,), [gate_block] * 2, gate_block, token_half, moved=3 * 2**20)(grad, gate_in)

    coef_part = call(
        total_kernel, (), [vmem], vmem, jax.ShapeDtypeStruct((SUB, LANES), F32), limit=SMALL_LIMIT
    )(returned)
    other = lax.ppermute(coef_part, "dp", [(0, 1), (1, 0)])

    grad_key, grad_value = call(
        output_kernel, steps,
        [token_block, token_block, slab_block, mode_block, mode_block, token_block, token_block],
        [token_block] * 2, [token_half] * 2,
        [table(MODES, WIDTH), table(MODES, WIDTH), table(2, 32, LANES), table(2, TOKENS, LANES)],
        10**9, 9 * 2**20,
    )(near, lead, returned, rates, residue, key, value)

    coef = (coef_part + other)[4:].reshape(MODES, own).T
    return (grad_query[None], grad_key[None], grad_value[None], coef)


def solution(mesh):
    rows = P("dp", "ctx", None)
    return jax.shard_map(
        local,
        mesh=mesh,
        in_specs=(rows, rows, rows, rows, rows, P(), P()),
        out_specs=(rows, rows, rows, P("ctx", None)),
        check_vma=False,
    )
```

time: 110 us -> 74.2 us (0.67)
  Pallas kernels: 50.5 us -> 30.9 us
  local copies, waits for them, and re-layouts: 17.9 us -> 2.4 us
  starting transfers between devices: 30.1 us -> 25.9 us
  waiting for transfers between devices: 10.5 us -> 13.9 us
    pallas_call x6, Pallas kernels: 50.5 us -> 30.9 us  [the longest x1 10.1 us: local(): call(summary_kernel, steps, [token_block] * 4 + [mode_block], [token_bloc...]
    unnamed x32 -> x4, local copies, waits for them, and re-layouts: 16.3 us -> 0.95 us
    all_to_all x2, starting transfers between devices: 27.4 us -> 23.2 us  [exchange(): lax.all_to_all(rows.reshape(blocks, SUB, LANES), 'ctx', split_axis=0, con...]
    all_to_all x2, waiting for transfers between devices: 10.5 us -> 13.9 us  [exchange(): lax.all_to_all(rows.reshape(blocks, SUB, LANES), 'ctx', split_axis=0, con...]
  transfers between devices with their start and end apart: 3 -> 3, of which waited for: 1 -> 2; matrix products, arithmetic and copies ran while one was open for 3% -> 1% of each run, Pallas kernels for 31% -> 26%
where the time goes in v2:
time: 74.2 us; the launch traced here: 73.8 us
  Pallas kernels  30.9 us (42%)
  starting transfers between devices  25.9 us (35%)
  waiting for transfers between devices  13.9 us (19%)
  local copies, waits for them, and re-layouts  2.4 us (3%)
    all_to_all x2, starting transfers between devices, exchange(): lax.all_to_all(rows.reshape(blocks, SUB, LANES), 'ctx', split_axis=0, con...  23.2 us
    all_to_all x2, waiting for transfers between devices, exchange(): lax.all_to_all(rows.reshape(blocks, SUB, LANES), 'ctx', split_axis=0, con...  13.9 us
    pallas_call x1, Pallas kernels, local(): call(summary_kernel, steps, [token_block] * 4 + [mode_block], [token_bloc...  10.1 us
    pallas_call x1, Pallas kernels, local(): call(functools.partial(local_kernel, scale), steps, [token_block] * 4 + [...  8.65 us
    pallas_call x1, Pallas kernels, local(): call(output_kernel, steps, [token_block, token_block, slab_block, mode_bl...  7.17 us
    pallas_call x1, Pallas kernels, local(): call(gate_kernel, (4,), [gate_block] * 2, gate_block, token_half, moved=3...  3.64 us
    ppermute x1, starting transfers between devices, local(): other = lax.ppermute(coef_part, 'dp', [(0, 1), (1, 0)])  2.71 us
  transfers between devices with their start and end apart: 3, of which 2 were waited for; matrix products, arithmetic and copies ran while one was open for 1% of the time, Pallas kernels for 26%

profile of v2, /device:TPU:1, one launch (start us, length us, event | category | flops | bytes accessed | tf_op | source)
XLA Modules:
  0.0 73.8 jit_solution(15372447145548341510)
XLA Ops:
  0.6 10.1 %shard_map.102 = (bf16[128,4096]{1,0:T(8,128)(2,1)}, bf16[128,4096]{1,0:T(8,128)(2,1)}, f32[128,4096]{1,0:T(8,128)}, f32[128,4096]{1,0:T(8,128)}, bf16[1024,128]{1,0:T(8,128)(2,1)}) custom-call(bf16[128,4096]{1,0:T(8,128)(2,1)} %bitcast.18, bf16[128,4096]{1,0:T(8,128)(2,1)} %bitcast.28, bf16[128,4096]{1,0:T(8,128)(2,1)} %bitcast.20, ...), custom_call_target="tpu_custom_call" | custom-call | flops 1000000000 | bytes 10485760 | tf_op jit(solution)/shard_map/pallas_call | solution.py:351
  10.7 14.8 %all-to-all-start = ((bf16[128,8,128]{2,1,0:T(8,128)(2,1)}), bf16[128,8,128]{2,1,0:T(8,128)(2,1)S(1)}, u32[]{:S(2)}, u32[]{:S(2)}) async-start(bf16[128,8,128]{2,1,0:T(8,128)(2,1)} %bitcast.33), calls=%async_computation | async-start | bytes 524288 | tf_op jit(solution)/shard_map/all_to_all | solution.py:361
  25.5 0.8 %dynamic_slice.3 = f32[4,128]{1,0:T(4,128)S(1)} dynamic-slice(f32[16,4096]{1,0:T(8,128)} %bitcast.25, s32[]{:T(128)S(6)} %select_n.18, s32[]{:T(128)S(6)} %select_n.20), dynamic_slice_sizes={4,128} | dynamic-slice | bytes 4100 | tf_op jit(solution)/shard_map/dynamic_slice | solution.py:380
  26.3 8.6 %shard_map.103 = (f32[128,4096]{1,0:T(8,128)}, f32[128,4096]{1,0:T(8,128)}, bf16[1024,128]{1,0:T(8,128)(2,1)}) custom-call(bf16[128,4096]{1,0:T(8,128)(2,1)} %get-tuple-element.17.mixed_ref, bf16[128,4096]{1,0:T(8,128)(2,1)} %get-tuple-element.18.product_ref, f32[128,4096]{1,0:T(8,128)} %get-tuple-element.19.state_ref, ...), custom_call_target="tpu_custom_call" | custom-call | flops 1000000000 | bytes 10485760 | tf_op jit(solution)/shard_map/pallas_call | solution.py:366
  35.0 4.0 %all-to-all-done = bf16[128,8,128]{2,1,0:T(8,128)(2,1)S(1)} async-done(((bf16[128,8,128]{2,1,0:T(8,128)(2,1)}), bf16[128,8,128]{2,1,0:T(8,128)(2,1)S(1)}, u32[]{:S(2)}, u32[]{:S(2)}) %all-to-all-start) | async-done | bytes 262176 | tf_op jit(solution)/shard_map/all_to_all | solution.py:361
  39.0 0.0 copy-start.1
  39.0 0.9 %copy-done.1 = bf16[1024,128]{1,0:T(8,128)(2,1)S(1)} copy-done((bf16[1024,128]{1,0:T(8,128)(2,1)S(1)}, bf16[1024,128]{1,0:T(8,128)(2,1)}, u32[]{:S(2)}) %copy-start.1) | copy-done | bytes 262168
  40.0 1.2 %shard_map.104 = bf16[1024,128]{1,0:T(8,128)(2,1)} custom-call(bf16[1024,128]{1,0:T(8,128)(2,1)S(1)} %bitcast.17, bf16[1024,128]{1,0:T(8,128)(2,1)S(1)} %copy-done.1, f32[8,128]{1,0:T(8,128)S(1)} %pad_maximum_fusion.rate_ref), custom_call_target="tpu_custom_call" | custom-call | flops 1000000 | bytes 1048576 | tf_op jit(solution)/shard_map/pallas_call | solution.py:384
  41.2 8.4 %all-to-all-start.1 = ((bf16[128,8,128]{2,1,0:T(8,128)(2,1)}), bf16[128,8,128]{2,1,0:T(8,128)(2,1)S(1)}, u32[]{:S(2)}, u32[]{:S(2)}) async-start(bf16[128,8,128]{2,1,0:T(8,128)(2,1)} %bitcast.10), calls=%async_computation.1 | async-start | bytes 524288 | tf_op jit(solution)/shard_map/all_to_all | solution.py:361
  49.6 3.6 %shard_map.105 = bf16[128,4096]{1,0:T(8,128)(2,1)} custom-call(bf16[128,4096]{1,0:T(8,128)(2,1)} %bitcast.19, bf16[128,4096]{1,0:T(8,128)(2,1)} %bitcast.29), custom_call_target="tpu_custom_call" | custom-call | flops 1000000 | bytes 3145728 | tf_op jit(solution)/shard_map/pallas_call | solution.py:392
  53.2 9.9 %all-to-all-done.1 = bf16[128,8,128]{2,1,0:T(8,128)(2,1)S(1)} async-done(((bf16[128,8,128]{2,1,0:T(8,128)(2,1)}), bf16[128,8,128]{2,1,0:T(8,128)(2,1)S(1)}, u32[]{:S(2)}, u32[]{:S(2)}) %all-to-all-start.1) | async-done | bytes 262176 | tf_op jit(solution)/shard_map/all_to_all | solution.py:361
  63.1 0.0 copy-start
  63.1 0.1 shard_map.107
  63.2 2.7 %collective-permute-start = (f32[8,128]{1,0:T(8,128)S(1)}, f32[8,128]{1,0:T(8,128)S(1)}, u32[]{:S(2)}, u32[]{:S(2)}) collective-permute-start(f32[8,128]{1,0:T(8,128)S(1)} %shard_map.107), channel_id=1, source_target_pairs={{0,1},{1,0},{2,3},{3,2},{4,5},{5,4},{6,7},{7,6},{8,9},{9,8},{10,11... | collective-permute-start | bytes 12296 | tf_op jit(solution)/shard_map/ppermute | solution.py:397
  65.9 0.0 copy-done
  65.9 7.2 %shard_map.106 = (bf16[128,4096]{1,0:T(8,128)(2,1)}, bf16[128,4096]{1,0:T(8,128)(2,1)}) custom-call(f32[128,4096]{1,0:T(8,128)} %get-tuple-element.24.near_ref, f32[128,4096]{1,0:T(8,128)} %get-tuple-element.25.lead_ref, bf16[1024,128]{1,0:T(8,128)(2,1)} %bitcast.16, f32[16,4096]{1,0:T(8,128)} %bitcast.27, f32[16,4096]{1,0:T(8,128)} %bitcast.32, ...), custom_call_target="tpu_custom_call" | custom-call | flops 1000000000 | bytes 9437184 | tf_op jit(solution)/shard_map/pallas_call | solution.py:399
  73.1 0.0 collective-permute-done
  73.1 0.7 reshape.27
  (3 shorter events, 0.0 us)
Async XLA Ops:
  10.7 28.3 %all-to-all-start = ((bf16[128,8,128]{2,1,0:T(8,128)(2,1)}), bf16[128,8,128]{2,1,0:T(8,128)(2,1)S(1)}, u32[]{:S(2)}, u32[]{:S(2)}) async-start(bf16[128,8,128]{2,1,0:T(8,128)(2,1)} %bitcast.33), calls=%async_computation | async-start | bytes 524288 | tf_op jit(solution)/shard_map/all_to_all | solution.py:361
  39.0 1.0 %copy-start.1 = (bf16[1024,128]{1,0:T(8,128)(2,1)S(1)}, bf16[1024,128]{1,0:T(8,128)(2,1)}, u32[]{:S(2)}) copy-start(bf16[1024,128]{1,0:T(8,128)(2,1)} %get-tuple-element.21.coef_ref) | copy-start | bytes 786436
  41.2 21.9 %all-to-all-start.1 = ((bf16[128,8,128]{2,1,0:T(8,128)(2,1)}), bf16[128,8,128]{2,1,0:T(8,128)(2,1)S(1)}, u32[]{:S(2)}, u32[]{:S(2)}) async-start(bf16[128,8,128]{2,1,0:T(8,128)(2,1)} %bitcast.10), calls=%async_computation.1 | async-start | bytes 524288 | tf_op jit(solution)/shard_map/all_to_all | solution.py:361
  63.1 2.8 %copy-start = (bf16[128,8,128]{2,1,0:T(8,128)(2,1)}, bf16[128,8,128]{2,1,0:T(8,128)(2,1)S(1)}, u32[]{:S(2)}) copy-start(bf16[128,8,128]{2,1,0:T(8,128)(2,1)S(1)} %all-to-all-done.1) | copy-start | bytes 786436
  63.2 9.9 %collective-permute-start = (f32[8,128]{1,0:T(8,128)S(1)}, f32[8,128]{1,0:T(8,128)S(1)}, u32[]{:S(2)}, u32[]{:S(2)}) collective-permute-start(f32[8,128]{1,0:T(8,128)S(1)} %shard_map.107), channel_id=1, source_target_pairs={{0,1},{1,0},{2,3},{3,2},{4,5},{5,4},{6,7},{7,6},{8,9},{9,8},{10,11... | collective-permute-start | bytes 12296 | tf_op jit(solution)/shard_map/ppermute | solution.py:397

commit v3 on v2

--- a/solution.py
+++ b/solution.py
@@ -19,6 +19,7 @@
 WIDTH = 1024
 VMEM_LIMIT = 60 * 1024 * 1024
 SMALL_LIMIT = 4 * 1024 * 1024
+STREAM_LIMIT = 40 * 1024 * 1024
 
 
 def lane_slice(tile):
@@ -274,30 +275,65 @@
 
     zero = jnp.zeros((SUB, LANES), F32)
     first, second = lax.fori_loop(0, received_ref.shape[0] // 16, step, (zero, zero), unroll=8)
-    out_ref[...] = first + second
+    total = first + second
+    width = out_ref.shape[1]
+    for k in range(QUADS):
+        for j in range(4):
+            out_ref[4 * k + j : 4 * k + j + 1, :] = total[4 + k : 5 + k, width * j : width * j + width]
+
+
+def stage_kernel(
+    rate_far, residue_far, near_far, lead_far, key_far, value_far,
+    reach_far, power_far, near_head, lead_head, reach_head, power_head, key_head, value_head,
+    rate_ref, residue_ref, reach_ref, power_ref, weights, sems,
+):
+    width = near_head.shape[1]
+    pairs = [(rate_far, rate_ref), (residue_far, residue_ref)]
+    heads = ((near_far, near_head), (lead_far, lead_head), (key_far, key_head), (value_far, value_head))
+    pairs += [(far.at[:, pl.ds(0, width)], head) for far, head in heads]
+    coming = [pltpu.make_async_copy(*pair, sems.at[i]) for i, pair in enumerate(pairs)]
+    for each in coming:
+        each.start()
+    for each in coming[:2]:
+        each.wait()
+    power_ref[...] = jnp.exp(-rate_ref[...])
+    weights[...] = residue_ref[...] * gain_of(rate_ref[...]) * power_ref[...]
+    back = (16 * (SUB - 1 - lax.broadcasted_iota(jnp.int32, (SUB, LANES), 0))).astype(F32)
+
+    def body(tile, slot):
+        lanes = lane_slice(tile)
+        for m in range(MODES):
+            reach = jnp.exp(-back * wide(rate_ref[m : m + 1, lanes]))
+            reach_ref[SUB * m : SUB * m + SUB, lanes] = reach * wide(weights[m : m + 1, lanes])
+
+    each_tile(rate_ref.shape[1], body)
+    going = [
+        pltpu.make_async_copy(reach_ref, reach_far, sems.at[len(pairs)]),
+        pltpu.make_async_copy(power_ref, power_far, sems.at[len(pairs) + 1]),
+    ]
+    for each in going:
+        each.start()
+    reach_head[...] = reach_ref[:, :width]
+    power_head[...] = power_ref[:, :width]
+    for each in coming[2:] + going:
+        each.wait()
 
 
 def output_kernel(
-    near_ref, lead_ref, received_ref, rate_ref, residue_ref, key_ref, value_ref,
+    near_ref, lead_ref, reach_ref, power_ref, key_ref, value_ref, received_ref,
     grad_key_ref, grad_value_ref,
-    powers, weights, slabs, mixes,
+    slabs, mixes,
 ):
-    rates = rate_ref[...]
-    powers[...] = jnp.exp(-rates)
-    weights[...] = residue_ref[...] * gain_of(rates) * powers[...]
-    back = (16 * (SUB - 1 - lax.broadcasted_iota(jnp.int32, (SUB, LANES), 0))).astype(F32)
-
     def body(tile, slot):
         lanes = lane_slice(tile)
         slab, mix_sub = slabs.at[slot], mixes.at[slot]
         slab[...] = received_ref[slab_rows(tile), :].astype(F32)
-        one = [wide(powers[m : m + 1, lanes]) for m in range(MODES)]
+        one = [wide(power_ref[m : m + 1, lanes]) for m in range(MODES)]
         state = []
         for m in range(MODES):
             row = SUB * (m // 4) + m % 4
-            head = wide(slab[row : row + 1, :] * weights[m : m + 1, lanes])
-            reach = jnp.exp(-back * wide(rate_ref[m : m + 1, lanes]))
-            state.append(lead_ref[SUB * m : SUB * m + SUB, lanes] + head * reach)
+            rows = slice(SUB * m, SUB * m + SUB)
+            state.append(lead_ref[rows, lanes] + wide(slab[row : row + 1, :]) * reach_ref[rows, lanes])
         for j in range(ROWS - 1, -1, -1):
             rows = slice(SUB * j, SUB * j + SUB)
             mix_sub[rows, :] = near_ref[rows, lanes] + halves_sum(state)
@@ -313,7 +349,78 @@
 
 
 def gate_kernel(grad_ref, conv_ref, out_ref):
-    out_ref[...] = (grad_ref[...].astype(F32) * conv_ref[...].astype(F32)).astype(BF16)
+    def body(tile, slot):
+        lanes = lane_slice(tile)
+        out_ref[:, lanes] = (grad_ref[:, lanes].astype(F32) * conv_ref[:, lanes].astype(F32)).astype(BF16)
+
+    each_tile(grad_ref.shape[1], body)
+
+
+def streamed(body, ins, outs, width, scratch, flops, moved, heads=(), ahead=3):
+    arrays = [x for x, _ in ins + outs]
+    n_in, n_all = len(ins), len(ins) + len(outs)
+    stays = [kept for _, kept in ins + outs]
+    steps = max(x.shape[1] for x in arrays) // width
+    moving = [i for i in range(n_all) if not stays[i]]
+    first = 1 if heads else 0
+
+    def block(ref, at):
+        if ref.shape[1] == LANES:
+            size = width // LANES * 32
+            return ref.at[pl.ds(pl.multiple_of(at * size, size), size), :]
+        return ref.at[:, pl.ds(pl.multiple_of(at * width, width), width)]
+
+    def kernel(*refs):
+        ready = refs[n_in : n_in + len(heads)]
+        refs = refs[:n_in] + refs[n_in + len(heads) :]
+        places = dict(zip(moving, refs[n_all : n_all + len(moving)]))
+        sems, *extra = refs[n_all + len(moving) :]
+
+        def copy(i, at):
+            ends = (block(refs[i], at), block(places[i], at))
+            return pltpu.make_async_copy(*(ends if i < n_in else ends[::-1]), sems.at[i, at])
+
+        coming = [i for i in moving if i < n_in]
+        going = [i for i in moving if i >= n_in]
+        for at in range(first, min(first + ahead, steps)):
+            for i in coming:
+                copy(i, at).start()
+
+        def work(at, held):
+            body(*(held.get(i, block(places.get(i, refs[i]), at)) for i in range(n_all)), *extra)
+            for i in going:
+                copy(i, at).start()
+
+        def step(at, _):
+            @pl.when(at + ahead < steps)
+            def _():
+                for i in coming:
+                    copy(i, at + ahead).start()
+
+            for i in coming:
+                copy(i, at).wait()
+            work(at, {})
+            return 0
+
+        if heads:
+            work(0, dict(zip(coming, ready)))
+        lax.fori_loop(first, steps, step, 0)
+        for at in range(steps):
+            for i in going:
+                copy(i, at).wait()
+
+    space = [pltpu.VMEM if kept else pltpu.HBM for kept in stays]
+    specs = [pl.BlockSpec(memory_space=kind) for kind in space]
+    held = [pltpu.with_memory_space_constraint(x, kind) for x, kind in zip(arrays[:n_in], space)]
+    held += [pltpu.with_memory_space_constraint(x, pltpu.VMEM) for x in heads]
+    results = [kind(x.shape, x.dtype) for x, kind in zip(arrays[n_in:], space[n_in:])]
+    return call(
+        kernel, (), specs[:n_in] + [pl.BlockSpec(memory_space=pltpu.VMEM)] * len(heads), specs[n_in:], results,
+        [pltpu.VMEM(arrays[i].shape, arrays[i].dtype) for i in moving]
+        + [pltpu.SemaphoreType.DMA((n_all, steps))]
+        + scratch,
+        flops, moved, STREAM_LIMIT,
+    )(*held)
 
 
 def call(kernel, grid, in_specs, out_specs, out_shape, scratch=(), flops=10**6, moved=2**20, limit=VMEM_LIMIT):
@@ -363,17 +470,17 @@
 
     received = exchange(summary)
 
-    near, lead, coef_slabs = call(
-        functools.partial(local_kernel, scale), steps,
-        [token_block] * 4 + [mode_block] * 2,
-        [token_block, token_block, slab_block],
-        [token_full, token_full, slabs],
+    near, lead, coef_slabs = streamed(
+        functools.partial(local_kernel, scale),
+        [(x, False) for x in (mixed, product, states, entries, rates, residue)],
+        [(token_full, False), (token_full, False), (slabs, True)],
+        WIDTH,
         [
             table(MODES, WIDTH), table(MODES, WIDTH), table(MODES, WIDTH), table(2, MODES, WIDTH),
             table(8, 32, LANES), table(3, MODES, WIDTH),
         ],
         10**9, 10 * 2**20,
-    )(mixed, product, states, entries, rates, residue)
+    )
 
     me = lax.axis_index("ctx")
     rates_late, _ = lax.optimization_barrier((rates, summary))
@@ -387,24 +494,34 @@
 
     returned = exchange(carries)
 
-    gate_in, _ = lax.optimization_barrier((conv, carries))
-    gate_block = pl.BlockSpec((tokens, channels // 4), lambda n: (0, n))
-    grad_query = call(gate_kernel, (4,), [gate_block] * 2, gate_block, token_half, moved=3 * 2**20)(grad, gate_in)
+    gate_in, key_late, value_late, _ = lax.optimization_barrier((conv, key, value, carries))
+    far_spec, near_spec = pl.BlockSpec(memory_space=pltpu.HBM), pl.BlockSpec(memory_space=pltpu.VMEM)
+    head_types = [pltpu.VMEM((x.shape[0], WIDTH), x.dtype) for x in (near, lead, near, rates, key, value)]
+    reach, power, *heads = call(
+        stage_kernel, (), [far_spec] * 6, [far_spec] * 2 + [near_spec] * 6,
+        [pltpu.HBM(near.shape, F32), pltpu.HBM(rates.shape, F32)] + head_types,
+        [pltpu.VMEM(x.shape, F32) for x in (rates, rates, near, rates, rates)] + [pltpu.SemaphoreType.DMA((8,))],
+        10**9, 4 * 2**20, STREAM_LIMIT,
+    )(*(pltpu.with_memory_space_constraint(x, pltpu.HBM) for x in (rates, residue, near, lead, key_late, value_late)))
+    grad_query = streamed(
+        gate_kernel, [(grad, False), (gate_in, False)], [(token_half, False)], WIDTH, [], 10**6, 3 * 2**20
+    )[0]
 
     coef_part = call(
-        total_kernel, (), [vmem], vmem, jax.ShapeDtypeStruct((SUB, LANES), F32), limit=SMALL_LIMIT
+        total_kernel, (), [vmem], vmem, jax.ShapeDtypeStruct((MODES, own), F32), limit=SMALL_LIMIT
     )(returned)
     other = lax.ppermute(coef_part, "dp", [(0, 1), (1, 0)])
 
-    grad_key, grad_value = call(
-        output_kernel, steps,
-        [token_block, token_block, slab_block, mode_block, mode_block, token_block, token_block],
-        [token_block] * 2, [token_half] * 2,
-        [table(MODES, WIDTH), table(MODES, WIDTH), table(2, 32, LANES), table(2, TOKENS, LANES)],
-        10**9, 9 * 2**20,
-    )(near, lead, returned, rates, residue, key, value)
-
-    coef = (coef_part + other)[4:].reshape(MODES, own).T
+    grad_key, grad_value = streamed(
+        output_kernel,
+        [(x, False) for x in (near, lead, reach, power, key, value)] + [(returned, True)],
+        [(token_half, False), (token_half, False)],
+        WIDTH,
+        [table(2, 32, LANES), table(2, TOKENS, LANES)],
+        10**9, 9 * 2**20, heads,
+    )
+
+    coef = (coef_part + other).T
     return (grad_query[None], grad_key[None], grad_value[None], coef)
 
 

time: 74.2 us -> 71.8 us (0.968)
  waiting for transfers between devices: 13.9 us -> 11.3 us
  local copies, waits for them, and re-layouts: 2.4 us -> 0.77 us
  Pallas kernels: 30.9 us -> 31.9 us
    all_to_all x2, waiting for transfers between devices: 13.9 us -> 11.3 us  [exchange(): lax.all_to_all(rows.reshape(blocks, SUB, LANES), 'ctx', split_axis=0, con...]
    pallas_call x4 -> x5, Pallas kernels: 19.6 us -> 20.6 us  [the longest x3 17.1 us: streamed(): call(kernel, (), specs[:n_in] + [pl.BlockSpec(memory_space=pltpu.VMEM)] *...]
    unnamed x4 -> x0, local copies, waits for them, and re-layouts: 0.95 us -> none
  transfers between devices with their start and end apart: 3 -> 3, of which waited for: 2 -> 2; matrix products, arithmetic and copies ran while one was open for 1% -> 1% of each run, Pallas kernels for 26% -> 28%
where the time goes in v3:
time: 71.8 us; the launch traced here: 71.5 us
  Pallas kernels  31.9 us (44%)
  starting transfers between devices  26.2 us (36%)
  waiting for transfers between devices  11.3 us (16%)
  local copies, waits for them, and re-layouts  0.77 us (1%)
  between operations  0.73 us (1%)
    all_to_all x2, starting transfers between devices, exchange(): lax.all_to_all(rows.reshape(blocks, SUB, LANES), 'ctx', split_axis=0, con...  23.5 us
    pallas_call x3, Pallas kernels, streamed(): call(kernel, (), specs[:n_in] + [pl.BlockSpec(memory_space=pltpu.VMEM)] *...  17.1 us
    all_to_all x2, waiting for transfers between devices, exchange(): lax.all_to_all(rows.reshape(blocks, SUB, LANES), 'ctx', split_axis=0, con...  11.3 us
    pallas_call x1, Pallas kernels, local(): call(summary_kernel, steps, [token_block] * 4 + [mode_block], [token_bloc...  10.1 us
    pallas_call x1, Pallas kernels, local(): call(stage_kernel, (), [far_spec] * 6, [far_spec] * 2 + [near_spec] * 6,...  3.33 us
    ppermute x1, starting transfers between devices, local(): other = lax.ppermute(coef_part, 'dp', [(0, 1), (1, 0)])  2.65 us
  transfers between devices with their start and end apart: 3, of which 2 were waited for; matrix products, arithmetic and copies ran while one was open for 1% of the time, Pallas kernels for 28%

profile of v3, /device:TPU:1, one launch (start us, length us, event | category | flops | bytes accessed | tf_op | source)
XLA Modules:
  0.0 71.5 jit_solution(14285006755744345718)
XLA Ops:
  0.6 10.1 %shard_map.102 = (bf16[128,4096]{1,0:T(8,128)(2,1)}, bf16[128,4096]{1,0:T(8,128)(2,1)}, f32[128,4096]{1,0:T(8,128)}, f32[128,4096]{1,0:T(8,128)}, bf16[1024,128]{1,0:T(8,128)(2,1)}) custom-call(bf16[128,4096]{1,0:T(8,128)(2,1)} %bitcast.25, bf16[128,4096]{1,0:T(8,128)(2,1)} %bitcast.31, bf16[128,4096]{1,0:T(8,128)(2,1)} %bitcast.19, ...), custom_call_target="tpu_custom_call" | custom-call | flops 1000000000 | bytes 10485760 | tf_op jit(solution)/shard_map/pallas_call | solution.py:458
  10.8 14.8 %all-to-all-start = ((bf16[128,8,128]{2,1,0:T(8,128)(2,1)}), bf16[128,8,128]{2,1,0:T(8,128)(2,1)S(1)}, u32[]{:S(2)}, u32[]{:S(2)}) async-start(bf16[128,8,128]{2,1,0:T(8,128)(2,1)} %bitcast.36), calls=%async_computation | async-start | bytes 524288 | tf_op jit(solution)/shard_map/all_to_all | solution.py:468
  25.6 0.8 %dynamic_slice.3 = f32[4,128]{1,0:T(4,128)S(1)} dynamic-slice(f32[16,4096]{1,0:T(8,128)} %bitcast.28, s32[]{:T(128)S(6)} %select_n.18, s32[]{:T(128)S(6)} %select_n.20), dynamic_slice_sizes={4,128} | dynamic-slice | bytes 4100 | tf_op jit(solution)/shard_map/dynamic_slice | solution.py:487
  26.3 9.0 %shard_map.103 = (f32[128,4096]{1,0:T(8,128)}, f32[128,4096]{1,0:T(8,128)}, bf16[1024,128]{1,0:T(8,128)(2,1)S(1)}) custom-call(bf16[128,4096]{1,0:T(8,128)(2,1)} %get-tuple-element.27.refs_0_, bf16[128,4096]{1,0:T(8,128)(2,1)} %get-tuple-element.28.refs_1_, f32[128,4096]{1,0:T(8,128)} %get-tuple-element.29.refs_2_, f32[128,4096]{1,0:T(8,128)} %get-tuple-element.30.refs_3_, ...), custom_call_target="tpu_custom_call" | custom-call | flops 1000000000 | bytes 10485760 | tf_op jit(solution)/shard_map/pallas_call | solution.py:417
  35.3 3.7 %all-to-all-done = bf16[128,8,128]{2,1,0:T(8,128)(2,1)S(1)} async-done(((bf16[128,8,128]{2,1,0:T(8,128)(2,1)}), bf16[128,8,128]{2,1,0:T(8,128)(2,1)S(1)}, u32[]{:S(2)}, u32[]{:S(2)}) %all-to-all-start) | async-done | bytes 262176 | tf_op jit(solution)/shard_map/all_to_all | solution.py:468
  39.0 1.2 %shard_map.104 = bf16[1024,128]{1,0:T(8,128)(2,1)} custom-call(bf16[1024,128]{1,0:T(8,128)(2,1)S(1)} %bitcast.18, bf16[1024,128]{1,0:T(8,128)(2,1)S(1)} %get-tuple-element.31.coef_ref, f32[8,128]{1,0:T(8,128)S(1)} %pad_maximum_fusion.rate_ref), custom_call_target="tpu_custom_call" | custom-call | flops 1000000 | bytes 1048576 | tf_op jit(solution)/shard_map/pallas_call | solution.py:491
  40.3 8.7 %all-to-all-start.1 = ((bf16[128,8,128]{2,1,0:T(8,128)(2,1)}), bf16[128,8,128]{2,1,0:T(8,128)(2,1)S(1)}, u32[]{:S(2)}, u32[]{:S(2)}) async-start(bf16[128,8,128]{2,1,0:T(8,128)(2,1)} %bitcast.10), calls=%async_computation.1 | async-start | bytes 524288 | tf_op jit(solution)/shard_map/all_to_all | solution.py:468
  49.0 2.6 %shard_map.105 = bf16[128,4096]{1,0:T(8,128)(2,1)} custom-call(bf16[128,4096]{1,0:T(8,128)(2,1)} %bitcast.26, bf16[128,4096]{1,0:T(8,128)(2,1)} %bitcast.32), custom_call_target="tpu_custom_call" | custom-call | flops 1000000 | bytes 3145728 | tf_op jit(solution)/shard_map/pallas_call | solution.py:417
  51.6 3.3 %shard_map.106 = (f32[128,4096]{1,0:T(8,128)}, f32[16,4096]{1,0:T(8,128)}, f32[128,1024]{1,0:T(8,128)S(1)}, f32[128,1024]{1,0:T(8,128)S(1)}, f32[128,1024]{1,0:T...) custom-call(f32[16,4096]{1,0:T(8,128)} %bitcast.30, ...), custom_call_target="tpu_custom_call" | custom-call | flops 1000000000 | bytes 4194304 | tf_op jit(solution)/shard_map/pallas_call | solution.py:500
  54.9 7.6 %all-to-all-done.1 = bf16[128,8,128]{2,1,0:T(8,128)(2,1)S(1)} async-done(((bf16[128,8,128]{2,1,0:T(8,128)(2,1)}), bf16[128,8,128]{2,1,0:T(8,128)(2,1)S(1)}, u32[]{:S(2)}, u32[]{:S(2)}) %all-to-all-start.1) | async-done | bytes 262176 | tf_op jit(solution)/shard_map/all_to_all | solution.py:468
  62.5 0.2 shard_map.108
  62.7 2.7 %collective-permute-start = (f32[16,32]{1,0:T(8,128)S(1)}, f32[16,32]{1,0:T(8,128)S(1)}, u32[]{:S(2)}, u32[]{:S(2)}) collective-permute-start(f32[16,32]{1,0:T(8,128)S(1)} %shard_map.108), channel_id=1, source_target_pairs={{0,1},{1,0},{2,3},{3,2},{4,5},{5,4},{6,7},{7,6},{8,9},{9,8},{10,11... | collective-permute-start | bytes 6152 | tf_op jit(solution)/shard_map/ppermute | solution.py:513
  65.3 5.5 %shard_map.107 = (bf16[128,4096]{1,0:T(8,128)(2,1)}, bf16[128,4096]{1,0:T(8,128)(2,1)}) custom-call(f32[128,4096]{1,0:T(8,128)} %get-tuple-element.34.near_far.refs_0_, f32[128,4096]{1,0:T(8,128)} %get-tuple-element.35.lead_far.refs_1_, f32[128,4096]{1,0:T(8,128)} %get-tuple-element.38.refs_2_, f32[16,4096]{1,0:T(8,128)} %get-tuple-element.39.refs_3_, ...), custom_call_target="tpu_custom_call" | custom-call | flops 1000000000 | bytes 9437184 | tf_op jit(solution)/shard_map/pallas_call | solution.py:417
  70.9 0.0 collective-permute-done
  70.9 0.6 add_bitcast_fusion
  (1 shorter events, 0.0 us)
Async XLA Ops:
  10.8 28.3 %all-to-all-start = ((bf16[128,8,128]{2,1,0:T(8,128)(2,1)}), bf16[128,8,128]{2,1,0:T(8,128)(2,1)S(1)}, u32[]{:S(2)}, u32[]{:S(2)}) async-start(bf16[128,8,128]{2,1,0:T(8,128)(2,1)} %bitcast.36), calls=%async_computation | async-start | bytes 524288 | tf_op jit(solution)/shard_map/all_to_all | solution.py:468
  40.3 22.2 %all-to-all-start.1 = ((bf16[128,8,128]{2,1,0:T(8,128)(2,1)}), bf16[128,8,128]{2,1,0:T(8,128)(2,1)S(1)}, u32[]{:S(2)}, u32[]{:S(2)}) async-start(bf16[128,8,128]{2,1,0:T(8,128)(2,1)} %bitcast.10), calls=%async_computation.1 | async-start | bytes 524288 | tf_op jit(solution)/shard_map/all_to_all | solution.py:468
  62.7 8.2 %collective-permute-start = (f32[16,32]{1,0:T(8,128)S(1)}, f32[16,32]{1,0:T(8,128)S(1)}, u32[]{:S(2)}, u32[]{:S(2)}) collective-permute-start(f32[16,32]{1,0:T(8,128)S(1)} %shard_map.108), channel_id=1, source_target_pairs={{0,1},{1,0},{2,3},{3,2},{4,5},{5,4},{6,7},{7,6},{8,9},{9,8},{10,11... | collective-permute-start | bytes 6152 | tf_op jit(solution)/shard_map/ppermute | solution.py:513

commit v4 on v3

--- a/solution.py
+++ b/solution.py
@@ -164,18 +164,13 @@
 
 def local_kernel(
     scale, mixed_ref, product_ref, state_ref, entry_ref, rate_ref, residue_ref,
-    near_ref, lead_ref, send_ref,
-    powers, weights, taps, lags, slabs, runs,
+    lead_ref, send_ref,
+    powers, weights, lags, slabs, runs,
 ):
     rates = rate_ref[...]
     powers[...] = jnp.exp(-rates)
     gains = gain_of(rates)
-    term = residue_ref[...] * gains
-    for d in range(ROWS):
-        taps[d : d + 1, :] = jnp.sum(term, axis=0, keepdims=True)
-        term = term * powers[...]
-        if d == 0:
-            weights[...] = term
+    weights[...] = residue_ref[...] * gains * powers[...]
     for index, power in enumerate((16.0, 32.0, 64.0)):
         runs[index] = jnp.exp(-power * rates)
     place = lax.broadcasted_iota(jnp.int32, (SUB, LANES), 0)
@@ -189,13 +184,6 @@
             g += [pair[:SUB, :], pair[SUB:, :]]
             pair = product_ref[rows, lanes].astype(F32)
             p += [pair[:SUB, :], pair[SUB:, :]]
-        near = [None] * ROWS
-        for d in range(ROWS):
-            tap = wide(taps[d : d + 1, lanes])
-            for j in range(ROWS - d):
-                near[j] = tap * g[j + d] if d == 0 else near[j] + tap * g[j + d]
-        for j in range(ROWS):
-            near_ref[SUB * j : SUB * j + SUB, lanes] = near[j]
         lag = []
         for d in range(ROWS):
             total = g[d] * p[0]
@@ -245,23 +233,25 @@
     place = lax.broadcasted_iota(jnp.int32, (SUB, LANES), 0)
     low = place < 4
 
+    squared = decay * decay
+    gains = gain_of(rates) * scale
+
     def step(back, held):
-        state, far = held
+        state, far, far_even = held
         start = pl.multiple_of((blocks // 2 - 1 - back) * 16, 16)
         pair = received_ref[pl.ds(start, 16), :].astype(F32)
         coef = coef_ref[pl.ds(start, 16), :].astype(F32)
-        out = [None, None]
-        for which in (1, 0):
-            here = pair[SUB * which : SUB * which + SUB, :]
-            out[which] = jnp.where(low, state, coef[SUB * which : SUB * which + SUB, :])
-            far = far + here * state
-            state = jnp.where(low, here, pltpu.roll(here, 4, 0)) + decay * state
+        even, odd = pair[:SUB, :], pair[SUB:, :]
+        odd_own = jnp.where(low, odd, pltpu.roll(odd, 4, 0))
+        even_own = jnp.where(low, even, pltpu.roll(even, 4, 0))
+        before = odd_own + decay * state
+        out = [jnp.where(low, before, coef[:SUB, :]), jnp.where(low, state, coef[SUB:, :])]
         send_ref[pl.ds(start, 16), :] = jnp.concatenate(out, axis=0).astype(BF16)
-        return state, far
+        return (even_own + decay * odd_own) + squared * state, far + odd * state, far_even + even * before
 
     zero = jnp.zeros((SUB, LANES), F32)
-    _, far = lax.fori_loop(0, blocks // 2, step, (zero, zero), unroll=4)
-    far = swap_quarters(far * gain_of(rates) * scale)
+    _, far, far_even = lax.fori_loop(0, blocks // 2, step, (zero, zero, zero), unroll=8)
+    far = swap_quarters((far + far_even) * gains)
     me = lax.axis_index("ctx")
     mine = slab_rows(me // QUADS)
     extra = [jnp.where(place == 4 + me % QUADS, wide(far[4 + q : 5 + q, :]), 0.0) for q in range(QUADS)]
@@ -283,13 +273,13 @@
 
 
 def stage_kernel(
-    rate_far, residue_far, near_far, lead_far, key_far, value_far,
-    reach_far, power_far, near_head, lead_head, reach_head, power_head, key_head, value_head,
-    rate_ref, residue_ref, reach_ref, power_ref, weights, sems,
+    mixed_far, rate_far, residue_far, lead_far, key_far, value_far,
+    near_far, reach_far, power_far, near_head, lead_head, reach_head, power_head, key_head, value_head,
+    mixed_ref, rate_ref, residue_ref, near_ref, reach_ref, power_ref, weights, taps, sems,
 ):
     width = near_head.shape[1]
-    pairs = [(rate_far, rate_ref), (residue_far, residue_ref)]
-    heads = ((near_far, near_head), (lead_far, lead_head), (key_far, key_head), (value_far, value_head))
+    heads = ((lead_far, lead_head), (key_far, key_head), (value_far, value_head))
+    pairs = [(rate_far, rate_ref), (residue_far, residue_ref), (mixed_far, mixed_ref)]
     pairs += [(far.at[:, pl.ds(0, width)], head) for far, head in heads]
     coming = [pltpu.make_async_copy(*pair, sems.at[i]) for i, pair in enumerate(pairs)]
     for each in coming:
@@ -297,25 +287,41 @@
     for each in coming[:2]:
         each.wait()
     power_ref[...] = jnp.exp(-rate_ref[...])
-    weights[...] = residue_ref[...] * gain_of(rate_ref[...]) * power_ref[...]
+    term = residue_ref[...] * gain_of(rate_ref[...])
+    for d in range(ROWS):
+        taps[d : d + 1, :] = jnp.sum(term, axis=0, keepdims=True)
+        term = term * power_ref[...]
+        if d == 0:
+            weights[...] = term
     back = (16 * (SUB - 1 - lax.broadcasted_iota(jnp.int32, (SUB, LANES), 0))).astype(F32)
+    coming[2].wait()
 
     def body(tile, slot):
         lanes = lane_slice(tile)
+        g = []
+        for j in range(0, ROWS, 2):
+            pair = mixed_ref[SUB * j : SUB * j + 16, lanes].astype(F32)
+            g += [pair[:SUB, :], pair[SUB:, :]]
+        near = [None] * ROWS
+        for d in range(ROWS):
+            tap = wide(taps[d : d + 1, lanes])
+            for j in range(ROWS - d):
+                near[j] = tap * g[j + d] if d == 0 else near[j] + tap * g[j + d]
+        for j in range(ROWS):
+            near_ref[SUB * j : SUB * j + SUB, lanes] = near[j]
         for m in range(MODES):
             reach = jnp.exp(-back * wide(rate_ref[m : m + 1, lanes]))
             reach_ref[SUB * m : SUB * m + SUB, lanes] = reach * wide(weights[m : m + 1, lanes])
 
     each_tile(rate_ref.shape[1], body)
-    going = [
-        pltpu.make_async_copy(reach_ref, reach_far, sems.at[len(pairs)]),
-        pltpu.make_async_copy(power_ref, power_far, sems.at[len(pairs) + 1]),
-    ]
+    tables = ((near_ref, near_far), (reach_ref, reach_far), (power_ref, power_far))
+    going = [pltpu.make_async_copy(*pair, sems.at[len(pairs) + i]) for i, pair in enumerate(tables)]
     for each in going:
         each.start()
+    near_head[...] = near_ref[:, :width]
     reach_head[...] = reach_ref[:, :width]
     power_head[...] = power_ref[:, :width]
-    for each in coming[2:] + going:
+    for each in coming[3:] + going:
         each.wait()
 
 
@@ -470,13 +476,13 @@
 
     received = exchange(summary)
 
-    near, lead, coef_slabs = streamed(
+    lead, coef_slabs = streamed(
         functools.partial(local_kernel, scale),
         [(x, False) for x in (mixed, product, states, entries, rates, residue)],
-        [(token_full, False), (token_full, False), (slabs, True)],
+        [(token_full, False), (slabs, True)],
         WIDTH,
         [
-            table(MODES, WIDTH), table(MODES, WIDTH), table(MODES, WIDTH), table(2, MODES, WIDTH),
+            table(MODES, WIDTH), table(MODES, WIDTH), table(2, MODES, WIDTH),
             table(8, 32, LANES), table(3, MODES, WIDTH),
         ],
         10**9, 10 * 2**20,
@@ -494,15 +500,20 @@
 
     returned = exchange(carries)
 
-    gate_in, key_late, value_late, _ = lax.optimization_barrier((conv, key, value, carries))
+    gate_in, key_late, value_late, mixed_late, _ = lax.optimization_barrier((conv, key, value, mixed, carries))
     far_spec, near_spec = pl.BlockSpec(memory_space=pltpu.HBM), pl.BlockSpec(memory_space=pltpu.VMEM)
-    head_types = [pltpu.VMEM((x.shape[0], WIDTH), x.dtype) for x in (near, lead, near, rates, key, value)]
-    reach, power, *heads = call(
-        stage_kernel, (), [far_spec] * 6, [far_spec] * 2 + [near_spec] * 6,
-        [pltpu.HBM(near.shape, F32), pltpu.HBM(rates.shape, F32)] + head_types,
-        [pltpu.VMEM(x.shape, F32) for x in (rates, rates, near, rates, rates)] + [pltpu.SemaphoreType.DMA((8,))],
+    head_types = [pltpu.VMEM((x.shape[0], WIDTH), x.dtype) for x in (lead, lead, lead, rates, key, value)]
+    near, reach, power, *heads = call(
+        stage_kernel, (), [far_spec] * 6, [far_spec] * 3 + [near_spec] * 6,
+        [pltpu.HBM(x.shape, F32) for x in (lead, lead, rates)] + head_types,
+        [pltpu.VMEM(mixed.shape, BF16)]
+        + [pltpu.VMEM(x.shape, F32) for x in (rates, rates, lead, lead, rates, rates, rates)]
+        + [pltpu.SemaphoreType.DMA((9,))],
         10**9, 4 * 2**20, STREAM_LIMIT,
-    )(*(pltpu.with_memory_space_constraint(x, pltpu.HBM) for x in (rates, residue, near, lead, key_late, value_late)))
+    )(*(
+        pltpu.with_memory_space_constraint(x, pltpu.HBM)
+        for x in (mixed_late, rates, residue, lead, key_late, value_late)
+    ))
     grad_query = streamed(
         gate_kernel, [(grad, False), (gate_in, False)], [(token_half, False)], WIDTH, [], 10**6, 3 * 2**20
     )[0]

time: 71.8 us -> 69.6 us (0.969)
  starting transfers between devices: 26.2 us -> 24.1 us
    pallas_call x1, Pallas kernels: 3.33 us -> 6.18 us  [local(): call(stage_kernel, (), [far_spec] * 6, [far_spec] * 3 + [near_spec] * 6,...]
    all_to_all x2, starting transfers between devices: 23.5 us -> 21.4 us  [exchange(): lax.all_to_all(rows.reshape(blocks, SUB, LANES), 'ctx', split_axis=0, con...]
    pallas_call x3, Pallas kernels: 17.1 us -> 14.9 us  [streamed(): call(kernel, (), specs[:n_in] + [pl.BlockSpec(memory_space=pltpu.VMEM)] *...]
    all_to_all x2, waiting for transfers between devices: 11.3 us -> 10.6 us  [exchange(): lax.all_to_all(rows.reshape(blocks, SUB, LANES), 'ctx', split_axis=0, con...]
  transfers between devices with their start and end apart: 3 -> 3, of which waited for: 2 -> 2; matrix products, arithmetic and copies ran while one was open for 1% -> 1% of each run, Pallas kernels for 28% -> 31%
where the time goes in v4:
time: 69.6 us; the launch traced here: 69.2 us
  Pallas kernels  32.5 us (47%)
  starting transfers between devices  24.1 us (35%)
  waiting for transfers between devices  10.6 us (15%)
  local copies, waits for them, and re-layouts  0.77 us (1%)
  between operations  0.73 us (1%)
    all_to_all x2, starting transfers between devices, exchange(): lax.all_to_all(rows.reshape(blocks, SUB, LANES), 'ctx', split_axis=0, con...  21.4 us
    pallas_call x3, Pallas kernels, streamed(): call(kernel, (), specs[:n_in] + [pl.BlockSpec(memory_space=pltpu.VMEM)] *...  14.9 us
    all_to_all x2, waiting for transfers between devices, exchange(): lax.all_to_all(rows.reshape(blocks, SUB, LANES), 'ctx', split_axis=0, con...  10.6 us
    pallas_call x1, Pallas kernels, local(): call(summary_kernel, steps, [token_block] * 4 + [mode_block], [token_bloc...  10.1 us
    pallas_call x1, Pallas kernels, local(): call(stage_kernel, (), [far_spec] * 6, [far_spec] * 3 + [near_spec] * 6,...  6.18 us
    ppermute x1, starting transfers between devices, local(): other = lax.ppermute(coef_part, 'dp', [(0, 1), (1, 0)])  2.65 us
  transfers between devices with their start and end apart: 3, of which 2 were waited for; matrix products, arithmetic and copies ran while one was open for 1% of the time, Pallas kernels for 31%

profile of v4, /device:TPU:1, one launch (start us, length us, event | category | flops | bytes accessed | tf_op | source)
XLA Modules:
  0.0 69.2 jit_solution(14250546184356361577)
XLA Ops:
  0.6 10.1 %shard_map.102 = (bf16[128,4096]{1,0:T(8,128)(2,1)}, bf16[128,4096]{1,0:T(8,128)(2,1)}, f32[128,4096]{1,0:T(8,128)}, f32[128,4096]{1,0:T(8,128)}, bf16[1024,128]{1,0:T(8,128)(2,1)}) custom-call(bf16[128,4096]{1,0:T(8,128)(2,1)} %bitcast.25, bf16[128,4096]{1,0:T(8,128)(2,1)} %bitcast.31, bf16[128,4096]{1,0:T(8,128)(2,1)} %bitcast.19, ...), custom_call_target="tpu_custom_call" | custom-call | flops 1000000000 | bytes 10485760 | tf_op jit(solution)/shard_map/pallas_call | solution.py:464
  10.8 14.8 %all-to-all-start = ((bf16[128,8,128]{2,1,0:T(8,128)(2,1)}), bf16[128,8,128]{2,1,0:T(8,128)(2,1)S(1)}, u32[]{:S(2)}, u32[]{:S(2)}) async-start(bf16[128,8,128]{2,1,0:T(8,128)(2,1)} %bitcast.36), calls=%async_computation | async-start | bytes 524288 | tf_op jit(solution)/shard_map/all_to_all | solution.py:474
  25.6 0.8 %dynamic_slice.3 = f32[4,128]{1,0:T(4,128)S(1)} dynamic-slice(f32[16,4096]{1,0:T(8,128)} %bitcast.28, s32[]{:T(128)S(6)} %select_n.18, s32[]{:T(128)S(6)} %select_n.20), dynamic_slice_sizes={4,128} | dynamic-slice | bytes 4100 | tf_op jit(solution)/shard_map/dynamic_slice | solution.py:493
  26.4 6.8 %shard_map.103 = (f32[128,4096]{1,0:T(8,128)}, bf16[1024,128]{1,0:T(8,128)(2,1)S(1)}) custom-call(bf16[128,4096]{1,0:T(8,128)(2,1)} %get-tuple-element.35.refs_0_.mixed_far, bf16[128,4096]{1,0:T(8,128)(2,1)} %get-tuple-element.29.refs_1_, f32[128,4096]{1,0:T(8,128)} %get-tuple-element.30.refs_2_, f32[128,4096]{1,0:T(8,128)} %get-tuple-element.31.refs_3_, ...), custom_call_target="tpu_custom_call" | custom-call | flops 1000000000 | bytes 10485760 | tf_op jit(solution)/shard_map/pallas_call | solution.py:423
  33.2 5.8 %all-to-all-done = bf16[128,8,128]{2,1,0:T(8,128)(2,1)S(1)} async-done(((bf16[128,8,128]{2,1,0:T(8,128)(2,1)}), bf16[128,8,128]{2,1,0:T(8,128)(2,1)S(1)}, u32[]{:S(2)}, u32[]{:S(2)}) %all-to-all-start) | async-done | bytes 262176 | tf_op jit(solution)/shard_map/all_to_all | solution.py:474
  39.0 1.1 %shard_map.104 = bf16[1024,128]{1,0:T(8,128)(2,1)} custom-call(bf16[1024,128]{1,0:T(8,128)(2,1)S(1)} %bitcast.18, bf16[1024,128]{1,0:T(8,128)(2,1)S(1)} %get-tuple-element.32.coef_ref, f32[8,128]{1,0:T(8,128)S(1)} %pad_maximum_fusion.rate_ref), custom_call_target="tpu_custom_call" | custom-call | flops 1000000 | bytes 1048576 | tf_op jit(solution)/shard_map/pallas_call | solution.py:497
  40.1 6.6 %all-to-all-start.1 = ((bf16[128,8,128]{2,1,0:T(8,128)(2,1)}), bf16[128,8,128]{2,1,0:T(8,128)(2,1)S(1)}, u32[]{:S(2)}, u32[]{:S(2)}) async-start(bf16[128,8,128]{2,1,0:T(8,128)(2,1)} %bitcast.10), calls=%async_computation.1 | async-start | bytes 524288 | tf_op jit(solution)/shard_map/all_to_all | solution.py:474
  46.8 2.6 %shard_map.105 = bf16[128,4096]{1,0:T(8,128)(2,1)} custom-call(bf16[128,4096]{1,0:T(8,128)(2,1)} %bitcast.26, bf16[128,4096]{1,0:T(8,128)(2,1)} %bitcast.32), custom_call_target="tpu_custom_call" | custom-call | flops 1000000 | bytes 3145728 | tf_op jit(solution)/shard_map/pallas_call | solution.py:423
  49.4 6.2 %shard_map.106 = (f32[128,4096]{1,0:T(8,128)}, f32[128,4096]{1,0:T(8,128)}, f32[16,4096]{1,0:T(8,128)}, f32[128,1024]{1,0:T(8,128)S(1)}, f32[128,1024]{1,0:T(8,1...) custom-call(bf16[128,4096]{1,0:T(8,128)(2,1)} %get-tuple-element.35., ...), custom_call_target="tpu_custom_call" | custom-call | flops 1000000000 | bytes 4194304 | tf_op jit(solution)/shard_map/pallas_call | solution.py:506
  55.5 4.7 %all-to-all-done.1 = bf16[128,8,128]{2,1,0:T(8,128)(2,1)S(1)} async-done(((bf16[128,8,128]{2,1,0:T(8,128)(2,1)}), bf16[128,8,128]{2,1,0:T(8,128)(2,1)S(1)}, u32[]{:S(2)}, u32[]{:S(2)}) %all-to-all-start.1) | async-done | bytes 262176 | tf_op jit(solution)/shard_map/all_to_all | solution.py:474
  60.3 0.2 shard_map.108
  60.4 2.7 %collective-permute-start = (f32[16,32]{1,0:T(8,128)S(1)}, f32[16,32]{1,0:T(8,128)S(1)}, u32[]{:S(2)}, u32[]{:S(2)}) collective-permute-start(f32[16,32]{1,0:T(8,128)S(1)} %shard_map.108), channel_id=1, source_target_pairs={{0,1},{1,0},{2,3},{3,2},{4,5},{5,4},{6,7},{7,6},{8,9},{9,8},{10,11... | collective-permute-start | bytes 6152 | tf_op jit(solution)/shard_map/ppermute | solution.py:524
  63.1 5.5 %shard_map.107 = (bf16[128,4096]{1,0:T(8,128)(2,1)}, bf16[128,4096]{1,0:T(8,128)(2,1)}) custom-call(f32[128,4096]{1,0:T(8,128)} %get-tuple-element.39.refs_0_, f32[128,4096]{1,0:T(8,128)} %get-tuple-element.36.lead_far.refs_1_, f32[128,4096]{1,0:T(8,128)} %get-tuple-element.40.refs_2_, f32[16,4096]{1,0:T(8,128)} %get-tuple-element.41.refs_3_, ...), custom_call_target="tpu_custom_call" | custom-call | flops 1000000000 | bytes 9437184 | tf_op jit(solution)/shard_map/pallas_call | solution.py:423
  68.6 0.0 collective-permute-done
  68.6 0.6 add_bitcast_fusion
  (1 shorter events, 0.0 us)
Async XLA Ops:
  10.8 28.3 %all-to-all-start = ((bf16[128,8,128]{2,1,0:T(8,128)(2,1)}), bf16[128,8,128]{2,1,0:T(8,128)(2,1)S(1)}, u32[]{:S(2)}, u32[]{:S(2)}) async-start(bf16[128,8,128]{2,1,0:T(8,128)(2,1)} %bitcast.36), calls=%async_computation | async-start | bytes 524288 | tf_op jit(solution)/shard_map/all_to_all | solution.py:474
  40.1 20.1 %all-to-all-start.1 = ((bf16[128,8,128]{2,1,0:T(8,128)(2,1)}), bf16[128,8,128]{2,1,0:T(8,128)(2,1)S(1)}, u32[]{:S(2)}, u32[]{:S(2)}) async-start(bf16[128,8,128]{2,1,0:T(8,128)(2,1)} %bitcast.10), calls=%async_computation.1 | async-start | bytes 524288 | tf_op jit(solution)/shard_map/all_to_all | solution.py:474
  60.4 8.2 %collective-permute-start = (f32[16,32]{1,0:T(8,128)S(1)}, f32[16,32]{1,0:T(8,128)S(1)}, u32[]{:S(2)}, u32[]{:S(2)}) collective-permute-start(f32[16,32]{1,0:T(8,128)S(1)} %shard_map.108), channel_id=1, source_target_pairs={{0,1},{1,0},{2,3},{3,2},{4,5},{5,4},{6,7},{7,6},{8,9},{9,8},{10,11... | collective-permute-start | bytes 6152 | tf_op jit(solution)/shard_map/ppermute | solution.py:524

commit v5 on v4

--- a/solution.py
+++ b/solution.py
@@ -16,6 +16,7 @@
 ROWS = TOKENS // SUB
 MODES = 16
 QUADS = 4
+PITCH = 24
 WIDTH = 1024
 VMEM_LIMIT = 60 * 1024 * 1024
 SMALL_LIMIT = 4 * 1024 * 1024
@@ -26,8 +27,8 @@
     return pl.ds(pl.multiple_of(tile * LANES, LANES), LANES)
 
 
-def slab_rows(tile):
-    return pl.ds(pl.multiple_of(tile * 32, 32), 32)
+def slab_rows(tile, tiles):
+    return pl.ds(pl.multiple_of((tiles - 1 - tile) * 32, 32), 32)
 
 
 def gain_of(rates):
@@ -120,10 +121,13 @@
         mixed_full, product_full = full.at[slot, 0], full.at[slot, 1]
         mixed = (grad_ref[:, lanes].astype(F32) * query_ref[:, lanes].astype(F32)).astype(BF16)
         product = (key_ref[:, lanes].astype(F32) * value_ref[:, lanes].astype(F32)).astype(BF16)
-        mixed_full[...] = mixed.astype(F32)
-        product_full[...] = product.astype(F32)
-        g = [mixed_full[pl.ds(j, SUB, stride=ROWS), :] for j in range(ROWS)]
-        p = [product_full[pl.ds(j, SUB, stride=ROWS), :] for j in range(ROWS)]
+        mixed, product = mixed.astype(F32), product.astype(F32)
+        for i in range(ROWS):
+            at, rows = PITCH * (i // 2) + SUB * (i % 2), slice(SUB * i, SUB * i + SUB)
+            mixed_full[at : at + SUB, :] = mixed[rows, :]
+            product_full[at : at + SUB, :] = product[rows, :]
+        g = [mixed_full[pl.ds(j, SUB, stride=PITCH), :] for j in range(ROWS)]
+        p = [product_full[pl.ds(j, SUB, stride=PITCH), :] for j in range(ROWS)]
         for j in range(0, ROWS, 2):
             rows = slice(SUB * j, SUB * j + 16)
             mixed_ref[rows, lanes] = jnp.concatenate([g[j], g[j + 1]], axis=0).astype(BF16)
@@ -157,7 +161,8 @@
             s, e = weighted_sums(states, entries, rows_of, place)
             low = place < 4
             sums += [jnp.where(low, s, pltpu.roll(e, 4, 0)), jnp.where(low, pltpu.roll(s, 4, 0), e)]
-        send_ref[slab_rows(tile), :] = jnp.concatenate(sums, axis=0).astype(BF16)
+        rows = slab_rows(tile, grad_ref.shape[1] // LANES)
+        send_ref[rows, :] = jnp.concatenate(sums[::-1], axis=0).astype(BF16)
 
     each_tile(grad_ref.shape[1], body)
 
@@ -219,9 +224,9 @@
             moved = swap_quarters(lags[1, SUB * pair : SUB * pair + SUB, lanes])
             for k in range(2):
                 for q in range(4):
-                    row = SUB * q + 4 + 2 * pair + k
+                    row = SUB * (QUADS - 1 - q) + 4 + 2 * pair + k
                     slab[row : row + 1, :] = moved[4 * k + q : 4 * k + q + 1, :]
-        send_ref[slab_rows(tile), :] = slab[...].astype(BF16)
+        send_ref[slab_rows(tile, mixed_ref.shape[1] // LANES), :] = slab[...].astype(BF16)
 
     each_tile(mixed_ref.shape[1], ship, 8)
 
@@ -238,14 +243,14 @@
 
     def step(back, held):
         state, far, far_even = held
-        start = pl.multiple_of((blocks // 2 - 1 - back) * 16, 16)
+        start = pl.multiple_of(back * 16, 16)
         pair = received_ref[pl.ds(start, 16), :].astype(F32)
         coef = coef_ref[pl.ds(start, 16), :].astype(F32)
-        even, odd = pair[:SUB, :], pair[SUB:, :]
+        odd, even = pair[:SUB, :], pair[SUB:, :]
         odd_own = jnp.where(low, odd, pltpu.roll(odd, 4, 0))
         even_own = jnp.where(low, even, pltpu.roll(even, 4, 0))
         before = odd_own + decay * state
-        out = [jnp.where(low, before, coef[:SUB, :]), jnp.where(low, state, coef[SUB:, :])]
+        out = [jnp.where(low, state, coef[:SUB, :]), jnp.where(low, before, coef[SUB:, :])]
         send_ref[pl.ds(start, 16), :] = jnp.concatenate(out, axis=0).astype(BF16)
         return (even_own + decay * odd_own) + squared * state, far + odd * state, far_even + even * before
 
@@ -253,8 +258,8 @@
     _, far, far_even = lax.fori_loop(0, blocks // 2, step, (zero, zero, zero), unroll=8)
     far = swap_quarters((far + far_even) * gains)
     me = lax.axis_index("ctx")
-    mine = slab_rows(me // QUADS)
-    extra = [jnp.where(place == 4 + me % QUADS, wide(far[4 + q : 5 + q, :]), 0.0) for q in range(QUADS)]
+    mine = slab_rows(me // QUADS, blocks // QUADS)
+    extra = [jnp.where(place == 4 + me % QUADS, wide(far[4 + q : 5 + q, :]), 0.0) for q in range(QUADS - 1, -1, -1)]
     send_ref[mine, :] = (send_ref[mine, :].astype(F32) + jnp.concatenate(extra, axis=0)).astype(BF16)
 
 
@@ -333,11 +338,11 @@
     def body(tile, slot):
         lanes = lane_slice(tile)
         slab, mix_sub = slabs.at[slot], mixes.at[slot]
-        slab[...] = received_ref[slab_rows(tile), :].astype(F32)
+        slab[...] = received_ref[slab_rows(tile, near_ref.shape[1] // LANES), :].astype(F32)
         one = [wide(power_ref[m : m + 1, lanes]) for m in range(MODES)]
         state = []
         for m in range(MODES):
-            row = SUB * (m // 4) + m % 4
+            row = SUB * (QUADS - 1 - m // 4) + m % 4
             rows = slice(SUB * m, SUB * m + SUB)
             state.append(lead_ref[rows, lanes] + wide(slab[row : row + 1, :]) * reach_ref[rows, lanes])
         for j in range(ROWS - 1, -1, -1):
@@ -351,7 +356,7 @@
             grad_key_ref[rows, lanes] = (mix * value_ref[rows, lanes].astype(F32)).astype(BF16)
             grad_value_ref[rows, lanes] = (mix * key_ref[rows, lanes].astype(F32)).astype(BF16)
 
-    each_tile(near_ref.shape[1], body)
+    each_tile(near_ref.shape[1], body, 8)
 
 
 def gate_kernel(grad_ref, conv_ref, out_ref):
@@ -373,7 +378,7 @@
     def block(ref, at):
         if ref.shape[1] == LANES:
             size = width // LANES * 32
-            return ref.at[pl.ds(pl.multiple_of(at * size, size), size), :]
+            return ref.at[pl.ds(pl.multiple_of((steps - 1 - at) * size, size), size), :]
         return ref.at[:, pl.ds(pl.multiple_of(at * width, width), width)]
 
     def kernel(*refs):
@@ -455,7 +460,7 @@
 
     token_block = pl.BlockSpec((tokens, WIDTH), lambda n: (0, n))
     mode_block = pl.BlockSpec((MODES, WIDTH), lambda n: (0, n))
-    slab_block = pl.BlockSpec((WIDTH // LANES * 32, LANES), lambda n: (n, 0))
+    slab_block = pl.BlockSpec((WIDTH // LANES * 32, LANES), lambda n: (channels // WIDTH - 1 - n, 0))
     token_half = jax.ShapeDtypeStruct((tokens, channels), BF16)
     token_full = jax.ShapeDtypeStruct((tokens, channels), F32)
     slabs = jax.ShapeDtypeStruct((blocks * SUB, LANES), BF16)
@@ -466,12 +471,14 @@
         [token_block] * 4 + [mode_block],
         [token_block] * 4 + [slab_block],
         [token_half, token_half, token_full, token_full, slabs],
-        [table(4, MODES, WIDTH), table(2, 2, TOKENS, LANES)],
+        [table(4, MODES, WIDTH), table(2, 2, SUB * PITCH, LANES)],
         10**9, 10 * 2**20,
     )(grad, query, key, value, rates)
 
     def exchange(rows):
-        moved = lax.all_to_all(rows.reshape(blocks, SUB, LANES), "ctx", split_axis=0, concat_axis=0, tiled=True)
+        pieces = rows.reshape(blocks, SUB, LANES)
+        backwards = [list(range(blocks - 1, -1, -1))]
+        moved = lax.all_to_all(pieces, "ctx", split_axis=0, concat_axis=0, axis_index_groups=backwards, tiled=True)
         return moved.reshape(blocks * SUB, LANES)
 
     received = exchange(summary)
@@ -528,7 +535,7 @@
         [(x, False) for x in (near, lead, reach, power, key, value)] + [(returned, True)],
         [(token_half, False), (token_half, False)],
         WIDTH,
-        [table(2, 32, LANES), table(2, TOKENS, LANES)],
+        [table(8, 32, LANES), table(8, TOKENS, LANES)],
         10**9, 9 * 2**20, heads,
     )
 

time: 69.6 us -> 65.3 us (0.938)
  waiting for transfers between devices: 10.6 us -> 0.56 us
  starting transfers between devices: 24.1 us -> 30.5 us
    all_to_all x2, waiting for transfers between devices: 10.6 us -> 0.55 us  [exchange(): lax.all_to_all(pieces, 'ctx', split_axis=0, concat_axis=0, axis_index_gro...]
    all_to_all x2, starting transfers between devices: 21.4 us -> 27.7 us  [exchange(): lax.all_to_all(pieces, 'ctx', split_axis=0, concat_axis=0, axis_index_gro...]
  transfers between devices with their start and end apart: 3 -> 3, of which waited for: 2 -> 1; matrix products, arithmetic and copies ran while one was open for 1% -> 1% of each run, Pallas kernels for 31% -> 32%
where the time goes in v5:
time: 65.3 us; the launch traced here: 65 us
  Pallas kernels  31.9 us (49%)
  starting transfers between devices  30.5 us (47%)
  local copies, waits for them, and re-layouts  0.77 us (1%)
  between operations  0.73 us (1%)
    all_to_all x2, starting transfers between devices, exchange(): lax.all_to_all(pieces, 'ctx', split_axis=0, concat_axis=0, axis_index_gro...  27.7 us
    pallas_call x3, Pallas kernels, streamed(): call(kernel, (), specs[:n_in] + [pl.BlockSpec(memory_space=pltpu.VMEM)] *...  14.7 us
    pallas_call x1, Pallas kernels, local(): call(summary_kernel, steps, [token_block] * 4 + [mode_block], [token_bloc...  9.68 us
    pallas_call x1, Pallas kernels, local(): call(stage_kernel, (), [far_spec] * 6, [far_spec] * 3 + [near_spec] * 6,...  6.18 us
    ppermute x1, starting transfers between devices, local(): other = lax.ppermute(coef_part, 'dp', [(0, 1), (1, 0)])  2.83 us
  transfers between devices with their start and end apart: 3, of which 1 were waited for; matrix products, arithmetic and copies ran while one was open for 1% of the time, Pallas kernels for 32%

profile of v5, /device:TPU:1, one launch (start us, length us, event | category | flops | bytes accessed | tf_op | source)
XLA Modules:
  0.0 65.0 jit_solution(9495191280314030280)
XLA Ops:
  0.6 9.7 %shard_map.102 = (bf16[128,4096]{1,0:T(8,128)(2,1)}, bf16[128,4096]{1,0:T(8,128)(2,1)}, f32[128,4096]{1,0:T(8,128)}, f32[128,4096]{1,0:T(8,128)}, bf16[1024,128]{1,0:T(8,128)(2,1)}) custom-call(bf16[128,4096]{1,0:T(8,128)(2,1)} %bitcast.25, bf16[128,4096]{1,0:T(8,128)(2,1)} %bitcast.31, bf16[128,4096]{1,0:T(8,128)(2,1)} %bitcast.19, ...), custom_call_target="tpu_custom_call" | custom-call | flops 1000000000 | bytes 10485760 | tf_op jit(solution)/shard_map/pallas_call | solution.py:469
  10.3 16.0 %all-to-all-start = ((bf16[128,8,128]{2,1,0:T(8,128)(2,1)}), bf16[128,8,128]{2,1,0:T(8,128)(2,1)S(1)}, u32[]{:S(2)}, u32[]{:S(2)}) async-start(bf16[128,8,128]{2,1,0:T(8,128)(2,1)} %bitcast.36), calls=%async_computation | async-start | bytes 524288 | tf_op jit(solution)/shard_map/all_to_all | solution.py:481
  26.3 0.8 %dynamic_slice.3 = f32[4,128]{1,0:T(4,128)S(1)} dynamic-slice(f32[16,4096]{1,0:T(8,128)} %bitcast.28, s32[]{:T(128)S(6)} %select_n.18, s32[]{:T(128)S(6)} %select_n.20), dynamic_slice_sizes={4,128} | dynamic-slice | bytes 4100 | tf_op jit(solution)/shard_map/dynamic_slice | solution.py:500
  27.1 6.8 %shard_map.103 = (f32[128,4096]{1,0:T(8,128)}, bf16[1024,128]{1,0:T(8,128)(2,1)S(1)}) custom-call(bf16[128,4096]{1,0:T(8,128)(2,1)} %get-tuple-element.35.refs_0_.mixed_far, bf16[128,4096]{1,0:T(8,128)(2,1)} %get-tuple-element.29.refs_1_, f32[128,4096]{1,0:T(8,128)} %get-tuple-element.30.refs_2_, f32[128,4096]{1,0:T(8,128)} %get-tuple-element.31.refs_3_, ...), custom_call_target="tpu_custom_call" | custom-call | flops 1000000000 | bytes 10485760 | tf_op jit(solution)/shard_map/pallas_call | solution.py:428
  34.0 0.6 all-to-all-done
  34.5 1.1 %shard_map.104 = bf16[1024,128]{1,0:T(8,128)(2,1)} custom-call(bf16[1024,128]{1,0:T(8,128)(2,1)S(1)} %bitcast.18, bf16[1024,128]{1,0:T(8,128)(2,1)S(1)} %get-tuple-element.32.coef_ref, f32[8,128]{1,0:T(8,128)S(1)} %pad_maximum_fusion.rate_ref), custom_call_target="tpu_custom_call" | custom-call | flops 1000000 | bytes 1048576 | tf_op jit(solution)/shard_map/pallas_call | solution.py:504
  35.6 11.7 %all-to-all-start.1 = ((bf16[128,8,128]{2,1,0:T(8,128)(2,1)}), bf16[128,8,128]{2,1,0:T(8,128)(2,1)S(1)}, u32[]{:S(2)}, u32[]{:S(2)}) async-start(bf16[128,8,128]{2,1,0:T(8,128)(2,1)} %bitcast.10), calls=%async_computation.1 | async-start | bytes 524288 | tf_op jit(solution)/shard_map/all_to_all | solution.py:481
  47.3 2.6 %shard_map.105 = bf16[128,4096]{1,0:T(8,128)(2,1)} custom-call(bf16[128,4096]{1,0:T(8,128)(2,1)} %bitcast.26, bf16[128,4096]{1,0:T(8,128)(2,1)} %bitcast.32), custom_call_target="tpu_custom_call" | custom-call | flops 1000000 | bytes 3145728 | tf_op jit(solution)/shard_map/pallas_call | solution.py:428
  49.9 6.2 %shard_map.106 = (f32[128,4096]{1,0:T(8,128)}, f32[128,4096]{1,0:T(8,128)}, f32[16,4096]{1,0:T(8,128)}, f32[128,1024]{1,0:T(8,128)S(1)}, f32[128,1024]{1,0:T(8,1...) custom-call(bf16[128,4096]{1,0:T(8,128)(2,1)} %get-tuple-element.35., ...), custom_call_target="tpu_custom_call" | custom-call | flops 1000000000 | bytes 4194304 | tf_op jit(solution)/shard_map/pallas_call | solution.py:513
  56.0 0.0 all-to-all-done.1
  56.1 0.2 shard_map.108
  56.2 2.8 %collective-permute-start = (f32[16,32]{1,0:T(8,128)S(1)}, f32[16,32]{1,0:T(8,128)S(1)}, u32[]{:S(2)}, u32[]{:S(2)}) collective-permute-start(f32[16,32]{1,0:T(8,128)S(1)} %shard_map.108), channel_id=1, source_target_pairs={{0,1},{1,0},{2,3},{3,2},{4,5},{5,4},{6,7},{7,6},{8,9},{9,8},{10,11... | collective-permute-start | bytes 6152 | tf_op jit(solution)/shard_map/ppermute | solution.py:531
  59.1 5.3 %shard_map.107 = (bf16[128,4096]{1,0:T(8,128)(2,1)}, bf16[128,4096]{1,0:T(8,128)(2,1)}) custom-call(f32[128,4096]{1,0:T(8,128)} %get-tuple-element.39.refs_0_, f32[128,4096]{1,0:T(8,128)} %get-tuple-element.36.lead_far.refs_1_, f32[128,4096]{1,0:T(8,128)} %get-tuple-element.40.refs_2_, f32[16,4096]{1,0:T(8,128)} %get-tuple-element.41.refs_3_, ...), custom_call_target="tpu_custom_call" | custom-call | flops 1000000000 | bytes 9437184 | tf_op jit(solution)/shard_map/pallas_call | solution.py:428
  64.4 0.0 collective-permute-done
  64.4 0.6 add_bitcast_fusion
  (1 shorter events, 0.0 us)
Async XLA Ops:
  10.3 24.2 %all-to-all-start = ((bf16[128,8,128]{2,1,0:T(8,128)(2,1)}), bf16[128,8,128]{2,1,0:T(8,128)(2,1)S(1)}, u32[]{:S(2)}, u32[]{:S(2)}) async-start(bf16[128,8,128]{2,1,0:T(8,128)(2,1)} %bitcast.36), calls=%async_computation | async-start | bytes 524288 | tf_op jit(solution)/shard_map/all_to_all | solution.py:481
  35.6 20.4 %all-to-all-start.1 = ((bf16[128,8,128]{2,1,0:T(8,128)(2,1)}), bf16[128,8,128]{2,1,0:T(8,128)(2,1)S(1)}, u32[]{:S(2)}, u32[]{:S(2)}) async-start(bf16[128,8,128]{2,1,0:T(8,128)(2,1)} %bitcast.10), calls=%async_computation.1 | async-start | bytes 524288 | tf_op jit(solution)/shard_map/all_to_all | solution.py:481
  56.2 8.2 %collective-permute-start = (f32[16,32]{1,0:T(8,128)S(1)}, f32[16,32]{1,0:T(8,128)S(1)}, u32[]{:S(2)}, u32[]{:S(2)}) collective-permute-start(f32[16,32]{1,0:T(8,128)S(1)} %shard_map.108), channel_id=1, source_target_pairs={{0,1},{1,0},{2,3},{3,2},{4,5},{5,4},{6,7},{7,6},{8,9},{9,8},{10,11... | collective-permute-start | bytes 6152 | tf_op jit(solution)/shard_map/ppermute | solution.py:531

commit v6 on v5

--- a/solution.py
+++ b/solution.py
@@ -108,13 +108,24 @@
 
 def summary_kernel(
     grad_ref, query_ref, key_ref, value_ref, rate_ref,
-    mixed_ref, product_ref, state_ref, entry_ref, send_ref,
+    mixed_ref, product_ref, state_ref, entry_ref, send_ref, own_ref,
     powers, full,
 ):
     rates = rate_ref[...]
     for index, power in enumerate((1.0, 16.0, 32.0, 64.0)):
         powers[index] = jnp.exp(-power * rates)
     place = lax.broadcasted_iota(jnp.int32, (SUB, LANES), 0)
+    low = place < 4
+    tiles = grad_ref.shape[1] // LANES
+    me = lax.axis_index("ctx")
+    tile_own, quad = me // QUADS, me % QUADS
+
+    @pl.when(pl.program_id(0) == tile_own // tiles)
+    def _():
+        lanes = lane_slice(tile_own % tiles)
+        eight = jnp.where(quad >= 2, rate_ref[SUB:, lanes], rate_ref[:SUB, lanes])
+        turned = pltpu.roll(eight, 4, 0)
+        own_ref[...] = jnp.where(low == (quad % 2 == 0), eight, turned)
 
     def body(tile, slot):
         lanes = lane_slice(tile)
@@ -159,7 +170,6 @@
                 return out
 
             s, e = weighted_sums(states, entries, rows_of, place)
-            low = place < 4
             sums += [jnp.where(low, s, pltpu.roll(e, 4, 0)), jnp.where(low, pltpu.roll(s, 4, 0), e)]
         rows = slab_rows(tile, grad_ref.shape[1] // LANES)
         send_ref[rows, :] = jnp.concatenate(sums[::-1], axis=0).astype(BF16)
@@ -278,15 +288,16 @@
 
 
 def stage_kernel(
-    mixed_far, rate_far, residue_far, lead_far, key_far, value_far,
-    near_far, reach_far, power_far, near_head, lead_head, reach_head, power_head, key_head, value_head,
-    mixed_ref, rate_ref, residue_ref, near_ref, reach_ref, power_ref, weights, taps, sems,
+    mixed_far, rate_far, residue_far, lead_far, key_far, value_far, grad_far, conv_far,
+    near_far, reach_far, power_far, gate_far, near_head, lead_head, reach_head, power_head, key_head, value_head,
+    mixed_ref, rate_ref, residue_ref, near_ref, reach_ref, power_ref, grad_ref, conv_ref, gate_ref, weights, taps, sems,
 ):
     width = near_head.shape[1]
+    steps = mixed_ref.shape[1] // width
     heads = ((lead_far, lead_head), (key_far, key_head), (value_far, value_head))
-    pairs = [(rate_far, rate_ref), (residue_far, residue_ref), (mixed_far, mixed_ref)]
+    pairs = [(rate_far, rate_ref), (residue_far, residue_ref), (mixed_far, mixed_ref), (grad_far, grad_ref), (conv_far, conv_ref)]
     pairs += [(far.at[:, pl.ds(0, width)], head) for far, head in heads]
-    coming = [pltpu.make_async_copy(*pair, sems.at[i]) for i, pair in enumerate(pairs)]
+    coming = [pltpu.make_async_copy(*pair, sems.at[i, 0]) for i, pair in enumerate(pairs)]
     for each in coming:
         each.start()
     for each in coming[:2]:
@@ -299,10 +310,17 @@
         if d == 0:
             weights[...] = term
     back = (16 * (SUB - 1 - lax.broadcasted_iota(jnp.int32, (SUB, LANES), 0))).astype(F32)
-    coming[2].wait()
+    for each in coming[2:5]:
+        each.wait()
+
+    def out_copy(i, at):
+        source, target = ((near_ref, near_far), (reach_ref, reach_far), (power_ref, power_far), (gate_ref, gate_far))[i]
+        lanes = pl.ds(pl.multiple_of(at * width, width), width)
+        return pltpu.make_async_copy(source.at[:, lanes], target.at[:, lanes], sems.at[len(pairs) + i, at])
 
     def body(tile, slot):
         lanes = lane_slice(tile)
+        gate_ref[:, lanes] = (grad_ref[:, lanes].astype(F32) * conv_ref[:, lanes].astype(F32)).astype(BF16)
         g = []
         for j in range(0, ROWS, 2):
             pair = mixed_ref[SUB * j : SUB * j + 16, lanes].astype(F32)
@@ -318,16 +336,21 @@
             reach = jnp.exp(-back * wide(rate_ref[m : m + 1, lanes]))
             reach_ref[SUB * m : SUB * m + SUB, lanes] = reach * wide(weights[m : m + 1, lanes])
 
-    each_tile(rate_ref.shape[1], body)
-    tables = ((near_ref, near_far), (reach_ref, reach_far), (power_ref, power_far))
-    going = [pltpu.make_async_copy(*pair, sems.at[len(pairs) + i]) for i, pair in enumerate(tables)]
-    for each in going:
-        each.start()
+    def step(at, _):
+        each_tile(width, lambda tile, slot: body(tile + at * (width // LANES), slot))
+        for i in range(4):
+            out_copy(i, at).start()
+        return 0
+
+    lax.fori_loop(0, steps, step, 0)
     near_head[...] = near_ref[:, :width]
     reach_head[...] = reach_ref[:, :width]
     power_head[...] = power_ref[:, :width]
-    for each in coming[3:] + going:
+    for each in coming[5:]:
         each.wait()
+    for at in range(steps):
+        for i in range(4):
+            out_copy(i, at).wait()
 
 
 def output_kernel(
@@ -359,14 +382,6 @@
     each_tile(near_ref.shape[1], body, 8)
 
 
-def gate_kernel(grad_ref, conv_ref, out_ref):
-    def body(tile, slot):
-        lanes = lane_slice(tile)
-        out_ref[:, lanes] = (grad_ref[:, lanes].astype(F32) * conv_ref[:, lanes].astype(F32)).astype(BF16)
-
-    each_tile(grad_ref.shape[1], body)
-
-
 def streamed(body, ins, outs, width, scratch, flops, moved, heads=(), ahead=3):
     arrays = [x for x, _ in ins + outs]
     n_in, n_all = len(ins), len(ins) + len(outs)
@@ -466,11 +481,11 @@
     slabs = jax.ShapeDtypeStruct((blocks * SUB, LANES), BF16)
     steps = (channels // WIDTH,)
 
-    mixed, product, states, entries, summary = call(
+    mixed, product, states, entries, summary, rate_own = call(
         summary_kernel, steps,
         [token_block] * 4 + [mode_block],
-        [token_block] * 4 + [slab_block],
-        [token_half, token_half, token_full, token_full, slabs],
+        [token_block] * 4 + [slab_block, pl.BlockSpec((SUB, LANES), lambda n: (0, 0))],
+        [token_half, token_half, token_full, token_full, slabs, jax.ShapeDtypeStruct((SUB, LANES), F32)],
         [table(4, MODES, WIDTH), table(2, 2, SUB * PITCH, LANES)],
         10**9, 10 * 2**20,
     )(grad, query, key, value, rates)
@@ -495,11 +510,6 @@
         10**9, 10 * 2**20,
     )
 
-    me = lax.axis_index("ctx")
-    rates_late, _ = lax.optimization_barrier((rates, summary))
-    rate_own = lax.dynamic_slice(rates_late, (4 * (me % QUADS), LANES * (me // QUADS)), (4, LANES))
-    rate_own = jnp.concatenate([rate_own, rate_own], axis=0)
-
     vmem = pl.BlockSpec(memory_space=pltpu.VMEM)
     carries = call(
         functools.partial(scan_kernel, scale), (), [vmem] * 3, vmem, slabs, limit=SMALL_LIMIT
@@ -507,23 +517,24 @@
 
     returned = exchange(carries)
 
-    gate_in, key_late, value_late, mixed_late, _ = lax.optimization_barrier((conv, key, value, mixed, carries))
+    conv_late, key_late, value_late, mixed_late, grad_late, _ = lax.optimization_barrier(
+        (conv, key, value, mixed, grad, carries)
+    )
     far_spec, near_spec = pl.BlockSpec(memory_space=pltpu.HBM), pl.BlockSpec(memory_space=pltpu.VMEM)
     head_types = [pltpu.VMEM((x.shape[0], WIDTH), x.dtype) for x in (lead, lead, lead, rates, key, value)]
-    near, reach, power, *heads = call(
-        stage_kernel, (), [far_spec] * 6, [far_spec] * 3 + [near_spec] * 6,
-        [pltpu.HBM(x.shape, F32) for x in (lead, lead, rates)] + head_types,
+    near, reach, power, grad_query, *heads = call(
+        stage_kernel, (), [far_spec] * 8, [far_spec] * 4 + [near_spec] * 6,
+        [pltpu.HBM(x.shape, x.dtype) for x in (lead, lead, rates, key)] + head_types,
         [pltpu.VMEM(mixed.shape, BF16)]
-        + [pltpu.VMEM(x.shape, F32) for x in (rates, rates, lead, lead, rates, rates, rates)]
-        + [pltpu.SemaphoreType.DMA((9,))],
-        10**9, 4 * 2**20, STREAM_LIMIT,
+        + [pltpu.VMEM(x.shape, F32) for x in (rates, rates, lead, lead, rates)]
+        + [pltpu.VMEM(mixed.shape, BF16)] * 3
+        + [pltpu.VMEM(x.shape, F32) for x in (rates, rates)]
+        + [pltpu.SemaphoreType.DMA((12, steps[0]))],
+        10**9, 8 * 2**20, STREAM_LIMIT,
     )(*(
         pltpu.with_memory_space_constraint(x, pltpu.HBM)
-        for x in (mixed_late, rates, residue, lead, key_late, value_late)
+        for x in (mixed_late, rates, residue, lead, key_late, value_late, grad_late, conv_late)
     ))
-    grad_query = streamed(
-        gate_kernel, [(grad, False), (gate_in, False)], [(token_half, False)], WIDTH, [], 10**6, 3 * 2**20
-    )[0]
 
     coef_part = call(
         total_kernel, (), [vmem], vmem, jax.ShapeDtypeStruct((MODES, own), F32), limit=SMALL_LIMIT

time: 65.3 us -> 64.2 us (0.983)
  waiting for transfers between devices: 0.56 us -> 3.54 us
  Pallas kernels: 31.9 us -> 29.1 us
  local copies, waits for them, and re-layouts: 0.77 us -> 0.01 us
    all_to_all x2, waiting for transfers between devices: 0.55 us -> 3.54 us  [exchange(): lax.all_to_all(pieces, 'ctx', split_axis=0, concat_axis=0, axis_index_gro...]
    pallas_call x3 -> x2, Pallas kernels: 14.7 us -> 12.1 us  [streamed(): call(kernel, (), specs[:n_in] + [pl.BlockSpec(memory_space=pltpu.VMEM)] *...]
    dynamic_slice x1 -> x0, local copies, waits for them, and re-layouts: 0.77 us -> none  [local(): lax.dynamic_slice(rates_late, (4 * (me % QUADS), LANES * (me // QUADS)),...]
  transfers between devices with their start and end apart: 3 -> 3, of which waited for: 1 -> 2; matrix products, arithmetic and copies ran while one was open for 1% -> 0% of each run, Pallas kernels for 32% -> 28%
where the time goes in v6:
time: 64.2 us; the launch traced here: 63.9 us
  starting transfers between devices  30 us (47%)
  Pallas kernels  29.1 us (45%)
  waiting for transfers between devices  3.54 us (6%)
  between operations  0.69 us (1%)
    all_to_all x2, starting transfers between devices, exchange(): lax.all_to_all(pieces, 'ctx', split_axis=0, concat_axis=0, axis_index_gro...  27.2 us
    pallas_call x2, Pallas kernels, streamed(): call(kernel, (), specs[:n_in] + [pl.BlockSpec(memory_space=pltpu.VMEM)] *...  12.1 us
    pallas_call x1, Pallas kernels, local(): call(summary_kernel, steps, [token_block] * 4 + [mode_block], [token_bloc...  9.66 us
    pallas_call x1, Pallas kernels, local(): call(stage_kernel, (), [far_spec] * 8, [far_spec] * 4 + [near_spec] * 6,...  6.09 us
    all_to_all x2, waiting for transfers between devices, exchange(): lax.all_to_all(pieces, 'ctx', split_axis=0, concat_axis=0, axis_index_gro...  3.54 us
    ppermute x1, starting transfers between devices, local(): other = lax.ppermute(coef_part, 'dp', [(0, 1), (1, 0)])  2.83 us
  transfers between devices with their start and end apart: 3, of which 2 were waited for; matrix products, arithmetic and copies ran while one was open for 0% of the time, Pallas kernels for 28%

profile of v6, /device:TPU:1, one launch (start us, length us, event | category | flops | bytes accessed | tf_op | source)
XLA Modules:
  0.0 63.9 jit_solution(3944137268647351326)
XLA Ops:
  0.6 9.7 %shard_map.102 = (bf16[128,4096]{1,0:T(8,128)(2,1)}, bf16[128,4096]{1,0:T(8,128)(2,1)}, f32[128,4096]{1,0:T(8,128)}, f32[128,4096]{1,0:T(8,128)}, bf16[1024,128]{1,0:T(8,128)(2,1)}, /*index=5*/f32[8,128]{1,0:T(8,128)}) custom-call(bf16[128,4096]{1,0:T(8,128)(2,1)} %bitcast.25, bf16[128,4096]{1,0:T(8,128)(2,1)} %bitcast.30, bf16[128,4096]{1,0:T(8,128)(2,1)} %bitcast.19, ...), custom_call_target="tpu_custom_call" | custom-call | flops 1000000000 | bytes 10485760 | tf_op jit(solution)/shard_map/pallas_call | solution.py:484
  10.3 16.0 %all-to-all-start = ((bf16[128,8,128]{2,1,0:T(8,128)(2,1)}), bf16[128,8,128]{2,1,0:T(8,128)(2,1)S(1)}, u32[]{:S(2)}, u32[]{:S(2)}) async-start(bf16[128,8,128]{2,1,0:T(8,128)(2,1)} %bitcast.34), calls=%async_computation | async-start | bytes 524288 | tf_op jit(solution)/shard_map/all_to_all | solution.py:496
  26.3 0.0 copy-start
  26.3 6.8 %shard_map.103 = (f32[128,4096]{1,0:T(8,128)}, bf16[1024,128]{1,0:T(8,128)(2,1)S(1)}) custom-call(bf16[128,4096]{1,0:T(8,128)(2,1)} %get-tuple-element.36.refs_0_.mixed_far, bf16[128,4096]{1,0:T(8,128)(2,1)} %get-tuple-element.31.refs_1_, f32[128,4096]{1,0:T(8,128)} %get-tuple-element.32.refs_2_, f32[128,4096]{1,0:T(8,128)} %get-tuple-element.33.refs_3_, ...), custom_call_target="tpu_custom_call" | custom-call | flops 1000000000 | bytes 10485760 | tf_op jit(solution)/shard_map/pallas_call | solution.py:443
  33.1 1.4 %all-to-all-done = bf16[128,8,128]{2,1,0:T(8,128)(2,1)S(1)} async-done(((bf16[128,8,128]{2,1,0:T(8,128)(2,1)}), bf16[128,8,128]{2,1,0:T(8,128)(2,1)S(1)}, u32[]{:S(2)}, u32[]{:S(2)}) %all-to-all-start) | async-done | bytes 262176 | tf_op jit(solution)/shard_map/all_to_all | solution.py:496
  34.5 0.0 copy-done
  34.5 1.1 %shard_map.104 = bf16[1024,128]{1,0:T(8,128)(2,1)} custom-call(bf16[1024,128]{1,0:T(8,128)(2,1)S(1)} %bitcast.18, bf16[1024,128]{1,0:T(8,128)(2,1)S(1)} %get-tuple-element.34.coef_ref, f32[8,128]{1,0:T(8,128)S(1)} %copy-done), custom_call_target="tpu_custom_call" | custom-call | flops 1000000 | bytes 1048576 | tf_op jit(solution)/shard_map/pallas_call | solution.py:514
  35.6 11.2 %all-to-all-start.1 = ((bf16[128,8,128]{2,1,0:T(8,128)(2,1)}), bf16[128,8,128]{2,1,0:T(8,128)(2,1)S(1)}, u32[]{:S(2)}, u32[]{:S(2)}) async-start(bf16[128,8,128]{2,1,0:T(8,128)(2,1)} %bitcast.10), calls=%async_computation.1 | async-start | bytes 524288 | tf_op jit(solution)/shard_map/all_to_all | solution.py:496
  46.8 6.1 %shard_map.105 = (f32[128,4096]{1,0:T(8,128)}, f32[128,4096]{1,0:T(8,128)}, f32[16,4096]{1,0:T(8,128)}, bf16[128,4096]{1,0:T(8,128)(2,1)}, f32[128,1024]{1,0:T(8...) custom-call(bf16[128,4096]{1,0:T(8,128)(2,1)} %get-tuple-element.36., ...), custom_call_target="tpu_custom_call" | custom-call | flops 1000000000 | bytes 8388608 | tf_op jit(solution)/shard_map/pallas_call | solution.py:525
  52.9 2.1 %all-to-all-done.1 = bf16[128,8,128]{2,1,0:T(8,128)(2,1)S(1)} async-done(((bf16[128,8,128]{2,1,0:T(8,128)(2,1)}), bf16[128,8,128]{2,1,0:T(8,128)(2,1)S(1)}, u32[]{:S(2)}, u32[]{:S(2)}) %all-to-all-start.1) | async-done | bytes 262176 | tf_op jit(solution)/shard_map/all_to_all | solution.py:496
  55.0 0.2 shard_map.107
  55.2 2.8 %collective-permute-start = (f32[16,32]{1,0:T(8,128)S(1)}, f32[16,32]{1,0:T(8,128)S(1)}, u32[]{:S(2)}, u32[]{:S(2)}) collective-permute-start(f32[16,32]{1,0:T(8,128)S(1)} %shard_map.107), channel_id=1, source_target_pairs={{0,1},{1,0},{2,3},{3,2},{4,5},{5,4},{6,7},{7,6},{8,9},{9,8},{10,11... | collective-permute-start | bytes 6152 | tf_op jit(solution)/shard_map/ppermute | solution.py:542
  58.0 5.3 %shard_map.106 = (bf16[128,4096]{1,0:T(8,128)(2,1)}, bf16[128,4096]{1,0:T(8,128)(2,1)}) custom-call(f32[128,4096]{1,0:T(8,128)} %get-tuple-element.43.refs_0_, f32[128,4096]{1,0:T(8,128)} %get-tuple-element.37.lead_far.refs_1_, f32[128,4096]{1,0:T(8,128)} %get-tuple-element.44.refs_2_, f32[16,4096]{1,0:T(8,128)} %get-tuple-element.45.refs_3_, ...), custom_call_target="tpu_custom_call" | custom-call | flops 1000000000 | bytes 9437184 | tf_op jit(solution)/shard_map/pallas_call | solution.py:443
  63.3 0.0 collective-permute-done
  63.3 0.6 add_bitcast_fusion
Async XLA Ops:
  10.3 24.2 %all-to-all-start = ((bf16[128,8,128]{2,1,0:T(8,128)(2,1)}), bf16[128,8,128]{2,1,0:T(8,128)(2,1)S(1)}, u32[]{:S(2)}, u32[]{:S(2)}) async-start(bf16[128,8,128]{2,1,0:T(8,128)(2,1)} %bitcast.34), calls=%async_computation | async-start | bytes 524288 | tf_op jit(solution)/shard_map/all_to_all | solution.py:496
  26.3 8.2 %copy-start = (f32[8,128]{1,0:T(8,128)S(1)}, f32[8,128]{1,0:T(8,128)}, u32[]{:S(2)}) copy-start(f32[8,128]{1,0:T(8,128)} %get-tuple-element.35.rate_ref) | copy-start | bytes 12292
  35.6 19.4 %all-to-all-start.1 = ((bf16[128,8,128]{2,1,0:T(8,128)(2,1)}), bf16[128,8,128]{2,1,0:T(8,128)(2,1)S(1)}, u32[]{:S(2)}, u32[]{:S(2)}) async-start(bf16[128,8,128]{2,1,0:T(8,128)(2,1)} %bitcast.10), calls=%async_computation.1 | async-start | bytes 524288 | tf_op jit(solution)/shard_map/all_to_all | solution.py:496
  55.2 8.2 %collective-permute-start = (f32[16,32]{1,0:T(8,128)S(1)}, f32[16,32]{1,0:T(8,128)S(1)}, u32[]{:S(2)}, u32[]{:S(2)}) collective-permute-start(f32[16,32]{1,0:T(8,128)S(1)} %shard_map.107), channel_id=1, source_target_pairs={{0,1},{1,0},{2,3},{3,2},{4,5},{5,4},{6,7},{7,6},{8,9},{9,8},{10,11... | collective-permute-start | bytes 6152 | tf_op jit(solution)/shard_map/ppermute | solution.py:542

commit v7 on v6

--- a/solution.py
+++ b/solution.py
@@ -17,6 +17,7 @@
 MODES = 16
 QUADS = 4
 PITCH = 24
+FIRST = 107
 WIDTH = 1024
 VMEM_LIMIT = 60 * 1024 * 1024
 SMALL_LIMIT = 4 * 1024 * 1024
@@ -28,7 +29,7 @@
 
 
 def slab_rows(tile, tiles):
-    return pl.ds(pl.multiple_of((tiles - 1 - tile) * 32, 32), 32)
+    return pl.ds(pl.multiple_of((tile ^ ((FIRST >> 2) & (tiles - 1))) * 32, 32), 32)
 
 
 def gain_of(rates):
@@ -253,7 +254,7 @@
 
     def step(back, held):
         state, far, far_even = held
-        start = pl.multiple_of(back * 16, 16)
+        start = pl.multiple_of(((blocks // 2 - 1 - back) ^ (FIRST >> 1)) * 16, 16)
         pair = received_ref[pl.ds(start, 16), :].astype(F32)
         coef = coef_ref[pl.ds(start, 16), :].astype(F32)
         odd, even = pair[:SUB, :], pair[SUB:, :]
@@ -393,7 +394,7 @@
     def block(ref, at):
         if ref.shape[1] == LANES:
             size = width // LANES * 32
-            return ref.at[pl.ds(pl.multiple_of((steps - 1 - at) * size, size), size), :]
+            return ref.at[pl.ds(pl.multiple_of((at ^ (FIRST * SUB // size)) * size, size), size), :]
         return ref.at[:, pl.ds(pl.multiple_of(at * width, width), width)]
 
     def kernel(*refs):
@@ -475,7 +476,7 @@
 
     token_block = pl.BlockSpec((tokens, WIDTH), lambda n: (0, n))
     mode_block = pl.BlockSpec((MODES, WIDTH), lambda n: (0, n))
-    slab_block = pl.BlockSpec((WIDTH // LANES * 32, LANES), lambda n: (channels // WIDTH - 1 - n, 0))
+    slab_block = pl.BlockSpec((WIDTH // LANES * 32, LANES), lambda n: (n ^ (FIRST * SUB // (WIDTH // LANES * 32)), 0))
     token_half = jax.ShapeDtypeStruct((tokens, channels), BF16)
     token_full = jax.ShapeDtypeStruct((tokens, channels), F32)
     slabs = jax.ShapeDtypeStruct((blocks * SUB, LANES), BF16)
@@ -492,8 +493,8 @@
 
     def exchange(rows):
         pieces = rows.reshape(blocks, SUB, LANES)
-        backwards = [list(range(blocks - 1, -1, -1))]
-        moved = lax.all_to_all(pieces, "ctx", split_axis=0, concat_axis=0, axis_index_groups=backwards, tiled=True)
+        order = [[j ^ FIRST for j in range(blocks)]]
+        moved = lax.all_to_all(pieces, "ctx", split_axis=0, concat_axis=0, axis_index_groups=order, tiled=True)
         return moved.reshape(blocks * SUB, LANES)
 
     received = exchange(summary)

time: 64.2 us -> 63.2 us (0.984)
  waiting for transfers between devices: 3.54 us -> 0.77 us
  starting transfers between devices: 30 us -> 31.8 us
    all_to_all x2, waiting for transfers between devices: 3.54 us -> 0.77 us  [exchange(): lax.all_to_all(pieces, 'ctx', split_axis=0, concat_axis=0, axis_index_gro...]
    all_to_all x2, starting transfers between devices: 27.2 us -> 29.1 us  [exchange(): lax.all_to_all(pieces, 'ctx', split_axis=0, concat_axis=0, axis_index_gro...]
  transfers between devices with their start and end apart: 3 -> 3, of which waited for: 2 -> 1; matrix products, arithmetic and copies ran while one was open for 0% -> 0% of each run, Pallas kernels for 28% -> 29%
where the time goes in v7:
time: 63.2 us; the launch traced here: 63 us
  starting transfers between devices  31.8 us (50%)
  Pallas kernels  29.1 us (46%)
  waiting for transfers between devices  0.77 us (1%)
  between operations  0.69 us (1%)
    all_to_all x2, starting transfers between devices, exchange(): lax.all_to_all(pieces, 'ctx', split_axis=0, concat_axis=0, axis_index_gro...  29.1 us
    pallas_call x2, Pallas kernels, streamed(): call(kernel, (), specs[:n_in] + [pl.BlockSpec(memory_space=pltpu.VMEM)] *...  12.1 us
    pallas_call x1, Pallas kernels, local(): call(summary_kernel, steps, [token_block] * 4 + [mode_block], [token_bloc...  9.66 us
    pallas_call x1, Pallas kernels, local(): call(stage_kernel, (), [far_spec] * 8, [far_spec] * 4 + [near_spec] * 6,...  6.09 us
    ppermute x1, starting transfers between devices, local(): other = lax.ppermute(coef_part, 'dp', [(0, 1), (1, 0)])  2.65 us
  transfers between devices with their start and end apart: 3, of which 1 were waited for; matrix products, arithmetic and copies ran while one was open for 0% of the time, Pallas kernels for 29%

profile of v7, /device:TPU:1, one launch (start us, length us, event | category | flops | bytes accessed | tf_op | source)
XLA Modules:
  0.0 63.0 jit_solution(2137153511715332822)
XLA Ops:
  0.6 9.7 %shard_map.102 = (bf16[128,4096]{1,0:T(8,128)(2,1)}, bf16[128,4096]{1,0:T(8,128)(2,1)}, f32[128,4096]{1,0:T(8,128)}, f32[128,4096]{1,0:T(8,128)}, bf16[1024,128]{1,0:T(8,128)(2,1)}, /*index=5*/f32[8,128]{1,0:T(8,128)}) custom-call(bf16[128,4096]{1,0:T(8,128)(2,1)} %bitcast.25, bf16[128,4096]{1,0:T(8,128)(2,1)} %bitcast.30, bf16[128,4096]{1,0:T(8,128)(2,1)} %bitcast.19, ...), custom_call_target="tpu_custom_call" | custom-call | flops 1000000000 | bytes 10485760 | tf_op jit(solution)/shard_map/pallas_call | solution.py:485
  10.3 16.7 %all-to-all-start = ((bf16[128,8,128]{2,1,0:T(8,128)(2,1)}), bf16[128,8,128]{2,1,0:T(8,128)(2,1)S(1)}, u32[]{:S(2)}, u32[]{:S(2)}) async-start(bf16[128,8,128]{2,1,0:T(8,128)(2,1)} %bitcast.34), calls=%async_computation | async-start | bytes 524288 | tf_op jit(solution)/shard_map/all_to_all | solution.py:497
  27.0 0.0 copy-start
  27.0 6.8 %shard_map.103 = (f32[128,4096]{1,0:T(8,128)}, bf16[1024,128]{1,0:T(8,128)(2,1)S(1)}) custom-call(bf16[128,4096]{1,0:T(8,128)(2,1)} %get-tuple-element.36.refs_0_.mixed_far, bf16[128,4096]{1,0:T(8,128)(2,1)} %get-tuple-element.31.refs_1_, f32[128,4096]{1,0:T(8,128)} %get-tuple-element.32.refs_2_, f32[128,4096]{1,0:T(8,128)} %get-tuple-element.33.refs_3_, ...), custom_call_target="tpu_custom_call" | custom-call | flops 1000000000 | bytes 10485760 | tf_op jit(solution)/shard_map/pallas_call | solution.py:444
  33.8 0.0 all-to-all-done
  33.8 0.0 copy-done
  33.8 1.1 %shard_map.104 = bf16[1024,128]{1,0:T(8,128)(2,1)} custom-call(bf16[1024,128]{1,0:T(8,128)(2,1)S(1)} %bitcast.18, bf16[1024,128]{1,0:T(8,128)(2,1)S(1)} %get-tuple-element.34.coef_ref, f32[8,128]{1,0:T(8,128)S(1)} %copy-done), custom_call_target="tpu_custom_call" | custom-call | flops 1000000 | bytes 1048576 | tf_op jit(solution)/shard_map/pallas_call | solution.py:515
  34.9 12.4 %all-to-all-start.1 = ((bf16[128,8,128]{2,1,0:T(8,128)(2,1)}), bf16[128,8,128]{2,1,0:T(8,128)(2,1)S(1)}, u32[]{:S(2)}, u32[]{:S(2)}) async-start(bf16[128,8,128]{2,1,0:T(8,128)(2,1)} %bitcast.10), calls=%async_computation.1 | async-start | bytes 524288 | tf_op jit(solution)/shard_map/all_to_all | solution.py:497
  47.4 6.1 %shard_map.105 = (f32[128,4096]{1,0:T(8,128)}, f32[128,4096]{1,0:T(8,128)}, f32[16,4096]{1,0:T(8,128)}, bf16[128,4096]{1,0:T(8,128)(2,1)}, f32[128,1024]{1,0:T(8...) custom-call(bf16[128,4096]{1,0:T(8,128)(2,1)} %get-tuple-element.36., ...), custom_call_target="tpu_custom_call" | custom-call | flops 1000000000 | bytes 8388608 | tf_op jit(solution)/shard_map/pallas_call | solution.py:526
  53.5 0.7 %all-to-all-done.1 = bf16[128,8,128]{2,1,0:T(8,128)(2,1)S(1)} async-done(((bf16[128,8,128]{2,1,0:T(8,128)(2,1)}), bf16[128,8,128]{2,1,0:T(8,128)(2,1)S(1)}, u32[]{:S(2)}, u32[]{:S(2)}) %all-to-all-start.1) | async-done | bytes 262176 | tf_op jit(solution)/shard_map/all_to_all | solution.py:497
  54.2 0.2 shard_map.107
  54.4 2.7 %collective-permute-start = (f32[16,32]{1,0:T(8,128)S(1)}, f32[16,32]{1,0:T(8,128)S(1)}, u32[]{:S(2)}, u32[]{:S(2)}) collective-permute-start(f32[16,32]{1,0:T(8,128)S(1)} %shard_map.107), channel_id=1, source_target_pairs={{0,1},{1,0},{2,3},{3,2},{4,5},{5,4},{6,7},{7,6},{8,9},{9,8},{10,11... | collective-permute-start | bytes 6152 | tf_op jit(solution)/shard_map/ppermute | solution.py:543
  57.0 5.3 %shard_map.106 = (bf16[128,4096]{1,0:T(8,128)(2,1)}, bf16[128,4096]{1,0:T(8,128)(2,1)}) custom-call(f32[128,4096]{1,0:T(8,128)} %get-tuple-element.43.refs_0_, f32[128,4096]{1,0:T(8,128)} %get-tuple-element.37.lead_far.refs_1_, f32[128,4096]{1,0:T(8,128)} %get-tuple-element.44.refs_2_, f32[16,4096]{1,0:T(8,128)} %get-tuple-element.45.refs_3_, ...), custom_call_target="tpu_custom_call" | custom-call | flops 1000000000 | bytes 9437184 | tf_op jit(solution)/shard_map/pallas_call | solution.py:444
  62.3 0.0 collective-permute-done
  62.4 0.6 add_bitcast_fusion
Async XLA Ops:
  10.3 23.5 %all-to-all-start = ((bf16[128,8,128]{2,1,0:T(8,128)(2,1)}), bf16[128,8,128]{2,1,0:T(8,128)(2,1)S(1)}, u32[]{:S(2)}, u32[]{:S(2)}) async-start(bf16[128,8,128]{2,1,0:T(8,128)(2,1)} %bitcast.34), calls=%async_computation | async-start | bytes 524288 | tf_op jit(solution)/shard_map/all_to_all | solution.py:497
  27.0 6.8 %copy-start = (f32[8,128]{1,0:T(8,128)S(1)}, f32[8,128]{1,0:T(8,128)}, u32[]{:S(2)}) copy-start(f32[8,128]{1,0:T(8,128)} %get-tuple-element.35.rate_ref) | copy-start | bytes 12292
  34.9 19.3 %all-to-all-start.1 = ((bf16[128,8,128]{2,1,0:T(8,128)(2,1)}), bf16[128,8,128]{2,1,0:T(8,128)(2,1)S(1)}, u32[]{:S(2)}, u32[]{:S(2)}) async-start(bf16[128,8,128]{2,1,0:T(8,128)(2,1)} %bitcast.10), calls=%async_computation.1 | async-start | bytes 524288 | tf_op jit(solution)/shard_map/all_to_all | solution.py:497
  54.4 8.0 %collective-permute-start = (f32[16,32]{1,0:T(8,128)S(1)}, f32[16,32]{1,0:T(8,128)S(1)}, u32[]{:S(2)}, u32[]{:S(2)}) collective-permute-start(f32[16,32]{1,0:T(8,128)S(1)} %shard_map.107), channel_id=1, source_target_pairs={{0,1},{1,0},{2,3},{3,2},{4,5},{5,4},{6,7},{7,6},{8,9},{9,8},{10,11... | collective-permute-start | bytes 6152 | tf_op jit(solution)/shard_map/ppermute | solution.py:543

commit v8 on v7

--- a/solution.py
+++ b/solution.py
@@ -175,7 +175,7 @@
         rows = slab_rows(tile, grad_ref.shape[1] // LANES)
         send_ref[rows, :] = jnp.concatenate(sums[::-1], axis=0).astype(BF16)
 
-    each_tile(grad_ref.shape[1], body)
+    each_tile(grad_ref.shape[1], body, 8)
 
 
 def local_kernel(
@@ -221,7 +221,7 @@
                 lead_ref[mode_rows, lanes] = carry * wide(weights[m : m + 1, lanes])
             lags[1, rows, lanes] = sublane_sums(cross, place)
 
-    each_tile(mixed_ref.shape[1], body)
+    each_tile(mixed_ref.shape[1], body, 4)
     coef = jnp.broadcast_to(lags[0, ROWS - 1 : ROWS, :], rates.shape)
     for d in range(ROWS - 2, -1, -1):
         coef = coef * powers[...] + lags[0, d : d + 1, :]
@@ -487,7 +487,7 @@
         [token_block] * 4 + [mode_block],
         [token_block] * 4 + [slab_block, pl.BlockSpec((SUB, LANES), lambda n: (0, 0))],
         [token_half, token_half, token_full, token_full, slabs, jax.ShapeDtypeStruct((SUB, LANES), F32)],
-        [table(4, MODES, WIDTH), table(2, 2, SUB * PITCH, LANES)],
+        [table(4, MODES, WIDTH), table(8, 2, SUB * PITCH, LANES)],
         10**9, 10 * 2**20,
     )(grad, query, key, value, rates)
 

time: 63.2 us -> 63 us (level)
  transfers between devices with their start and end apart: 3 -> 3, of which waited for: 1 -> 2; matrix products, arithmetic and copies ran while one was open for 0% -> 0% of each run, Pallas kernels for 29% -> 29%
where the time goes in v8:
time: 63 us; the launch traced here: 62.7 us
  starting transfers between devices  31.8 us (50%)
  Pallas kernels  28.8 us (46%)
  waiting for transfers between devices  0.87 us (1%)
  between operations  0.69 us (1%)
    all_to_all x2, starting transfers between devices, exchange(): lax.all_to_all(pieces, 'ctx', split_axis=0, concat_axis=0, axis_index_gro...  29.1 us
    pallas_call x2, Pallas kernels, streamed(): call(kernel, (), specs[:n_in] + [pl.BlockSpec(memory_space=pltpu.VMEM)] *...  12 us
    pallas_call x1, Pallas kernels, local(): call(summary_kernel, steps, [token_block] * 4 + [mode_block], [token_bloc...  9.44 us
    pallas_call x1, Pallas kernels, local(): call(stage_kernel, (), [far_spec] * 8, [far_spec] * 4 + [near_spec] * 6,...  6.09 us
    ppermute x1, starting transfers between devices, local(): other = lax.ppermute(coef_part, 'dp', [(0, 1), (1, 0)])  2.65 us
  transfers between devices with their start and end apart: 3, of which 2 were waited for; matrix products, arithmetic and copies ran while one was open for 0% of the time, Pallas kernels for 29%

profile of v8, /device:TPU:1, one launch (start us, length us, event | category | flops | bytes accessed | tf_op | source)
XLA Modules:
  0.0 62.7 jit_solution(6833440055912528849)
XLA Ops:
  0.6 9.4 %shard_map.102 = (bf16[128,4096]{1,0:T(8,128)(2,1)}, bf16[128,4096]{1,0:T(8,128)(2,1)}, f32[128,4096]{1,0:T(8,128)}, f32[128,4096]{1,0:T(8,128)}, bf16[1024,128]{1,0:T(8,128)(2,1)}, /*index=5*/f32[8,128]{1,0:T(8,128)}) custom-call(bf16[128,4096]{1,0:T(8,128)(2,1)} %bitcast.25, bf16[128,4096]{1,0:T(8,128)(2,1)} %bitcast.30, bf16[128,4096]{1,0:T(8,128)(2,1)} %bitcast.19, ...), custom_call_target="tpu_custom_call" | custom-call | flops 1000000000 | bytes 10485760 | tf_op jit(solution)/shard_map/pallas_call | solution.py:485
  10.1 16.7 %all-to-all-start = ((bf16[128,8,128]{2,1,0:T(8,128)(2,1)}), bf16[128,8,128]{2,1,0:T(8,128)(2,1)S(1)}, u32[]{:S(2)}, u32[]{:S(2)}) async-start(bf16[128,8,128]{2,1,0:T(8,128)(2,1)} %bitcast.34), calls=%async_computation | async-start | bytes 524288 | tf_op jit(solution)/shard_map/all_to_all | solution.py:497
  26.7 0.0 copy-start
  26.8 6.7 %shard_map.103 = (f32[128,4096]{1,0:T(8,128)}, bf16[1024,128]{1,0:T(8,128)(2,1)S(1)}) custom-call(bf16[128,4096]{1,0:T(8,128)(2,1)} %get-tuple-element.36.refs_0_.mixed_far, bf16[128,4096]{1,0:T(8,128)(2,1)} %get-tuple-element.31.refs_1_, f32[128,4096]{1,0:T(8,128)} %get-tuple-element.32.refs_2_, f32[128,4096]{1,0:T(8,128)} %get-tuple-element.33.refs_3_, ...), custom_call_target="tpu_custom_call" | custom-call | flops 1000000000 | bytes 10485760 | tf_op jit(solution)/shard_map/pallas_call | solution.py:444
  33.4 0.1 all-to-all-done
  33.6 0.0 copy-done
  33.6 1.1 %shard_map.104 = bf16[1024,128]{1,0:T(8,128)(2,1)} custom-call(bf16[1024,128]{1,0:T(8,128)(2,1)S(1)} %bitcast.18, bf16[1024,128]{1,0:T(8,128)(2,1)S(1)} %get-tuple-element.34.coef_ref, f32[8,128]{1,0:T(8,128)S(1)} %copy-done), custom_call_target="tpu_custom_call" | custom-call | flops 1000000 | bytes 1048576 | tf_op jit(solution)/shard_map/pallas_call | solution.py:515
  34.7 12.4 %all-to-all-start.1 = ((bf16[128,8,128]{2,1,0:T(8,128)(2,1)}), bf16[128,8,128]{2,1,0:T(8,128)(2,1)S(1)}, u32[]{:S(2)}, u32[]{:S(2)}) async-start(bf16[128,8,128]{2,1,0:T(8,128)(2,1)} %bitcast.10), calls=%async_computation.1 | async-start | bytes 524288 | tf_op jit(solution)/shard_map/all_to_all | solution.py:497
  47.1 6.1 %shard_map.105 = (f32[128,4096]{1,0:T(8,128)}, f32[128,4096]{1,0:T(8,128)}, f32[16,4096]{1,0:T(8,128)}, bf16[128,4096]{1,0:T(8,128)(2,1)}, f32[128,1024]{1,0:T(8...) custom-call(bf16[128,4096]{1,0:T(8,128)(2,1)} %get-tuple-element.36., ...), custom_call_target="tpu_custom_call" | custom-call | flops 1000000000 | bytes 8388608 | tf_op jit(solution)/shard_map/pallas_call | solution.py:526
  53.2 0.7 %all-to-all-done.1 = bf16[128,8,128]{2,1,0:T(8,128)(2,1)S(1)} async-done(((bf16[128,8,128]{2,1,0:T(8,128)(2,1)}), bf16[128,8,128]{2,1,0:T(8,128)(2,1)S(1)}, u32[]{:S(2)}, u32[]{:S(2)}) %all-to-all-start.1) | async-done | bytes 262176 | tf_op jit(solution)/shard_map/all_to_all | solution.py:497
  54.0 0.2 shard_map.107
  54.1 2.7 %collective-permute-start = (f32[16,32]{1,0:T(8,128)S(1)}, f32[16,32]{1,0:T(8,128)S(1)}, u32[]{:S(2)}, u32[]{:S(2)}) collective-permute-start(f32[16,32]{1,0:T(8,128)S(1)} %shard_map.107), channel_id=1, source_target_pairs={{0,1},{1,0},{2,3},{3,2},{4,5},{5,4},{6,7},{7,6},{8,9},{9,8},{10,11... | collective-permute-start | bytes 6152 | tf_op jit(solution)/shard_map/ppermute | solution.py:543
  56.8 5.3 %shard_map.106 = (bf16[128,4096]{1,0:T(8,128)(2,1)}, bf16[128,4096]{1,0:T(8,128)(2,1)}) custom-call(f32[128,4096]{1,0:T(8,128)} %get-tuple-element.43.refs_0_, f32[128,4096]{1,0:T(8,128)} %get-tuple-element.37.lead_far.refs_1_, f32[128,4096]{1,0:T(8,128)} %get-tuple-element.44.refs_2_, f32[16,4096]{1,0:T(8,128)} %get-tuple-element.45.refs_3_, ...), custom_call_target="tpu_custom_call" | custom-call | flops 1000000000 | bytes 9437184 | tf_op jit(solution)/shard_map/pallas_call | solution.py:444
  62.1 0.0 collective-permute-done
  62.1 0.6 add_bitcast_fusion
Async XLA Ops:
  10.1 23.5 %all-to-all-start = ((bf16[128,8,128]{2,1,0:T(8,128)(2,1)}), bf16[128,8,128]{2,1,0:T(8,128)(2,1)S(1)}, u32[]{:S(2)}, u32[]{:S(2)}) async-start(bf16[128,8,128]{2,1,0:T(8,128)(2,1)} %bitcast.34), calls=%async_computation | async-start | bytes 524288 | tf_op jit(solution)/shard_map/all_to_all | solution.py:497
  26.7 6.8 %copy-start = (f32[8,128]{1,0:T(8,128)S(1)}, f32[8,128]{1,0:T(8,128)}, u32[]{:S(2)}) copy-start(f32[8,128]{1,0:T(8,128)} %get-tuple-element.35.rate_ref) | copy-start | bytes 12292
  34.7 19.3 %all-to-all-start.1 = ((bf16[128,8,128]{2,1,0:T(8,128)(2,1)}), bf16[128,8,128]{2,1,0:T(8,128)(2,1)S(1)}, u32[]{:S(2)}, u32[]{:S(2)}) async-start(bf16[128,8,128]{2,1,0:T(8,128)(2,1)} %bitcast.10), calls=%async_computation.1 | async-start | bytes 524288 | tf_op jit(solution)/shard_map/all_to_all | solution.py:497
  54.1 8.0 %collective-permute-start = (f32[16,32]{1,0:T(8,128)S(1)}, f32[16,32]{1,0:T(8,128)S(1)}, u32[]{:S(2)}, u32[]{:S(2)}) collective-permute-start(f32[16,32]{1,0:T(8,128)S(1)} %shard_map.107), channel_id=1, source_target_pairs={{0,1},{1,0},{2,3},{3,2},{4,5},{5,4},{6,7},{7,6},{8,9},{9,8},{10,11... | collective-permute-start | bytes 6152 | tf_op jit(solution)/shard_map/ppermute | solution.py:543
